TPU v7x, 32 devices: a whole 2x2x4 slice. The times are simulated.
32 devices in a mesh: dp: 4 (over x, core), seq: 8 (over z, y).
Axes of the slice: x: 2, y: 2, z: 4, core: 2. Of those that a mesh axis runs over, the one named last changes fastest.
Arguments:
- tokens: bfloat16 [4, 2048, 512], P('dp', 'seq'), may hold values from -6 to 6
- segment_ids: int32 [4, 2048], P('dp'), may hold values from 0 to 2, as said below
- gain_one: float32 [512], replicated, may hold values from 0.5 to 1.5
- bias_one: float32 [512], replicated, may hold values from -3 to 3
- w_qkv: bfloat16 [512, 1536], replicated, may hold values from -0.375 to 0.375
- b_val: float32 [512], replicated, may hold values from -0.3 to 0.3
- w_out: bfloat16 [512, 512], replicated, may hold values from -4 to 4
- b_out: float32 [512], replicated, may hold values from -3 to 3
- gain_two: float32 [512], replicated, may hold values from 0.5 to 1.5
- bias_two: float32 [512], replicated, may hold values from -3 to 3
- w_up: bfloat16 [512, 2048], replicated, may hold values from -0.25 to 0.25
- b_up: float32 [2048], replicated, may hold values from -3 to 3
- w_down: bfloat16 [2048, 512], replicated, may hold values from -0.125 to 0.125
- b_down: float32 [512], replicated, may hold values from -3 to 3
- cotangent: bfloat16 [4, 2048, 512], P('dp', 'seq'), may hold values from -6 to 6
Outputs:
- output: bfloat16 [4, 2048, 512], P('dp', 'seq')
- tokens_grad: float32 [4, 2048, 512], P('dp', 'seq')
- gain_one_grad: float32 [512], replicated
- bias_one_grad: float32 [512], replicated
- w_qkv_grad: float32 [512, 1536], replicated
- b_val_grad: float32 [512], replicated
- w_out_grad: float32 [512, 512], replicated
- b_out_grad: float32 [512], replicated
- gain_two_grad: float32 [512], replicated
- bias_two_grad: float32 [512], replicated
- w_up_grad: float32 [512, 2048], replicated
- b_up_grad: float32 [2048], replicated
- w_down_grad: float32 [2048, 512], replicated
- b_down_grad: float32 [512], replicated
Inputs may be any that keep to these rules, and one draw needn't show every extreme that they name: `segment_ids`: every row holds exactly three documents, numbered 0, 1, 2 in order along the row, each a run of equal ids; the first ends within the first 256 positions and the last begins within the last 256.
All inputs are finite; a program needn't handle non-finite values.
Results may differ from a plain program's by a relative error of at most 0.019.
Values may be sent and summed in bfloat16 or wider, within the bound.
A program may use at most 192 MiB of HBM per device.

v0:
```python
import math

import jax
import jax.numpy as jnp
from jax import lax
from jax.sharding import PartitionSpec as P

HD = 64


norm_eps = 1e-05
select_weight = 4.0
neg_large = -1e30
highest = lax.Precision.HIGHEST


def prefix(array, axis, combine, identity, reverse):
    length, here = (lax.axis_size(axis), lax.axis_index(axis))
    everything = lax.all_gather(array.astype(jnp.bfloat16), axis)
    start = jnp.broadcast_to(jnp.asarray(identity, array.dtype), array.shape)

    def hop(k, before):
        at = length - 1 - k if reverse else k
        reached = at > here if reverse else at < here
        new = combine(before, everything[at].astype(array.dtype))
        return jnp.where(reached, new, before)

    return lax.fori_loop(0, length, hop, start)


def layer_norm(values, norm_gain, norm_shift):
    centered = values - jnp.mean(values, axis=-1, keepdims=True)
    variance = jnp.mean(centered * centered, axis=-1, keepdims=True)
    return centered * lax.rsqrt(variance + norm_eps) * norm_gain + norm_shift


def exact_gelu(values):
    return jax.nn.gelu(values, approximate=False)


def add_arrays(earlier, later):
    return earlier + later


def keep_state(state_in):
    return state_in


def pick_block():
    return 512


def local(
    tokens,
    segment_ids,
    gain_one,
    bias_one,
    w_qkv,
    b_val,
    w_out,
    b_out,
    gain_two,
    bias_two,
    w_up,
    b_up,
    w_down,
    b_down,
    cotangent,
):
    seq_count = lax.axis_size("seq")
    seq_rank = lax.axis_index("seq")
    row_tokens = tokens[0].astype(jnp.float32)
    tok_rows = row_tokens.shape[0]
    model_width = row_tokens.shape[1]
    head_count = model_width // HD
    length = tok_rows * seq_count
    score_scale = 1.0 / math.sqrt(HD)
    select_coeff = select_weight / length
    row_segments = segment_ids[0]
    row_base = seq_rank * tok_rows
    query_pos = row_base + jnp.arange(tok_rows, dtype=jnp.int32)
    query_segs = lax.dynamic_slice_in_dim(row_segments, row_base, tok_rows)
    last_query = row_base + tok_rows - 1
    lower_mask = (jnp.arange(tok_rows)[:, None] > jnp.arange(tok_rows)[None, :]).astype(jnp.float32)
    upper_mask = lower_mask.T
    normed_one, norm_one_back = jax.vjp(layer_norm, row_tokens, gain_one, bias_one)
    normed_one_low = normed_one.astype(jnp.bfloat16)
    value_bias = jnp.concatenate([jnp.zeros((2 * model_width,), jnp.float32), b_val])
    joined_low = (
        jnp.dot(normed_one_low, w_qkv, preferred_element_type=jnp.float32) + value_bias
    ).astype(jnp.bfloat16)
    queries = joined_low[:, :model_width]
    keys_mine = joined_low[:, model_width : 2 * model_width]
    values_mine = joined_low[:, 2 * model_width :]
    query_heads = queries.reshape(tok_rows, head_count, HD)
    query_zero = queries[:, :HD]
    query_rest = query_heads[:, 1:]

    def pair_masks(key_start, key_rows):
        key_pos = key_start + jnp.arange(key_rows, dtype=jnp.int32)
        key_segs = lax.dynamic_slice_in_dim(row_segments, key_start, key_rows)
        same_doc = query_segs[:, None] == key_segs[None, :]
        attend_mask = same_doc & (key_pos[None, :] <= query_pos[:, None])
        select_mask = same_doc & (key_pos[None, :] < query_pos[:, None])
        return (attend_mask, select_mask)

    select_init = (
        jnp.zeros((tok_rows, length), jnp.float32),
        jnp.zeros((tok_rows, length), jnp.float32),
        jnp.zeros((length,), jnp.float32),
    )
    running = select_init
    key_piece = lax.all_gather(keys_mine[:, :HD], "seq", axis=0, tiled=True)
    piece_rows = key_piece.shape[0]
    block_rows = pick_block()

    def select_block(state_now, offset):
        zero_scores, local_forgot, column_sums = state_now
        key_block = lax.dynamic_slice_in_dim(key_piece, offset, block_rows)
        attend_mask, select_mask = pair_masks(offset, block_rows)
        scores = (
            jnp.einsum("qd,kd->qk", query_zero, key_block, preferred_element_type=jnp.float32)
            * score_scale
        )
        chosen = jnp.where(select_mask, jax.nn.softplus(scores), 0.0)
        forgot = jnp.dot(lower_mask, chosen, precision=highest)
        zero_scores = lax.dynamic_update_slice_in_dim(zero_scores, scores, offset, 1)
        local_forgot = lax.dynamic_update_slice_in_dim(local_forgot, forgot, offset, 1)
        column_sums = lax.dynamic_update_slice_in_dim(
            column_sums, jnp.sum(chosen, axis=0), offset, 0
        )
        return ((zero_scores, local_forgot, column_sums), None)

    offsets = jnp.arange(piece_rows // block_rows, dtype=jnp.int32) * block_rows
    running, unused = lax.scan(select_block, running, offsets)
    zero_scores, local_forgot, column_sums = running
    column_prefix = prefix(column_sums, "seq", add_arrays, jnp.zeros((length,), jnp.float32), False)
    attend_init = (
        jnp.full((head_count, tok_rows), neg_large, jnp.float32),
        jnp.zeros((head_count, tok_rows), jnp.float32),
        jnp.zeros((tok_rows, head_count, HD), jnp.float32),
    )
    running = attend_init
    attend_key_piece = lax.all_gather(keys_mine, "seq", axis=0, tiled=True)
    value_piece = lax.all_gather(values_mine, "seq", axis=0, tiled=True)
    piece_rows = attend_key_piece.shape[0]
    attend_block_rows = pick_block()

    def attend_block(state_now, offset):
        key_start = offset

        def attend_compute(state_in):
            run_max, run_total, accumulated = state_in
            key_block = lax.dynamic_slice_in_dim(
                attend_key_piece, offset, attend_block_rows
            ).reshape(attend_block_rows, head_count, HD)
            value_block = lax.dynamic_slice_in_dim(value_piece, offset, attend_block_rows).reshape(
                attend_block_rows, head_count, HD
            )
            attend_mask, select_mask = pair_masks(key_start, attend_block_rows)
            rest_scores = (
                jnp.einsum(
                    "qhd,khd->hqk", query_rest, key_block[:, 1:], preferred_element_type=jnp.float32
                )
                * score_scale
            )
            head_zero = lax.dynamic_slice_in_dim(zero_scores, key_start, attend_block_rows, 1)
            scores = jnp.concatenate([head_zero[None], rest_scores], axis=0)
            forgot = lax.dynamic_slice_in_dim(column_prefix, key_start, attend_block_rows)[
                None, :
            ] + lax.dynamic_slice_in_dim(local_forgot, key_start, attend_block_rows, 1)
            logits = jnp.where(attend_mask[None], scores - select_coeff * forgot[None], neg_large)
            new_max = jnp.maximum(run_max, jnp.max(logits, axis=-1))
            weights = jnp.where(attend_mask[None], jnp.exp(logits - new_max[:, :, None]), 0.0)
            decay_factor = jnp.exp(run_max - new_max)
            run_total = run_total * decay_factor + jnp.sum(weights, axis=-1)
            accumulated = accumulated * decay_factor.T[:, :, None] + jnp.einsum(
                "hqk,khd->qhd",
                weights.astype(jnp.bfloat16),
                value_block,
                preferred_element_type=jnp.float32,
            )
            return (new_max, run_total, accumulated)

        state_now = lax.cond(key_start <= last_query, attend_compute, keep_state, state_now)
        return (state_now, None)

    offsets = jnp.arange(piece_rows // attend_block_rows, dtype=jnp.int32) * attend_block_rows
    running, unused = lax.scan(attend_block, running, offsets)
    run_max, run_total, accumulated = running
    log_total = run_max + jnp.log(run_total)
    mixed_float = accumulated / run_total.T[:, :, None]
    mixed_low = mixed_float.reshape(tok_rows, model_width).astype(jnp.bfloat16)
    middle = row_tokens + jnp.dot(mixed_low, w_out, preferred_element_type=jnp.float32) + b_out
    normed_two, norm_two_back = jax.vjp(layer_norm, middle, gain_two, bias_two)
    normed_two_low = normed_two.astype(jnp.bfloat16)
    hidden = jnp.dot(normed_two_low, w_up, preferred_element_type=jnp.float32) + b_up
    active, gelu_back = jax.vjp(exact_gelu, hidden)
    active_low = active.astype(jnp.bfloat16)
    output = middle + jnp.dot(active_low, w_down, preferred_element_type=jnp.float32) + b_down
    grad_out = cotangent[0]
    grad_float = grad_out.astype(jnp.float32)
    w_down_grad = jnp.einsum("tf,td->fd", active_low, grad_out, preferred_element_type=jnp.float32)
    b_down_grad = jnp.sum(grad_float, axis=0)
    grad_active = jnp.einsum("td,fd->tf", grad_out, w_down, preferred_element_type=jnp.float32)
    (grad_hidden,) = gelu_back(grad_active)
    grad_hidden_low = grad_hidden.astype(jnp.bfloat16)
    w_up_grad = jnp.einsum(
        "td,tf->df", normed_two_low, grad_hidden_low, preferred_element_type=jnp.float32
    )
    b_up_grad = jnp.sum(grad_hidden_low.astype(jnp.float32), axis=0)
    grad_normed_two = jnp.einsum(
        "tf,df->td", grad_hidden_low, w_up, preferred_element_type=jnp.float32
    )
    grad_middle_norm, gain_two_grad, bias_two_grad = norm_two_back(grad_normed_two)
    grad_middle = grad_float + grad_middle_norm
    grad_branch_low = grad_middle.astype(jnp.bfloat16)
    w_out_grad = jnp.einsum(
        "td,te->de", mixed_low, grad_branch_low, preferred_element_type=jnp.float32
    )
    b_out_grad = jnp.sum(grad_branch_low.astype(jnp.float32), axis=0)
    grad_mixed_low = jnp.einsum(
        "te,de->td", grad_branch_low, w_out, preferred_element_type=jnp.float32
    ).astype(jnp.bfloat16)
    grad_mixed_heads = grad_mixed_low.reshape(tok_rows, head_count, HD)
    row_delta = jnp.sum(grad_mixed_heads.astype(jnp.float32) * mixed_float, axis=-1).T
    keys_back, values_back = (
        lax.all_gather(keys_mine, "seq", axis=0, tiled=True),
        lax.all_gather(values_mine, "seq", axis=0, tiled=True),
    )
    back_rows = pick_block()
    key_heads = keys_back.reshape(length, head_count, HD)
    value_heads = values_back.reshape(length, head_count, HD)

    def grad_block(state_now, offset):

        def grad_compute(state_in):
            query_grad, key_grad, value_grad, first_part, second_part, grad_cols = state_in
            key_block = lax.dynamic_slice_in_dim(key_heads, offset, back_rows)
            value_block = lax.dynamic_slice_in_dim(value_heads, offset, back_rows)
            attend_mask, select_mask = pair_masks(offset, back_rows)
            scores = (
                jnp.einsum(
                    "qhd,khd->hqk", query_heads, key_block, preferred_element_type=jnp.float32
                )
                * score_scale
            )
            chosen = jnp.where(select_mask, jax.nn.softplus(scores[0]), 0.0)
            forgot = lax.dynamic_slice_in_dim(column_prefix, offset, back_rows)[None, :] + jnp.dot(
                lower_mask, chosen, precision=highest
            )
            logits = scores - select_coeff * forgot[None]
            prob_block = jnp.where(attend_mask[None], jnp.exp(logits - log_total[:, :, None]), 0.0)
            grad_probs = jnp.einsum(
                "qhd,khd->hqk", grad_mixed_heads, value_block, preferred_element_type=jnp.float32
            )
            grad_logits = prob_block * (grad_probs - row_delta[:, :, None])
            value_part = jnp.einsum(
                "hqk,qhd->khd",
                prob_block.astype(jnp.bfloat16),
                grad_mixed_heads,
                preferred_element_type=jnp.float32,
            )
            rest_low = grad_logits[1:].astype(jnp.bfloat16)
            query_grad = (
                query_grad
                + jnp.einsum(
                    "hqk,khd->qhd", rest_low, key_block[:, 1:], preferred_element_type=jnp.float32
                )
                * score_scale
            )
            key_part = (
                jnp.einsum("hqk,qhd->khd", rest_low, query_rest, preferred_element_type=jnp.float32)
                * score_scale
            )
            total_grad = jnp.sum(grad_logits, axis=0)
            suffix_local = jnp.dot(upper_mask, total_grad, precision=highest)
            select_gate = jnp.where(select_mask, select_coeff * jax.nn.sigmoid(scores[0]), 0.0)
            first_part = lax.dynamic_update_slice_in_dim(
                first_part, grad_logits[0] - select_gate * suffix_local, offset, 1
            )
            second_part = lax.dynamic_update_slice_in_dim(second_part, select_gate, offset, 1)
            key_grad = lax.dynamic_update_slice_in_dim(key_grad, key_part, offset, 0)
            value_grad = lax.dynamic_update_slice_in_dim(value_grad, value_part, offset, 0)
            grad_cols = lax.dynamic_update_slice_in_dim(
                grad_cols, jnp.sum(total_grad, axis=0), offset, 0
            )
            return (query_grad, key_grad, value_grad, first_part, second_part, grad_cols)

        state_now = lax.cond(offset <= last_query, grad_compute, keep_state, state_now)
        return (state_now, None)

    grad_init = (
        jnp.zeros((tok_rows, head_count - 1, HD), jnp.float32),
        jnp.zeros((length, head_count - 1, HD), jnp.float32),
        jnp.zeros((length, head_count, HD), jnp.float32),
        jnp.zeros((tok_rows, length), jnp.float32),
        jnp.zeros((tok_rows, length), jnp.float32),
        jnp.zeros((length,), jnp.float32),
    )
    back_offsets = jnp.arange(length // back_rows, dtype=jnp.int32) * back_rows
    grad_state, unused = lax.scan(grad_block, grad_init, back_offsets)
    query_grad, key_grad, value_grad, first_part, second_part, grad_cols = grad_state
    grad_suffix = prefix(grad_cols, "seq", add_arrays, jnp.zeros((length,), jnp.float32), True)
    zero_grad_low = (first_part - second_part * grad_suffix[None, :]).astype(jnp.bfloat16)
    query_zero_grad = (
        jnp.dot(zero_grad_low, keys_back[:, :HD], preferred_element_type=jnp.float32) * score_scale
    )
    key_zero_grad = (
        jnp.einsum("ql,qd->ld", zero_grad_low, query_zero, preferred_element_type=jnp.float32)
        * score_scale
    )
    key_total = jnp.concatenate([key_zero_grad[:, None, :], key_grad], axis=1).reshape(
        length, model_width
    )
    value_total = value_grad.reshape(length, model_width)
    key_mine_grad, value_mine_grad = (
        lax.psum_scatter(
            key_total.astype(jnp.bfloat16), "seq", scatter_dimension=0, tiled=True
        ).astype(jnp.float32),
        lax.psum_scatter(
            value_total.astype(jnp.bfloat16), "seq", scatter_dimension=0, tiled=True
        ).astype(jnp.float32),
    )
    query_total = jnp.concatenate([query_zero_grad[:, None, :], query_grad], axis=1).reshape(
        tok_rows, model_width
    )
    grad_joined_low = jnp.concatenate([query_total, key_mine_grad, value_mine_grad], axis=1).astype(
        jnp.bfloat16
    )
    b_val_grad = jnp.sum(grad_joined_low[:, 2 * model_width :].astype(jnp.float32), axis=0)
    w_qkv_grad = jnp.einsum(
        "td,te->de", normed_one_low, grad_joined_low, preferred_element_type=jnp.float32
    )
    grad_normed_one = jnp.einsum(
        "te,de->td", grad_joined_low, w_qkv, preferred_element_type=jnp.float32
    )
    grad_tokens_norm, gain_one_grad, bias_one_grad = norm_one_back(grad_normed_one)
    tokens_grad = grad_middle + grad_tokens_norm
    summed = lax.psum(
        (
            gain_one_grad,
            bias_one_grad,
            w_qkv_grad,
            b_val_grad,
            w_out_grad,
            b_out_grad,
            gain_two_grad,
            bias_two_grad,
            w_up_grad,
            b_up_grad,
            w_down_grad,
            b_down_grad,
        ),
        ("dp", "seq"),
    )
    return (
        output.astype(jnp.bfloat16)[None],
        tokens_grad[None],
        summed[0],
        summed[1],
        summed[2],
        summed[3],
        summed[4],
        summed[5],
        summed[6],
        summed[7],
        summed[8],
        summed[9],
        summed[10],
        summed[11],
    )


def solution(mesh):
    placed = (
        P("dp", "seq", None),
        P("dp", None),
        P(),
        P(),
        P(),
        P(),
        P(),
        P(),
        P(),
        P(),
        P(),
        P(),
        P(),
        P(),
        P("dp", "seq", None),
    )
    return jax.shard_map(
        local,
        mesh=mesh,
        in_specs=placed,
        out_specs=(
            P("dp", "seq", None),
            P("dp", "seq", None),
            P(),
            P(),
            P(),
            P(),
            P(),
            P(),
            P(),
            P(),
            P(),
            P(),
            P(),
            P(),
        ),
        check_vma=False,
    )
```

profile of v0, /device:TPU:0, one launch (start us, length us, event | category | flops | bytes accessed | tf_op | source)
XLA Modules:
  0.0 786.9 jit_solution(16967321479543268185)
XLA Ops:
  14.9 35.7 %all_gather.23 = bf16[2048,64]{1,0:T(8,128)(2,1)} all-gather(bf16[256,64]{1,0:T(8,128)(2,1)S(1)} %get-tuple-element.986), channel_id=1, replica_groups=mesh['dp'=4,'seq'=8] {'seq'}, dimensions={0}, use_global_device_ids=true | all-gather | bytes 294912 | tf_op jit(solution)/shard_map/all_gather | solution.py:113
  53.5 53.7 %while.81 = (s32[]{:T(128)}, f32[256,2048]{0,1:T(8,128)}, f32[256,2048]{0,1:T(8,128)}, bf16[2048]{0:T(1024)(128)(2,1)S(1)}, s32[4]{0:T(128)S(1)}, /*index=5*/bf1...) while((s32[]{:T(128)}, f32[256,2048]{0,1:T(8,128)}, ...), condition=%wide.region_4.5_spmd.clone, body=%wide.region_2.4_spmd.clone.sunk | while | flops 422445312 | bytes 7002347 | solution.py:135
  61.6 3.0 dynamic_update_slice.30
  64.6 2.9 dynamic_update_slice.31
  75.6 3.0 dynamic_update_slice.30
  78.6 2.9 dynamic_update_slice.31
  89.6 3.0 dynamic_update_slice.30
  92.5 2.9 dynamic_update_slice.31
  109.8 30.6 %all-gather = bf16[16384]{0:T(1024)(128)(2,1)S(1)} all-gather(bf16[2048]{0:T(1024)(128)(2,1)S(1)} %get-tuple-element.585), channel_id=2, replica_groups=mesh['dp'=4,'seq'=8] {'seq'}, dimensions={0}, use_global_device_ids=true | all-gather | bytes 36864 | tf_op jit(solution)/shard_map/all_gather | solution.py:19
  140.9 4.0 copy.60
  144.9 3.9 copy.59
  148.9 16.5 %while.82 = (s32[]{:T(128)}, f32[8,256]{1,0:T(8,128)S(1)}, f32[8,256]{1,0:T(8,128)S(1)}, f32[256,8,64]{0,2,1:T(8,128)S(1)}, s32[4]{0:T(128)S(1)}, /*index=5*/s32...) while((s32[]{:T(128)}, f32[8,256]{1,0:T(8,128)S(1)}, ...), condition=%wide.region_12.13_spmd.clone, body=%wide.region_7.12_spmd.clone.sunk | while | flops 270277376 | bytes 25023900 | solution.py:189
  150.2 11.4 %conditional.6 = ((f32[8,256]{1,0:T(8,128)S(1)}, f32[8,256]{1,0:T(8,128)S(1)}, f32[256,8,64]{0,2,1:T(8,128)S(1)})) conditional(s32[]{:T(128)} %convert_element_type.249, (f32[8,256]{1,0:T(8,128)S(1)}, f32[8,256]{1,0:T(8,128)S(1)}, f32[256,8,64]{0,2,1:T(8,128)S(1)}) %tuple.170, (s32[256]{0:T(256)S(1)}, s32[]{:T(128)}, s32[2048]{0:T(1024)S(1)}, ...), branch_computations={%region_8.8_spmd, %region_9.11_spmd} | conditional | flops 270277376 | bytes 25022558 | solution.py:185
  166.3 6.1 multiply_convert_fusion
  182.9 47.4 %while.83 = (s32[]{:T(128)}, f32[256,7,64]{0,2,1:T(8,128)}, bf16[2048,7,64]{0,2,1:T(8,128)(2,1)}, bf16[2048,8,64]{0,2,1:T(8,128)(2,1)}, f32[256,2048]{1,0:T(8,12...) while((s32[]{:T(128)}, f32[256,7,64]{0,2,1:T(8,128)}, ...), condition=%wide.region_23.24_spmd.clone, body=%wide.region_18.23_spmd.clone.sunk | while | flops 1459519744 | bytes 87650960 | solution.py:302
  184.2 42.1 %conditional.7 = ((f32[256,7,64]{0,2,1:T(8,128)}, bf16[2048,7,64]{0,2,1:T(8,128)(2,1)}, bf16[2048,8,64]{0,2,1:T(8,128)(2,1)}, f32[256,2048]{1,0:T(8,128)}, f32[2...) conditional(s32[]{:T(128)} %convert_element_type.251, (f32[256,7,64]{0,2,1:T(8,128)}, ...), branch_computations={%region_19.19_spmd, %region_20.22_spmd} | conditional | flops 1459257600 | bytes 87125208 | solution.py:290
  193.9 3.4 fusion.39
  197.3 3.1 fusion.126
  200.4 3.5 fusion.48
  208.4 5.5 dynamic_update_slice.19
  213.9 3.5 dynamic_update_slice.22
  217.3 3.4 dynamic_update_slice.21
  220.8 5.5 dynamic_update_slice.20
  230.4 188.1 %all-gather.1 = bf16[16384]{0:T(1024)(128)(2,1)S(1)} all-gather(bf16[2048]{0:T(1024)(128)(2,1)S(1)} %get-tuple-element.593), channel_id=3, replica_groups=mesh['dp'=4,'seq'=8] {'seq'}, dimensions={0}, use_global_device_ids=true | all-gather | bytes 36864 | tf_op jit(solution)/shard_map/all_gather | solution.py:19
  422.9 3.0 pad_maximum_fusion
  436.0 22.1 %reduce-scatter.5.cloned.1.call-done = bf16[256,512]{0,1:T(8,128)(2,1)} async-done(((bf16[2048,512]{0,1:T(8,128)(2,1)}), bf16[256,512]{0,1:T(8,128)(2,1)}) %reduce-scatter.5.cloned.1.call-update) | async-done | bytes 262160 | tf_op jit(solution)/shard_map/reduce_scatter | solution.py:321
  458.1 70.9 %reduce-scatter.3.cloned.1.call-done = bf16[256,512]{0,1:T(8,128)(2,1)} async-done(((bf16[2048,512]{0,1:T(8,128)(2,1)}), bf16[256,512]{0,1:T(8,128)(2,1)}) %reduce-scatter.3.cloned.1.call-update) | async-done | bytes 262160 | tf_op jit(solution)/shard_map/reduce_scatter | solution.py:318
  529.0 3.5 fusion.108
  533.1 3.1 fusion.91
  538.6 41.7 %all-reduce.1 = (f32[512]{0:T(512)}, f32[512]{0:T(512)}, f32[512]{0:T(512)}, f32[512]{0:T(512)}, f32[512]{0:T(512)}, /*index=5*/f32[512]{0:T(512)}, f32[2048]{0:T(1024)}, f32[512]{0:T(512)}) all-reduce(f32[512]{0:T(512)S(1)} %get-tuple-element.844, f32[512]{0:T(512)S(1)} %get-tuple-element.847, ...), channel_id=1, replica_groups=mesh['dp'=4,'seq'=8] {'dp','seq'}, use_global_device_ids=true, to_apply=%region_31.32 | all-reduce | flops 5632 | bytes 45056 | tf_op jit(solution)/shard_map/psum | solution.py:340
  580.4 188.3 %all-reduce.5.cloned.1.call-done = (f32[512,1536]{1,0:T(8,128)}, f32[512,512]{1,0:T(8,128)}, f32[512,2048]{1,0:T(8,128)}, f32[2048,512]{1,0:T(8,128)}) async-done(((f32[512,1536]{1,0:T(8,128)}, f32[512,512]{1,0:T(8,128)}, f32[512,2048]{1,0:T(8,128)}, f32[2048,512]{1,0:T(8,128)}), (f32[512,1536]{1,0:T(8,128)}, f32[512,512]{1,0:T(8,128)}, f32[512,2048]{1,0:T(8,128)}, ...) | async-done | bytes 12582928 | tf_op jit(solution)/shard_map/psum | solution.py:340
  768.7 3.9 copy.176
  (287 shorter events, 104.8 us)
Async XLA Ops:
  7.2 159.1 %copy-start = (bf16[512,2048]{1,0:T(8,128)(2,1)S(1)}, bf16[512,2048]{1,0:T(8,128)(2,1)}, u32[]{:S(2)}) copy-start(bf16[512,2048]{1,0:T(8,128)(2,1)} %param.39) | copy-start | bytes 6291460
  7.2 133.7 %all-gather.7.cloned.1.call-start = ((), (), s32[]{:S(2)}) async-start(), calls=%async_computation.3 | async-start | bytes 2359296 | tf_op jit(solution)/shard_map/all_gather | solution.py:145
  8.5 5.6 copy-start.31
  10.2 3.8 copy-start.35
  13.1 39.0 %copy-start.22 = (bf16[256,1536]{1,0:T(8,128)(2,1)}, bf16[256,1536]{1,0:T(8,128)(2,1)S(1)}, u32[]{:S(2)}) copy-start(bf16[256,1536]{1,0:T(8,128)(2,1)S(1)} %fusion.79) | copy-start | bytes 2359300
  13.1 37.5 %copy-start.28 = (s32[1,2048]{1,0:T(1,128)S(1)}, s32[1,2048]{1,0:T(1,128)}, u32[]{:S(2)}) copy-start(s32[1,2048]{1,0:T(1,128)} %param.30) | copy-start | bytes 24580
  14.1 130.8 %all-gather.5.cloned.1.call-start = ((), (), s32[]{:S(2)}) async-start(), calls=%async_computation.2 | async-start | bytes 2359296 | tf_op jit(solution)/shard_map/all_gather | solution.py:144
  14.8 443.2 %reduce-scatter.5.cloned.1.call-start = ((), (), s32[]{:S(2)}) async-start(), calls=%async_computation.5 | async-start | bytes 2359296 | tf_op jit(solution)/shard_map/reduce_scatter | solution.py:321
  148.9 16.7 %copy-start.6 = (bf16[1,256,512]{2,1,0:T(8,128)(2,1)S(1)}, bf16[1,256,512]{2,1,0:T(8,128)(2,1)}, u32[]{:S(2)}) copy-start(bf16[1,256,512]{2,1,0:T(8,128)(2,1)} %param.29) | copy-start | bytes 786436
  148.9 16.7 %copy-start.21 = (bf16[512,512]{1,0:T(8,128)(2,1)S(1)}, bf16[512,512]{1,0:T(8,128)(2,1)}, u32[]{:S(2)}) copy-start(bf16[512,512]{1,0:T(8,128)(2,1)} %param.35) | copy-start | bytes 1572868
  148.9 16.7 %copy-start.39 = (f32[512]{0:T(512)S(1)}, f32[512]{0:T(512)}, u32[]{:S(2)}) copy-start(f32[512]{0:T(512)} %param.36) | copy-start | bytes 6148
  166.0 8.8 %copy-start.8 = (f32[256,512]{1,0:T(8,128)}, f32[256,512]{1,0:T(8,128)S(1)}, u32[]{:S(2)}) copy-start(f32[256,512]{1,0:T(8,128)S(1)} %get-tuple-element.990) | copy-start | bytes 1572868
  166.3 6.1 copy-start.15
  166.3 6.1 copy-start.40
  175.1 3.1 copy-start.10
  193.9 3.5 copy-start.3
  200.4 3.5 copy-start.4
  230.3 298.6 %reduce-scatter.3.cloned.1.call-start = ((), (), s32[]{:S(2)}) async-start(), calls=%async_computation.4 | async-start | bytes 2359296 | tf_op jit(solution)/shard_map/reduce_scatter | solution.py:318
  425.9 342.8 %all-reduce.5.cloned.1.call-start = ((), (), s32[]{:S(2)}) async-start(), calls=%async_computation.6 | async-start | bytes 25165824 | tf_op jit(solution)/shard_map/psum | solution.py:340
  426.3 4.0 copy-start.14
  426.3 4.0 copy-start.16
  433.1 95.9 %copy-start.7 = (bf16[1,256,512]{2,1,0:T(8,128)(2,1)S(1)}, bf16[1,256,512]{2,1,0:T(8,128)(2,1)}, u32[]{:S(2)}) copy-start(bf16[1,256,512]{2,1,0:T(8,128)(2,1)} %param.29) | copy-start | bytes 786436
  433.1 95.9 %copy-start.29 = (f32[512]{0:T(512)S(1)}, f32[512]{0:T(512)}, u32[]{:S(2)}) copy-start(f32[512]{0:T(512)} %param.31) | copy-start | bytes 6148
  433.1 95.9 %copy-start.32 = (f32[256]{0:T(256)S(1)}, f32[256]{0:T(256)}, u32[]{:S(2)}) copy-start(f32[256]{0:T(256)} %copy-done.31) | copy-start | bytes 3076
  433.1 95.9 %copy-start.34 = (f32[512]{0:T(512)S(1)}, f32[512]{0:T(512)}, u32[]{:S(2)}) copy-start(f32[512]{0:T(512)} %param.32) | copy-start | bytes 6148
  433.1 95.9 %copy-start.36 = (f32[256]{0:T(256)S(1)}, f32[256]{0:T(256)}, u32[]{:S(2)}) copy-start(f32[256]{0:T(256)} %copy-done.35) | copy-start | bytes 3076
  533.1 3.2 copy-start.25
  533.1 3.3 copy-start.27
  533.1 3.3 copy-start.41
  768.7 3.9 copy-start.26
  768.7 4.9 copy-start.13
  773.6 3.7 copy-start.12
  (20 other events, 30.1 us)
Sparse Core Ops, SparseCore 0:
  14.2 53.2 all-gather.6
  70.2 48.9 all-gather.4
  230.4 227.5 reduce-scatter.4
  461.5 67.4 reduce-scatter.2
  536.4 232.2 all-reduce.4
where the time goes:
time: 792 us; the launch traced here: 787 us
  blocking collectives  296 us (37%)
  waiting for transfers between devices  282 us (36%)
  local copies, waits for them, and re-layouts  95.8 us (12%)
  matrix products  59.5 us (8%)
  other arithmetic  20.3 us (3%)
  loops' own time  18.3 us (2%)
  between operations  14.4 us (2%)
    all_gather x2, blocking collectives, prefix(): everything = lax.all_gather(array.astype(jnp.bfloat16), axis)  219 us
    psum x1, waiting for transfers between devices, local(): lax.psum((gain_one_grad, bias_one_grad, w_qkv_grad, b_val_grad, w_out_gra...  188 us
    reduce_scatter x1, waiting for transfers between devices, local(): lax.psum_scatter(key_total.astype(jnp.bfloat16), 'seq', scatter_dimension...  70.9 us
    psum x1, blocking collectives, local(): lax.psum((gain_one_grad, bias_one_grad, w_qkv_grad, b_val_grad, w_out_gra...  41.7 us
    all_gather x1, blocking collectives, local(): key_piece = lax.all_gather(keys_mine[:, :HD], 'seq', axis=0, tiled=True)  35.7 us
    reduce_scatter x1, waiting for transfers between devices, local(): lax.psum_scatter(value_total.astype(jnp.bfloat16), 'seq', scatter_dimensi...  22.1 us
    unnamed x86, local copies, waits for them, and re-layouts  21 us
  transfers between devices with their start and end apart: 5, of which 3 were waited for; matrix products, arithmetic and copies ran while one was open for 10% of the time, Pallas kernels for 0%

commit v1 on v0

--- a/solution.py
+++ b/solution.py
@@ -1,8 +1,11 @@
+import functools
 import math
 
 import jax
 import jax.numpy as jnp
 from jax import lax
+from jax.experimental import pallas as pl
+from jax.experimental.pallas import tpu as pltpu
 from jax.sharding import PartitionSpec as P
 
 HD = 64
@@ -12,6 +15,7 @@
 select_weight = 4.0
 neg_large = -1e30
 highest = lax.Precision.HIGHEST
+vmem_bytes = 60 * 1024 * 1024
 
 
 def prefix(array, axis, combine, identity, reverse):
@@ -372,6 +376,815 @@
     )
 
 
+low = jnp.bfloat16
+MESH = pl.DeviceIdType.MESH
+
+
+def dot_nn(left, right):
+    return lax.dot_general(left, right, (((1,), (0,)), ((), ())), preferred_element_type=jnp.float32)
+
+
+def dot_nt(left, right):
+    return lax.dot_general(left, right, (((1,), (1,)), ((), ())), preferred_element_type=jnp.float32)
+
+
+def dot_tn(left, right):
+    return lax.dot_general(left, right, (((0,), (0,)), ((), ())), preferred_element_type=jnp.float32)
+
+
+def swap_halves(wide):
+    return pltpu.roll(wide, HD, 1)
+
+
+def left_lanes(shape):
+    return lax.broadcasted_iota(jnp.int32, shape, 1) < HD
+
+
+def join_heads(left, right):
+    return jnp.where(left_lanes(left.shape), left, right)
+
+
+def fold_rows(wide):
+    half = wide.shape[0] // 2
+    return join_heads(wide[:half], swap_halves(wide[half:]))
+
+
+def spread_rows(folded):
+    return jnp.concatenate([folded, swap_halves(folded)], axis=0)
+
+
+def exact_cdf(values):
+    return 0.5 * (1.0 + lax.erf(values * (1.0 / math.sqrt(2.0))))
+
+
+def normalise(values):
+    centered = values - jnp.mean(values, axis=-1, keepdims=True)
+    rstd = lax.rsqrt(jnp.mean(centered * centered, axis=-1, keepdims=True) + norm_eps)
+    return centered * rstd, rstd
+
+
+def normalise_back(grad, unit, rstd, gain):
+    scaled = grad * gain
+    mean_one = jnp.mean(scaled, axis=-1, keepdims=True)
+    mean_two = jnp.mean(scaled * unit, axis=-1, keepdims=True)
+    return rstd * (scaled - mean_one - unit * mean_two)
+
+
+def layer_kernel(
+    tokens_ref,
+    seg_ref,
+    gain_one_ref,
+    bias_one_ref,
+    w_qkv_ref,
+    b_val_ref,
+    w_out_hbm,
+    b_out_ref,
+    gain_two_ref,
+    bias_two_ref,
+    w_up_hbm,
+    b_up_ref,
+    w_down_hbm,
+    b_down_ref,
+    cot_ref,
+    output_ref,
+    tokens_grad_ref,
+    vec_mid_ref,
+    vec_in_ref,
+    w_down_out,
+    w_up_out,
+    w_out_out,
+    w_qkv_out,
+    *scratch,
+):
+    (
+        w_out_ref, w_up_ref, w_down_ref, load_sem, store_sem,
+        send_qkv, recv_qkv, first, vals, query_t, first_t, wide_q, wide_first,
+        probs, gates, logit, carry, row_top, row_acc, mixed_keep,
+        send_mix, recv_mix, send_gmix, recv_gmix, grad_rows, grad_rows_t,
+        dq_acc, dq0_acc, dkv_acc, dk0_acc, back_carry,
+        send_back, recv_back, send_first, recv_first,
+        lower, upper,
+        normed_one_ref, unit_one_ref, rstd_one_ref,
+        mixed_ref, unit_two_ref, rstd_two_ref, normed_two_ref, middle_ref, out_acc, gn_acc, joined_ref,
+        mid_mine, mid_final, mid_core, mid_two, mid_three, mid_four,
+        in_mine, in_final, in_core, in_two, in_three, in_four,
+        vec_mid_mine, vec_mid_seq, vec_mid_sum, vec_mid_dp,
+        vec_in_mine, vec_in_seq, vec_in_sum, vec_in_dp,
+        qkv_s, qkv_r, first_s, first_r, mix_s, mix_r, gmix_s, gmix_r,
+        back_s, back_r, fback_s, fback_r,
+        mid_s, mid_r, in_s, in_r, mid_cs, mid_cr, vec_s, vec_r,
+    ) = scratch
+    dp_count, count = lax.axis_size("dp"), lax.axis_size("seq")
+    dp, me = lax.axis_index("dp"), lax.axis_index("seq")
+    rows, width = tokens_ref.shape[1], tokens_ref.shape[2]
+    half = rows // 2
+    length = rows * count
+    coeff = select_weight / length
+    hidden_width = w_up_hbm.shape[1]
+    pairs = width // (2 * HD)
+
+    barrier = pltpu.get_barrier_semaphore()
+
+    def greet_seq(step, carried):
+        pl.semaphore_signal(
+            barrier, inc=1, device_id=(dp, lax.rem(me + step, count)), device_id_type=MESH
+        )
+        return carried
+
+    def greet_dp(step, carried):
+        pl.semaphore_signal(
+            barrier, inc=1, device_id=(lax.rem(dp + step, dp_count), me), device_id_type=MESH
+        )
+        return carried
+
+    lax.fori_loop(1, count, greet_seq, 0)
+    lax.fori_loop(1, dp_count, greet_dp, 0)
+    loads = [
+        pltpu.make_async_copy(w_out_hbm, w_out_ref, load_sem.at[0]),
+        pltpu.make_async_copy(w_up_hbm, w_up_ref, load_sem.at[1]),
+        pltpu.make_async_copy(w_down_hbm, w_down_ref, load_sem.at[2]),
+    ]
+    for load in loads:
+        load.start()
+
+    def exchange(src, dst, send_sem, recv_sem, target):
+        return pltpu.make_async_remote_copy(
+            src_ref=src, dst_ref=dst, send_sem=send_sem, recv_sem=recv_sem,
+            device_id=(dp, target), device_id_type=MESH,
+        )
+
+    tokens = tokens_ref[0].astype(jnp.float32)
+    unit, rstd = normalise(tokens)
+    unit_one_ref[...] = unit
+    rstd_one_ref[...] = rstd
+    normed_one_ref[...] = (unit * gain_one_ref[...] + bias_one_ref[...]).astype(low)
+    score_scale = 1.0 / math.sqrt(HD)
+
+    def project(pair, carried):
+        at = pl.multiple_of(pair * 2 * HD, 2 * HD)
+        normed = normed_one_ref[...]
+        query = dot_nn(normed, w_qkv_ref[:, pl.ds(at, 2 * HD)]).astype(low).astype(jnp.float32) * score_scale
+        key = dot_nn(normed, w_qkv_ref[:, pl.ds(width + at, 2 * HD)]).astype(low).astype(jnp.float32)
+        value = dot_nn(normed, w_qkv_ref[:, pl.ds(2 * width + at, 2 * HD)]) + b_val_ref[:, pl.ds(at, 2 * HD)]
+        value = value.astype(low).astype(jnp.float32)
+        even, odd = 2 * pair, 2 * pair + 1
+        send_qkv[even, :rows] = join_heads(key, swap_halves(query)).astype(low)
+        send_qkv[odd, :rows] = join_heads(swap_halves(key), query).astype(low)
+        top, bottom = value[:half], value[half:]
+        send_qkv[even, rows:] = join_heads(top, swap_halves(bottom)).astype(low)
+        send_qkv[odd, rows:] = join_heads(swap_halves(top), bottom).astype(low)
+        return carried
+
+    lax.fori_loop(0, pairs, project, 0)
+    pl.semaphore_wait(barrier, count + dp_count - 2)
+
+    def send_projected(step, carried):
+        to = lax.rem(me + step, count)
+        exchange(send_qkv.at[to], recv_qkv.at[me], qkv_s.at[to], qkv_r.at[me], to).start()
+        exchange(send_qkv.at[0, pl.ds(0, rows)], first.at[me], first_s.at[to], first_r.at[me], to).start()
+        return carried
+
+    lax.fori_loop(1, count, send_projected, 0)
+    recv_qkv[me] = send_qkv[me]
+    first[me] = send_qkv[0, :rows]
+
+    ids = seg_ref[...]
+    start_one = jnp.sum(jnp.where(ids < 1, 1.0, 0.0), axis=1, keepdims=True)
+    start_two = jnp.sum(jnp.where(ids < 2, 1.0, 0.0), axis=1, keepdims=True)
+    square = (rows, rows)
+    row_at = lax.broadcasted_iota(jnp.int32, square, 0)
+    col_at = lax.broadcasted_iota(jnp.int32, square, 1)
+    lower[...] = jnp.where(row_at > col_at, -coeff, 0.0).astype(low)
+    upper[...] = jnp.where(row_at < col_at, -coeff, 0.0).astype(low)
+
+    def masks(i, j):
+        query_pos = lax.broadcasted_iota(jnp.int32, (rows, 1), 0).astype(jnp.float32) + (i * rows).astype(jnp.float32)
+        key_pos = lax.broadcasted_iota(jnp.int32, square, 1).astype(jnp.float32) + (j * rows).astype(jnp.float32)
+        begin = jnp.where(
+            query_pos >= start_two, start_two, jnp.where(query_pos >= start_one, start_one, 0.0)
+        )
+        inside = key_pos >= begin
+        return inside & (key_pos <= query_pos), inside & (key_pos < query_pos)
+
+    def needs_mask(i, j):
+        return (j == 0) | (j == i) | (i == count - 1)
+
+    def pair_at(i, j):
+        return i * (i + 1) // 2 + j
+
+    carry[...] = jnp.zeros_like(carry)
+
+    def forward_tile(i, j, masked):
+        start_scores = dot_nt(wide_first[...], first[j])
+        soft = jnp.maximum(start_scores, 0.0) + jnp.log(1.0 + jnp.exp(-jnp.abs(start_scores)))
+        gate = jnp.exp(start_scores - soft)
+        if masked:
+            attend, select = masks(i, j)
+            soft = jnp.where(select, soft, 0.0)
+            gate = jnp.where(select, gate, 0.0)
+        gates[pair_at(i, j)] = gate.astype(low)
+        soft_low = soft.astype(low)
+        forgot = dot_nn(lower[...], soft_low) + carry[j]
+        carry[j] = forgot[rows - 1 :] - coeff * soft_low[rows - 1 :].astype(jnp.float32)
+        scores = dot_nt(wide_q[...], recv_qkv[j, :rows]) + forgot
+        if masked:
+            scores = jnp.where(attend, scores, neg_large)
+        logit[j] = scores
+        top = row_top[...]
+        for at in range(0, rows, 2 * HD):
+            top = jnp.maximum(top, scores[:, at : at + 2 * HD])
+        row_top[...] = top
+
+    def forward_row(i, carried):
+        @pl.when(i != me)
+        def _():
+            exchange(send_qkv.at[i], recv_qkv.at[i], qkv_s.at[i], qkv_r.at[i], i).wait_recv()
+            exchange(send_qkv.at[0, pl.ds(0, rows)], first.at[i], first_s.at[i], first_r.at[i], i).wait_recv()
+
+        lane = lax.broadcasted_iota(jnp.int32, (rows, 2 * HD), 1)
+        query = swap_halves(recv_qkv[i, :rows].astype(jnp.float32))
+        wide_q[...] = jnp.where(lane < HD, query, 0.0).astype(low)
+        query_t[i] = query.T[:HD].astype(low)
+        query = swap_halves(first[i].astype(jnp.float32))
+        wide_first[...] = jnp.where(lane < HD, query, 0.0).astype(low)
+        first_t[i] = query.T[:HD].astype(low)
+        value = spread_rows(recv_qkv[i, rows:].astype(jnp.float32))
+        vals[i] = jnp.where(lane < HD, value, jnp.where(lane < HD + 2, 1.0, 0.0)).astype(low)
+        row_top[...] = jnp.full_like(row_top, neg_large)
+
+        def tiles(j, inner):
+            pl.when(needs_mask(i, j))(functools.partial(forward_tile, i, j, True))
+            pl.when(jnp.logical_not(needs_mask(i, j)))(functools.partial(forward_tile, i, j, False))
+            return inner
+
+        lax.fori_loop(0, i + 1, tiles, 0)
+        top = jnp.max(row_top[...], axis=1, keepdims=True)
+        row_acc[...] = jnp.zeros_like(row_acc)
+
+        def weigh(j, inner):
+            prob = jnp.exp(logit[j] - top).astype(low)
+            probs[pair_at(i, j)] = prob
+            row_acc[...] += dot_nn(prob, vals[j])
+            return inner
+
+        lax.fori_loop(0, i + 1, weigh, 0)
+        mixed = row_acc[...]
+        inverse = 1.0 / mixed[:, HD : HD + 1]
+        mixed = mixed * inverse
+        mixed_keep[i] = jnp.where(lane < HD, mixed, inverse)
+        send_mix[i] = fold_rows(mixed).astype(low)
+
+        @pl.when(i != me)
+        def _():
+            exchange(send_mix.at[i], recv_mix.at[me], mix_s.at[i], mix_r.at[me], i).start()
+
+        return carried
+
+    lax.fori_loop(0, count, forward_row, 0)
+    recv_mix[me] = send_mix[me]
+
+    for load in loads:
+        load.wait()
+
+    def wait_mixed(step, carried):
+        source = lax.rem(me + step, count)
+        exchange(send_mix.at[source], recv_mix.at[source], mix_s.at[source], mix_r.at[source], source).wait_recv()
+        return carried
+
+    lax.fori_loop(1, count, wait_mixed, 0)
+    for pair in range(pairs):
+        even = recv_mix[2 * pair].astype(jnp.float32)
+        odd = recv_mix[2 * pair + 1].astype(jnp.float32)
+        columns = pl.ds(pair * 2 * HD, 2 * HD)
+        mixed_ref[pl.ds(0, half), columns] = join_heads(even, swap_halves(odd)).astype(low)
+        mixed_ref[pl.ds(half, half), columns] = join_heads(swap_halves(even), odd).astype(low)
+    middle = tokens_ref[0].astype(jnp.float32) + dot_nn(mixed_ref[...], w_out_ref[...]) + b_out_ref[...]
+    middle_ref[...] = middle
+    unit, rstd = normalise(middle)
+    unit_two_ref[...] = unit
+    rstd_two_ref[...] = rstd
+    normed_two_ref[...] = (unit * gain_two_ref[...] + bias_two_ref[...]).astype(low)
+    out_acc[...] = jnp.zeros_like(out_acc)
+    gn_acc[...] = jnp.zeros_like(gn_acc)
+    core, x = lax.rem(dp, 2), dp // 2
+    y, z = lax.rem(me, 2), me // 2
+    mid_rows = mid_mine.shape[0]
+    core_dp = dp + 1 - 2 * core
+
+    def core_copy(at, size, slot):
+        return pltpu.make_async_remote_copy(
+            src_ref=mid_mine.at[pl.ds(pl.multiple_of((1 - core) * (mid_rows // 2) + at, 16), size)],
+            dst_ref=mid_core.at[pl.ds(pl.multiple_of(at, 16), size)],
+            send_sem=mid_cs.at[slot], recv_sem=mid_cr.at[slot],
+            device_id=(core_dp, me), device_id_type=MESH,
+        )
+
+    chunk = width
+
+    def dense(c, carried):
+        at = pl.multiple_of(c * chunk, chunk)
+        cols = pl.ds(at, chunk)
+        hidden = dot_nn(normed_two_ref[...], w_up_ref[:, cols]) + b_up_ref[:, cols]
+        cdf = exact_cdf(hidden)
+        slope = cdf + hidden * jnp.exp(-0.5 * hidden * hidden) * (1.0 / math.sqrt(2.0 * math.pi))
+        active = (hidden * cdf).astype(low)
+        out_acc[...] += dot_nn(active, w_down_ref[cols, :])
+        grad_hidden = (dot_nt(cot_ref[0], w_down_ref[cols, :]) * slope).astype(low)
+        mid_mine[cols, :] = dot_tn(active, cot_ref[0]).astype(low)
+        mid_mine[pl.ds(pl.multiple_of(mid_rows // 2 + at, 16), chunk), :] = dot_tn(
+            normed_two_ref[...], grad_hidden
+        ).astype(low)
+        vec_mid_mine[pl.ds(c, 1), :] = jnp.sum(grad_hidden.astype(jnp.float32), axis=0, keepdims=True)
+        gn_acc[...] += dot_nt(grad_hidden, w_up_ref[:, cols])
+        core_copy(at, chunk, c).start()
+        return carried
+
+    chunks = hidden_width // chunk
+    lax.fori_loop(0, chunks, dense, 0)
+    output_ref[0] = (middle_ref[...] + out_acc[...] + b_down_ref[...]).astype(low)
+    cot = cot_ref[0].astype(jnp.float32)
+    grad = gn_acc[...]
+    unit = unit_two_ref[...]
+    vec_mid_mine[pl.ds(chunks, 1), :] = jnp.sum(cot, axis=0, keepdims=True)
+    vec_mid_mine[pl.ds(chunks + 1, 1), :] = jnp.sum(grad * unit, axis=0, keepdims=True)
+    vec_mid_mine[pl.ds(chunks + 2, 1), :] = jnp.sum(grad, axis=0, keepdims=True)
+    middle = cot + normalise_back(grad, unit, rstd_two_ref[...], gain_two_ref[...])
+    middle_ref[...] = middle
+    branch = middle.astype(low)
+    vec_mid_mine[pl.ds(chunks + 3, 1), :] = jnp.sum(branch.astype(jnp.float32), axis=0, keepdims=True)
+    for pair in range(pairs):
+        back = dot_nt(branch, w_out_ref[pl.ds(pair * 2 * HD, 2 * HD), :]).astype(low).astype(jnp.float32)
+        top, bottom = back[:half], back[half:]
+        send_gmix[2 * pair] = join_heads(top, swap_halves(bottom)).astype(low)
+        send_gmix[2 * pair + 1] = join_heads(swap_halves(top), bottom).astype(low)
+
+    def send_grads(step, carried):
+        to = lax.rem(me + step, count)
+        exchange(send_gmix.at[to], recv_gmix.at[me], gmix_s.at[to], gmix_r.at[me], to).start()
+        return carried
+
+    lax.fori_loop(1, count, send_grads, 0)
+    recv_gmix[me] = send_gmix[me]
+    w_out_grad = dot_tn(mixed_ref[...], branch).astype(low)
+    mid_mine[pl.ds(hidden_width, width // 2), :] = w_out_grad[: width // 2]
+    mid_mine[pl.ds(mid_rows // 2 + hidden_width, width // 2), :] = w_out_grad[width // 2 :]
+    core_copy(hidden_width, width // 2, chunks).start()
+
+    def other(step_two):
+        along_x = (1 - core) if step_two else core
+        return (dp + along_x * (2 - 4 * x), me + (1 - along_x) * (1 - 2 * y))
+
+    two_bit = (1 - core) * x + core * y
+    three_bit = (1 - core) * y + core * x
+    piece_rows = 48
+
+    def add_rows(into, at, source, source_at, size):
+        def step(k, carried):
+            here = pl.ds(pl.multiple_of(at + k * piece_rows, 16), piece_rows)
+            there = pl.ds(pl.multiple_of(source_at + k * piece_rows, 16), piece_rows)
+            into[here, :] = (into[here, :].astype(jnp.float32) + source[there, :].astype(jnp.float32)).astype(low)
+            return carried
+
+        lax.fori_loop(0, size // piece_rows, step, 0)
+
+    def reducer(mine, final, core_got, two_got, three_got, four_got, send_sem, recv_sem):
+        total = mine.shape[0]
+        one = core * (total // 2)
+        keep_two, give_two = one + two_bit * (total // 4), one + (1 - two_bit) * (total // 4)
+        keep_three = keep_two + three_bit * (total // 8)
+        give_three = keep_two + (1 - three_bit) * (total // 8)
+        shard = total // 32
+        depth = count // 2
+
+        def remote(src, dst, slot, target):
+            return pltpu.make_async_remote_copy(
+                src_ref=src, dst_ref=dst, send_sem=send_sem.at[slot], recv_sem=recv_sem.at[slot],
+                device_id=target, device_id_type=MESH,
+            )
+
+        def piece(ref, at, size):
+            return ref.at[pl.ds(pl.multiple_of(at, 16), size)]
+
+        def scatter_core():
+            at = (1 - core) * (total // 2)
+            return remote(piece(mine, at, total // 2), core_got, 0, (core_dp, me))
+
+        copy_two = remote(piece(mine, give_two, total // 4), two_got, 1, other(True))
+        copy_three = remote(piece(mine, give_three, total // 8), three_got, 2, other(False))
+
+        def deep(step):
+            to_z = lax.rem(z + step, depth)
+            at = keep_three + to_z * shard
+            return pltpu.make_async_remote_copy(
+                src_ref=piece(mine, at, shard), dst_ref=four_got.at[depth - 1 - step],
+                send_sem=send_sem.at[2 + step], recv_sem=recv_sem.at[2 + step],
+                device_id=(dp, to_z * 2 + y), device_id_type=MESH,
+            )
+
+        def begin_two():
+            add_rows(mine, give_two, core_got, give_two - one, total // 4)
+            copy_two.start()
+            add_rows(mine, keep_two, core_got, keep_two - one, total // 4)
+
+        def begin_three():
+            copy_two.wait_recv()
+            add_rows(mine, give_three, two_got, give_three - keep_two, total // 8)
+            copy_three.start()
+            add_rows(mine, keep_three, two_got, keep_three - keep_two, total // 8)
+
+        def begin_deep():
+            copy_three.wait_recv()
+            add_rows(mine, keep_three, three_got, 0, total // 8)
+            for step in range(1, depth):
+                deep(step).start()
+
+        own = keep_three + z * shard
+
+        def gather_deep(step):
+            to_z = lax.rem(z + step, depth)
+            return pltpu.make_async_remote_copy(
+                src_ref=piece(final, own, shard), dst_ref=piece(final, own, shard),
+                send_sem=send_sem.at[5 + step], recv_sem=recv_sem.at[5 + step],
+                device_id=(dp, to_z * 2 + y), device_id_type=MESH,
+            )
+
+        def begin_gather():
+            for step in range(1, depth):
+                deep(step).wait_recv()
+
+            def step(k, carried):
+                at = pl.ds(pl.multiple_of(k * 16, 16), 16)
+                here = pl.ds(pl.multiple_of(own + k * 16, 16), 16)
+                summed = mine[here, :].astype(jnp.float32)
+                for slot in range(depth - 1):
+                    summed = summed + four_got[slot, at, :].astype(jnp.float32)
+                final[here, :] = summed.astype(low)
+                return carried
+
+            lax.fori_loop(0, shard // 16, step, 0)
+            for step in range(1, depth):
+                gather_deep(step).start()
+
+        back_three = remote(piece(final, keep_three, total // 8), piece(final, keep_three, total // 8), 9, other(False))
+        back_two = remote(piece(final, keep_two, total // 4), piece(final, keep_two, total // 4), 10, other(True))
+        back_core = remote(piece(final, one, total // 2), piece(final, one, total // 2), 11, (core_dp, me))
+
+        def gather_three():
+            for step in range(1, depth):
+                gather_deep(step).wait_recv()
+            back_three.start()
+
+        def gather_two():
+            back_three.wait_recv()
+            back_two.start()
+
+        def gather_core():
+            back_two.wait_recv()
+            back_core.start()
+
+        def finish():
+            back_core.wait_recv()
+
+        def drain(own_core):
+            if own_core:
+                scatter_core().wait_send()
+            copy_two.wait_send()
+            copy_three.wait_send()
+            for step in range(1, depth):
+                deep(step).wait_send()
+                gather_deep(step).wait_send()
+            back_three.wait_send()
+            back_two.wait_send()
+            back_core.wait_send()
+
+        return (scatter_core, begin_two, begin_three, begin_deep, begin_gather, gather_three, gather_two, gather_core, finish, drain)
+
+    def vector_sum(mine, seq_got, seq_sum, dp_got, base):
+        def over_seq(to, slot):
+            return pltpu.make_async_remote_copy(
+                src_ref=mine, dst_ref=seq_got.at[slot],
+                send_sem=vec_s.at[base, to], recv_sem=vec_r.at[base, slot],
+                device_id=(dp, to), device_id_type=MESH,
+            )
+
+        def over_dp(to, slot):
+            return pltpu.make_async_remote_copy(
+                src_ref=seq_sum, dst_ref=dp_got.at[slot],
+                send_sem=vec_s.at[base + 1, to], recv_sem=vec_r.at[base + 1, slot],
+                device_id=(to, me), device_id_type=MESH,
+            )
+
+        def start_seq():
+            def step(k, carried):
+                over_seq(lax.rem(me + k, count), me).start()
+                return carried
+
+            lax.fori_loop(1, count, step, 0)
+            seq_got[me] = mine[...]
+
+        def start_dp():
+            def step(k, carried):
+                source = lax.rem(me + k, count)
+                over_seq(source, source).wait_recv()
+                return carried
+
+            lax.fori_loop(1, count, step, 0)
+            summed = seq_got[0]
+            for k in range(1, count):
+                summed = summed + seq_got[k]
+            seq_sum[...] = summed
+
+            def send(k, carried):
+                over_dp(lax.rem(dp + k, dp_count), dp).start()
+                return carried
+
+            lax.fori_loop(1, dp_count, send, 0)
+            dp_got[dp] = seq_sum[...]
+
+        def finish():
+            def step(k, carried):
+                source = lax.rem(dp + k, dp_count)
+                over_dp(source, source).wait_recv()
+                return carried
+
+            lax.fori_loop(1, dp_count, step, 0)
+            summed = dp_got[0]
+            for k in range(1, dp_count):
+                summed = summed + dp_got[k]
+            return summed
+
+        def drain():
+            def step(k, carried):
+                over_seq(lax.rem(me + k, count), me).wait_send()
+                return carried
+
+            def send(k, carried):
+                over_dp(lax.rem(dp + k, dp_count), dp).wait_send()
+                return carried
+
+            lax.fori_loop(1, count, step, 0)
+            lax.fori_loop(1, dp_count, send, 0)
+
+        return start_seq, start_dp, finish, drain
+
+    mid_steps = reducer(mid_mine, mid_final, mid_core, mid_two, mid_three, mid_four, mid_s, mid_r)
+    in_steps = reducer(in_mine, in_final, in_core, in_two, in_three, in_four, in_s, in_r)
+    mid_vec = vector_sum(vec_mid_mine, vec_mid_seq, vec_mid_sum, vec_mid_dp, 0)
+    in_vec = vector_sum(vec_in_mine, vec_in_seq, vec_in_sum, vec_in_dp, 2)
+    mid_vec[0]()
+    for slot in range(chunks):
+        core_copy(slot * chunk, chunk, slot).wait_recv()
+    core_copy(hidden_width, width // 2, chunks).wait_recv()
+    mid_steps[1]()
+
+    dkv_acc[...] = jnp.zeros_like(dkv_acc)
+    dk0_acc[...] = jnp.zeros_like(dk0_acc)
+    back_carry[...] = jnp.zeros_like(back_carry)
+
+    def backward_tile(i, j):
+        prob = probs[pair_at(i, j)]
+        grad_logits = (prob.astype(jnp.float32) * dot_nt(grad_rows[...], vals[j])).astype(low)
+        dkv_acc[j, :HD] += dot_nn(grad_rows_t[...], prob)
+        dkv_acc[j, HD:] += dot_nn(query_t[i], grad_logits)
+        dq_acc[...] += dot_nn(grad_logits, recv_qkv[j, :rows])
+        later = dot_nn(upper[...], grad_logits) + back_carry[j]
+        back_carry[j] = later[:1] - coeff * grad_logits[:1].astype(jnp.float32)
+        gated = (later * gates[pair_at(i, j)].astype(jnp.float32)).astype(low)
+        dq0_acc[...] += dot_nn(gated, first[j])
+        dk0_acc[j, HD:] += dot_nn(first_t[i], gated)
+
+    def backward_row(step, carried):
+        i = count - 1 - step
+
+        @pl.when(i != me)
+        def _():
+            exchange(send_gmix.at[i], recv_gmix.at[i], gmix_s.at[i], gmix_r.at[i], i).wait_recv()
+
+        lane = lax.broadcasted_iota(jnp.int32, (rows, 2 * HD), 1)
+        grad = jnp.where(lane < HD, spread_rows(recv_gmix[i].astype(jnp.float32)), 0.0)
+        kept = mixed_keep[i]
+        inverse = kept[:, HD : HD + 1]
+        delta = -jnp.sum(grad * kept, axis=1, keepdims=True) * inverse
+        grad = grad * inverse
+        grad_rows_t[...] = grad.T[:HD].astype(low)
+        delta_high = delta.astype(low).astype(jnp.float32)
+        grad = jnp.where(lane == HD, delta_high, jnp.where(lane == HD + 1, delta - delta_high, grad))
+        grad_rows[...] = grad.astype(low)
+        dq_acc[...] = jnp.zeros_like(dq_acc)
+        dq0_acc[...] = jnp.zeros_like(dq0_acc)
+
+        def tiles(j, inner):
+            backward_tile(i, j)
+            return inner
+
+        lax.fori_loop(0, i + 1, tiles, 0)
+        flipped = dkv_acc[i].T
+        send_back[i, :rows] = join_heads(dq_acc[...] * score_scale, flipped).astype(low)
+        send_back[i, rows:] = fold_rows(flipped).astype(low)
+        send_first[i] = join_heads(dq0_acc[...] * score_scale, dk0_acc[i].T).astype(low)
+
+        @pl.when(i != me)
+        def _():
+            exchange(send_back.at[i], recv_back.at[me], back_s.at[i], back_r.at[me], i).start()
+            exchange(send_first.at[i], recv_first.at[me], fback_s.at[i], fback_r.at[me], i).start()
+
+        return carried
+
+    lax.fori_loop(0, count, backward_row, 0)
+    recv_back[me] = send_back[me]
+    recv_first[me] = send_first[me]
+    mid_steps[2]()
+    mid_vec[1]()
+
+    def wait_back(step, carried):
+        source = lax.rem(me + step, count)
+        exchange(send_back.at[source], recv_back.at[source], back_s.at[source], back_r.at[source], source).wait_recv()
+        exchange(send_first.at[source], recv_first.at[source], fback_s.at[source], fback_r.at[source], source).wait_recv()
+        return carried
+
+    lax.fori_loop(1, count, wait_back, 0)
+    first_sum = recv_first[0].astype(jnp.float32)
+    for source in range(1, count):
+        first_sum = first_sum + recv_first[source].astype(jnp.float32)
+    for pair in range(pairs):
+        even = recv_back[2 * pair, :rows].astype(jnp.float32)
+        odd = recv_back[2 * pair + 1, :rows].astype(jnp.float32)
+        if pair == 0:
+            even = even + first_sum
+        columns = 2 * HD * pair
+        joined_ref[:, pl.ds(columns, 2 * HD)] = join_heads(even, swap_halves(odd)).astype(low)
+        joined_ref[:, pl.ds(width + columns, 2 * HD)] = join_heads(swap_halves(even), odd).astype(low)
+        even = recv_back[2 * pair, rows:].astype(jnp.float32)
+        odd = recv_back[2 * pair + 1, rows:].astype(jnp.float32)
+        columns = pl.ds(2 * width + columns, 2 * HD)
+        joined_ref[pl.ds(0, half), columns] = join_heads(even, swap_halves(odd)).astype(low)
+        joined_ref[pl.ds(half, half), columns] = join_heads(swap_halves(even), odd).astype(low)
+
+    def project_back(c, carried):
+        cols = pl.ds(pl.multiple_of(c * width, width), width)
+        in_mine[cols, :] = dot_tn(normed_one_ref[...], joined_ref[:, cols]).astype(low)
+        return carried
+
+    lax.fori_loop(0, 3, project_back, 0)
+    in_steps[0]().start()
+    grad = dot_nt(joined_ref[...], w_qkv_ref[...])
+    unit = unit_one_ref[...]
+    vec_in_mine[...] = jnp.zeros_like(vec_in_mine)
+    vec_in_mine[pl.ds(0, 1), :] = jnp.sum(grad * unit, axis=0, keepdims=True)
+    vec_in_mine[pl.ds(1, 1), :] = jnp.sum(grad, axis=0, keepdims=True)
+    vec_in_mine[pl.ds(2, 1), :] = jnp.sum(joined_ref[:, pl.ds(2 * width, width)].astype(jnp.float32), axis=0, keepdims=True)
+    in_vec[0]()
+    tokens_grad_ref[0] = middle_ref[...] + normalise_back(grad, unit, rstd_one_ref[...], gain_one_ref[...])
+    in_steps[0]().wait_recv()
+    in_steps[1]()
+    mid_steps[3]()
+    in_steps[2]()
+    in_vec[1]()
+    vec_mid_ref[...] = mid_vec[2]()
+    mid_steps[4]()
+    in_steps[3]()
+    mid_steps[5]()
+    in_steps[4]()
+    mid_steps[6]()
+    in_steps[5]()
+    mid_steps[7]()
+    in_steps[6]()
+    mid_steps[8]()
+    stores = [
+        pltpu.make_async_copy(mid_final.at[pl.ds(0, hidden_width)], w_down_out, store_sem.at[0]),
+        pltpu.make_async_copy(mid_final.at[pl.ds(hidden_width, width // 2)], w_out_out.at[pl.ds(0, width // 2)], store_sem.at[1]),
+        pltpu.make_async_copy(mid_final.at[pl.ds(mid_rows // 2 + hidden_width, width // 2)], w_out_out.at[pl.ds(width // 2, width // 2)], store_sem.at[2]),
+    ]
+    for c in range(chunks):
+        stores.append(
+            pltpu.make_async_copy(
+                mid_final.at[pl.ds(mid_rows // 2 + c * chunk, chunk)],
+                w_up_out.at[:, pl.ds(c * chunk, chunk)], store_sem.at[3 + c],
+            )
+        )
+    for store in stores:
+        store.start()
+    in_steps[7]()
+    vec_in_ref[...] = in_vec[2]()
+    in_steps[8]()
+    for c in range(3):
+        store = pltpu.make_async_copy(
+            in_final.at[pl.ds(c * width, width)], w_qkv_out.at[:, pl.ds(c * width, width)],
+            store_sem.at[3 + chunks + c],
+        )
+        store.start()
+        stores.append(store)
+
+    def drain(step, carried):
+        to = lax.rem(me + step, count)
+        exchange(send_qkv.at[to], recv_qkv.at[me], qkv_s.at[to], qkv_r.at[me], to).wait_send()
+        exchange(send_qkv.at[0, pl.ds(0, rows)], first.at[me], first_s.at[to], first_r.at[me], to).wait_send()
+        exchange(send_mix.at[to], recv_mix.at[me], mix_s.at[to], mix_r.at[me], to).wait_send()
+        exchange(send_gmix.at[to], recv_gmix.at[me], gmix_s.at[to], gmix_r.at[me], to).wait_send()
+        exchange(send_back.at[to], recv_back.at[me], back_s.at[to], back_r.at[me], to).wait_send()
+        exchange(send_first.at[to], recv_first.at[me], fback_s.at[to], fback_r.at[me], to).wait_send()
+        return carried
+
+    lax.fori_loop(1, count, drain, 0)
+    for slot in range(chunks):
+        core_copy(slot * chunk, chunk, slot).wait_send()
+    core_copy(hidden_width, width // 2, chunks).wait_send()
+    mid_steps[9](False)
+    in_steps[9](True)
+    mid_vec[3]()
+    in_vec[3]()
+    for store in stores:
+        store.wait()
+
+
+def exchange_heads(
+    tokens, segment_ids, gain_one, bias_one, w_qkv, b_val, w_out, b_out,
+    gain_two, bias_two, w_up, b_up, w_down, b_down, cotangent,
+):
+    count, dp_count = lax.axis_size("seq"), lax.axis_size("dp")
+    rows, width = tokens.shape[1], tokens.shape[2]
+    hidden = w_up.shape[1]
+    half = rows // 2
+    tiles = count * (count + 1) // 2
+    wide = 2 * HD
+    f32 = jnp.float32
+    packed = rows + half
+    mid, inner = 2 * hidden + width, 3 * width
+    depth = count // 2
+
+    def vmem(*shape, dtype=low):
+        return pltpu.VMEM(shape, dtype)
+
+    def sems(*shape):
+        return pltpu.SemaphoreType.DMA(shape)
+
+    scratch = [
+        vmem(width, width), vmem(width, hidden), vmem(hidden, width), sems(3), sems(16),
+        vmem(count, packed, wide), vmem(count, packed, wide), vmem(count, rows, wide), vmem(count, rows, wide),
+        vmem(count, HD, rows), vmem(count, HD, rows), vmem(rows, wide), vmem(rows, wide),
+        vmem(tiles, rows, rows), vmem(tiles, rows, rows), vmem(count, rows, rows, dtype=f32),
+        vmem(count, 1, rows, dtype=f32), vmem(rows, wide, dtype=f32), vmem(rows, wide, dtype=f32), vmem(count, rows, wide, dtype=f32),
+        vmem(count, half, wide), vmem(count, half, wide), vmem(count, half, wide), vmem(count, half, wide), vmem(rows, wide), vmem(HD, rows),
+        vmem(rows, wide, dtype=f32), vmem(rows, wide, dtype=f32), vmem(count, wide, rows, dtype=f32), vmem(count, wide, rows, dtype=f32), vmem(count, 1, rows, dtype=f32),
+        vmem(count, packed, wide), vmem(count, packed, wide), vmem(count, rows, wide), vmem(count, rows, wide),
+        vmem(rows, rows), vmem(rows, rows),
+        vmem(rows, width), vmem(rows, width, dtype=f32), vmem(rows, 1, dtype=f32),
+        vmem(rows, width), vmem(rows, width, dtype=f32), vmem(rows, 1, dtype=f32), vmem(rows, width), vmem(rows, width, dtype=f32), vmem(rows, width, dtype=f32), vmem(rows, width, dtype=f32), vmem(rows, 3 * width),
+    ]
+    for total in (mid, inner):
+        scratch += [vmem(total, width), vmem(total, width), vmem(total // 2, width), vmem(total // 4, width), vmem(total // 8, width), vmem(depth - 1, total // 32, width)]
+    for _ in range(2):
+        scratch += [vmem(8, width, dtype=f32), vmem(count, 8, width, dtype=f32), vmem(8, width, dtype=f32), vmem(dp_count, 8, width, dtype=f32)]
+    scratch += [sems(count)] * 12
+    scratch += [sems(12)] * 4 + [sems(5), sems(5), sems(4, count), sems(4, count)]
+    in_vmem = pl.BlockSpec(memory_space=pltpu.VMEM)
+    anywhere = pl.BlockSpec(memory_space=pl.ANY)
+    specs = [in_vmem] * 15
+    for at in (6, 10, 12):
+        specs[at] = anywhere
+    shape = jax.ShapeDtypeStruct
+    results = pl.pallas_call(
+        layer_kernel,
+        out_shape=[
+            shape((1, rows, width), low), shape((1, rows, width), f32), shape((8, width), f32), shape((8, width), f32),
+            shape((hidden, width), low), shape((width, hidden), low), shape((width, width), low), shape((width, 3 * width), low),
+        ],
+        in_specs=specs,
+        out_specs=[in_vmem] * 4 + [anywhere] * 4,
+        scratch_shapes=scratch,
+        compiler_params=pltpu.CompilerParams(
+            collective_id=0, has_side_effects=True, vmem_limit_bytes=vmem_bytes
+        ),
+    )(
+        tokens, segment_ids, gain_one[None], bias_one[None], w_qkv, b_val[None], w_out, b_out[None],
+        gain_two[None], bias_two[None], w_up, b_up[None], w_down, b_down[None], cotangent,
+    )
+    output, tokens_grad, vec_mid, vec_in, w_down_grad, w_up_grad, w_out_grad, w_qkv_grad = results
+    chunks = hidden // width
+    return (
+        output,
+        tokens_grad,
+        vec_in[0],
+        vec_in[1],
+        w_qkv_grad.astype(f32),
+        vec_in[2],
+        w_out_grad.astype(f32),
+        vec_mid[chunks + 3],
+        vec_mid[chunks + 1],
+        vec_mid[chunks + 2],
+        w_up_grad.astype(f32),
+        vec_mid[:chunks].reshape(hidden),
+        w_down_grad.astype(f32),
+        vec_mid[chunks],
+    )
+
+
+def picks_heads(mesh, length, width, hidden):
+    dp_count, count = mesh.shape["dp"], mesh.shape["seq"]
+    power = length & (length - 1) == 0
+    return dp_count == 4 and count == 8 and width == count * HD and hidden == 4 * width and power
+
+
 def solution(mesh):
     placed = (
         P("dp", "seq", None),
@@ -390,8 +1203,15 @@
         P(),
         P("dp", "seq", None),
     )
+
+    def layer(tokens, *others):
+        width, hidden = tokens.shape[-1], others[9].shape[-1]
+        length = tokens.shape[1] * mesh.shape["seq"]
+        body = exchange_heads if picks_heads(mesh, length, width, hidden) else local
+        return body(tokens, *others)
+
     return jax.shard_map(
-        local,
+        layer,
         mesh=mesh,
         in_specs=placed,
         out_specs=(

time: 792 us -> 216 us (0.27)
  the two profiles are of different devices: /device:TPU:0 before, /device:TPU:29 now
where the time goes in v1:
time: 216 us; the launch traced here: 215 us
  Pallas kernels  200 us (93%)
  other arithmetic  10.1 us (5%)
  local copies, waits for them, and re-layouts  4.35 us (2%)
    pallas_call x1, Pallas kernels, exchange_heads(): pl.pallas_call(layer_kernel, out_shape=[shape((1, rows, width), low), sha...  200 us

profile of v1, /device:TPU:29, one launch (start us, length us, event | category | flops | bytes accessed | tf_op | source)
XLA Modules:
  0.0 215.2 jit_solution(2080385994516101605)
XLA Ops:
  0.7 200.2 %shard_map.254 = (bf16[1,256,512]{2,1,0:T(8,128)(2,1)}, f32[1,256,512]{2,1,0:T(8,128)}, f32[8,512]{1,0:T(8,128)}, f32[8,512]{1,0:T(8,128)}, bf16[2048,512]{1,0:T...) custom-call(bf16[1,256,512]{2,1,0:T(8,128)(2,1)} %tokens_ref.1, ...), custom_call_target="tpu_custom_call" | custom-call | tf_op jit(solution)/shard_map/pallas_call | solution.py:1146
  200.8 1.5 fusion
  202.3 0.7 slice_bitcast_fusion
  203.0 0.6 copy.29
  203.7 0.0 copy-start
  203.7 4.3 %convert_element_type.14 = f32[512,2048]{1,0:T(8,128)} convert(bf16[512,2048]{1,0:T(8,128)(2,1)} %get-tuple-element.28) | non-fusion elementwise | flops 1048576 | bytes 6291456 | tf_op jit(solution)/shard_map/convert_element_type | solution.py:1175
  207.9 0.0 copy-done
  207.9 0.0 copy-start.1
  207.9 2.6 %convert_element_type.15 = f32[2048,512]{1,0:T(8,128)} convert(bf16[2048,512]{1,0:T(8,128)(2,1)S(1)} %copy-done) | non-fusion elementwise | flops 1048576 | bytes 6291456 | tf_op jit(solution)/shard_map/convert_element_type | solution.py:1177
  210.5 0.0 copy-done.1
  210.5 0.0 copy-start.2
  210.6 0.0 copy-start.4
  210.6 2.1 convert_element_type.12
  212.6 0.0 copy-start.3
  212.6 0.0 copy-done.2
  212.6 1.1 convert_element_type.13
  213.7 0.0 copy-done.4
  213.7 0.7 copy.32
  214.4 0.0 copy-done.3
  214.4 0.8 copy.33
Async XLA Ops:
  203.7 4.3 %copy-start = (bf16[2048,512]{1,0:T(8,128)(2,1)S(1)}, bf16[2048,512]{1,0:T(8,128)(2,1)}, u32[]{:S(2)}) copy-start(bf16[2048,512]{1,0:T(8,128)(2,1)} %get-tuple-element.29) | copy-start | bytes 6291460
  207.9 2.6 %copy-start.1 = (bf16[512,1536]{1,0:T(8,128)(2,1)S(1)}, bf16[512,1536]{1,0:T(8,128)(2,1)}, u32[]{:S(2)}) copy-start(bf16[512,1536]{1,0:T(8,128)(2,1)} %get-tuple-element.25) | copy-start | bytes 4718596
  210.5 2.1 copy-start.2
  210.6 3.2 %copy-start.4 = (bf16[1,256,512]{2,1,0:T(8,128)(2,1)S(1)}, bf16[1,256,512]{2,1,0:T(8,128)(2,1)}, u32[]{:S(2)}) copy-start(bf16[1,256,512]{2,1,0:T(8,128)(2,1)} %get-tuple-element.54) | copy-start | bytes 786436
  212.6 1.8 copy-start.3

commit v2 on v0

--- a/solution.py
+++ b/solution.py
@@ -1,8 +1,11 @@
+import functools
 import math
 
 import jax
 import jax.numpy as jnp
 from jax import lax
+from jax.experimental import pallas as pl
+from jax.experimental.pallas import tpu as pltpu
 from jax.sharding import PartitionSpec as P
 
 HD = 64
@@ -12,6 +15,7 @@
 select_weight = 4.0
 neg_large = -1e30
 highest = lax.Precision.HIGHEST
+vmem_bytes = 63 * 1024 * 1024
 
 
 def prefix(array, axis, combine, identity, reverse):
@@ -372,6 +376,1042 @@
     )
 
 
+low = jnp.bfloat16
+MESH = pl.DeviceIdType.MESH
+
+
+def dot_nn(left, right):
+    return lax.dot_general(left, right, (((1,), (0,)), ((), ())), preferred_element_type=jnp.float32)
+
+
+def dot_nt(left, right):
+    return lax.dot_general(left, right, (((1,), (1,)), ((), ())), preferred_element_type=jnp.float32)
+
+
+def dot_tn(left, right):
+    return lax.dot_general(left, right, (((0,), (0,)), ((), ())), preferred_element_type=jnp.float32)
+
+
+def swap_halves(wide):
+    return pltpu.roll(wide, HD, 1)
+
+
+def left_lanes(shape):
+    return lax.broadcasted_iota(jnp.int32, shape, 1) < HD
+
+
+def join_heads(left, right):
+    return jnp.where(left_lanes(left.shape), left, right)
+
+
+def fold_rows(wide):
+    half = wide.shape[0] // 2
+    return join_heads(wide[:half], swap_halves(wide[half:]))
+
+
+def spread_rows(folded):
+    return jnp.concatenate([folded, swap_halves(folded)], axis=0)
+
+
+def exact_cdf(values):
+    return 0.5 * (1.0 + lax.erf(values * (1.0 / math.sqrt(2.0))))
+
+
+def normalise(values):
+    centered = values - jnp.mean(values, axis=-1, keepdims=True)
+    rstd = lax.rsqrt(jnp.mean(centered * centered, axis=-1, keepdims=True) + norm_eps)
+    return centered * rstd, rstd
+
+
+def normalise_back(grad, unit, rstd, gain):
+    scaled = grad * gain
+    mean_one = jnp.mean(scaled, axis=-1, keepdims=True)
+    mean_two = jnp.mean(scaled * unit, axis=-1, keepdims=True)
+    return rstd * (scaled - mean_one - unit * mean_two)
+
+
+def rows_of(ref, at, size):
+    return ref.at[pl.ds(pl.multiple_of(at, 16), size)]
+
+
+def add_rows(into, at, source, source_at, size, piece=16):
+    def step(k, carried):
+        here = pl.ds(pl.multiple_of(at + k * piece, 16), piece)
+        there = pl.ds(pl.multiple_of(source_at + k * piece, 16), piece)
+        summed = into[here, :].astype(jnp.float32) + source[there, :].astype(jnp.float32)
+        into[here, :] = summed.astype(low)
+        return carried
+
+    lax.fori_loop(0, size // piece, step, 0)
+
+
+class Places:
+    def __init__(self):
+        self.dp_count, self.count = lax.axis_size("dp"), lax.axis_size("seq")
+        self.dp, self.me = lax.axis_index("dp"), lax.axis_index("seq")
+        self.core, self.x = lax.rem(self.dp, 2), self.dp // 2
+        self.y, self.z = lax.rem(self.me, 2), self.me // 2
+        self.depth = self.count // 2
+        self.core_peer = (self.dp + 1 - 2 * self.core, self.me)
+        self.x_peer = (self.dp + 2 - 4 * self.x, self.me)
+        self.y_peer = (self.dp, self.me + 1 - 2 * self.y)
+        along_x = 1 - self.core
+        self.two_peer = (self.dp + along_x * (2 - 4 * self.x), self.me + (1 - along_x) * (1 - 2 * self.y))
+        self.three_peer = (self.dp + (1 - along_x) * (2 - 4 * self.x), self.me + along_x * (1 - 2 * self.y))
+        self.two_bit = along_x * self.x + (1 - along_x) * self.y
+        self.three_bit = (1 - along_x) * self.x + along_x * self.y
+        self.z_low, self.z_high = lax.rem(self.z, 2), self.z // 2
+        self.z_near = (self.dp, self.me + 2 * (1 - 2 * self.z_low))
+        self.z_far = (self.dp, self.me + 4 * (1 - 2 * self.z_high))
+
+
+def remote(src, dst, send_sem, recv_sem, target):
+    return pltpu.make_async_remote_copy(
+        src_ref=src, dst_ref=dst, send_sem=send_sem, recv_sem=recv_sem, device_id=target, device_id_type=MESH
+    )
+
+
+class StagedSum:
+    def __init__(self, at, mine, final, got, send_sem, recv_sem):
+        self.mine, self.final, self.got = mine, final, got
+        total = mine.shape[0]
+        bits = (at.core, at.two_bit, at.three_bit, at.z_low, at.z_high)
+        peers = (at.core_peer, at.two_peer, at.three_peer, at.z_near, at.z_far)
+        start, size = 0, total
+        self.down, self.up, self.keeps = [], [], []
+        for stage, (bit, peer) in enumerate(zip(bits, peers)):
+            size //= 2
+            keep, give = start + bit * size, start + (1 - bit) * size
+            self.keeps.append((start, keep, give, size))
+            self.down.append(
+                remote(rows_of(mine, give, size), got[stage], send_sem.at[stage], recv_sem.at[stage], peer)
+            )
+            self.up.append(
+                remote(
+                    rows_of(final, keep, size), rows_of(final, keep, size),
+                    send_sem.at[5 + stage], recv_sem.at[5 + stage], peer,
+                )
+            )
+            start = keep
+
+    def send(self, stage):
+        if stage > 0:
+            self.down[stage - 1].wait_recv()
+            begin, keep_before = self.keeps[stage - 1][1], self.keeps[stage]
+            _, keep, give, size = keep_before
+            add_rows(self.mine, give, self.got[stage - 1], give - begin, size)
+            self.down[stage].start()
+            add_rows(self.mine, keep, self.got[stage - 1], keep - begin, size)
+        else:
+            self.down[0].start()
+
+    def turn(self):
+        self.down[4].wait_recv()
+        _, keep, _, size = self.keeps[4]
+
+        def step(k, carried):
+            there = pl.ds(pl.multiple_of(k * 16, 16), 16)
+            here = pl.ds(pl.multiple_of(keep + k * 16, 16), 16)
+            summed = self.mine[here, :].astype(jnp.float32) + self.got[4][there, :].astype(jnp.float32)
+            self.final[here, :] = summed.astype(low)
+            return carried
+
+        lax.fori_loop(0, size // 16, step, 0)
+        self.up[4].start()
+
+    def gather(self, stage):
+        self.up[stage + 1].wait_recv()
+        self.up[stage].start()
+
+    def finish(self):
+        self.up[0].wait_recv()
+
+    def drain(self, first=0):
+        for copy in self.down[first:] + self.up:
+            copy.wait_send()
+
+
+class VectorSum:
+    def __init__(self, at, mine, seq_got, seq_sum, dp_got, send_sem, recv_sem, base):
+        self.at, self.mine, self.seq_got, self.seq_sum, self.dp_got = at, mine, seq_got, seq_sum, dp_got
+        self.send_sem, self.recv_sem, self.base = send_sem, recv_sem, base
+
+    def over_seq(self, to, slot):
+        return remote(
+            self.mine, self.seq_got.at[slot], self.send_sem.at[self.base, to], self.recv_sem.at[self.base, slot],
+            (self.at.dp, to),
+        )
+
+    def over_dp(self, to, slot):
+        return remote(
+            self.seq_sum, self.dp_got.at[slot], self.send_sem.at[self.base + 1, to],
+            self.recv_sem.at[self.base + 1, slot], (to, self.at.me),
+        )
+
+    def each(self, count, mine, act):
+        def step(k, carried):
+            act(lax.rem(mine + k, count))
+            return carried
+
+        lax.fori_loop(1, count, step, 0)
+
+    def start_seq(self):
+        at = self.at
+        self.each(at.count, at.me, lambda to: self.over_seq(to, at.me).start())
+        self.seq_got[at.me] = self.mine[...]
+
+    def start_dp(self):
+        at = self.at
+        self.each(at.count, at.me, lambda source: self.over_seq(source, source).wait_recv())
+        summed = self.seq_got[0]
+        for k in range(1, at.count):
+            summed = summed + self.seq_got[k]
+        self.seq_sum[...] = summed
+        self.each(at.dp_count, at.dp, lambda to: self.over_dp(to, at.dp).start())
+        self.dp_got[at.dp] = summed
+
+    def finish(self):
+        at = self.at
+        self.each(at.dp_count, at.dp, lambda source: self.over_dp(source, source).wait_recv())
+        summed = self.dp_got[0]
+        for k in range(1, at.dp_count):
+            summed = summed + self.dp_got[k]
+        return summed
+
+    def drain(self):
+        at = self.at
+        self.each(at.count, at.me, lambda to: self.over_seq(to, at.me).wait_send())
+        self.each(at.dp_count, at.dp, lambda to: self.over_dp(to, at.dp).wait_send())
+
+
+def layer_kernel(
+    tokens_ref,
+    seg_ref,
+    gain_one_ref,
+    bias_one_ref,
+    w_qkv_ref,
+    b_val_ref,
+    w_out_hbm,
+    b_out_ref,
+    gain_two_ref,
+    bias_two_ref,
+    w_up_hbm,
+    b_up_ref,
+    w_down_hbm,
+    b_down_ref,
+    cot_ref,
+    output_ref,
+    tokens_grad_ref,
+    vec_mid_ref,
+    vec_in_ref,
+    w_down_out,
+    w_up_out,
+    w_out_out,
+    w_qkv_out,
+    first_out,
+    *scratch,
+):
+    (
+        w_out_ref, w_up_ref, w_down_ref, load_sem, store_sem,
+        normed_all, w_head, w_value, b_value, key_query, first, vals, query_t, first_t, wide_q, wide_first,
+        probs, gates, logit, carry, row_top, row_acc, mixed_keep,
+        send_mix, recv_mix, send_gmix, recv_gmix, grad_rows, grad_rows_t,
+        dq_acc, dq0_acc, dkv_acc, dk0_acc, back_carry,
+        send_back, recv_back, send_first, y_first, recv_first,
+        lower, upper,
+        unit_one_ref, rstd_one_ref, unit_two_ref, rstd_two_ref,
+        mixed_ref, normed_two_ref, middle_ref, out_acc, gn_acc, joined_ref,
+        near_mine, near_final, near_core, near_two, near_three, near_four, near_five,
+        rest_mine, rest_final, rest_core, rest_two, rest_three, rest_four, rest_five,
+        wkv_acc, wqq_acc, wk0_acc, in_mine, in_core, in_x, in_final,
+        extra_mine, extra_seq, extra_sum, extra_dp, extra_all,
+        vec_mid_mine, vec_mid_seq, vec_mid_sum, vec_mid_dp,
+        vec_in_mine, vec_in_seq, vec_in_sum, vec_in_dp,
+        norm_y, norm_up, norm_down, norm_r, mix_s, mix_r, gmix_s, gmix_r,
+        back_s, back_r, fback_y, fback_yr, fback_s, fback_r, extra_s, extra_r, gather_s, gather_r,
+        near_s, near_r, rest_s, rest_r, in_s, in_r, part_s, part_r, vec_s, vec_r, edp_s, edp_r,
+    ) = scratch
+    at = Places()
+    dp_count, count, dp, me = at.dp_count, at.count, at.dp, at.me
+    y, z, depth = at.y, at.z, at.depth
+    rows, width = tokens_ref.shape[1], tokens_ref.shape[2]
+    half, wide = rows // 2, 2 * HD
+    coeff = select_weight / (rows * count)
+    hidden_width = w_up_hbm.shape[1]
+    pairs = width // wide
+    score_scale = 1.0 / math.sqrt(HD)
+
+    barrier = pltpu.get_barrier_semaphore()
+
+    def greet_seq(step, carried):
+        to = lax.rem(me + step, count)
+        pl.semaphore_signal(barrier, inc=1, device_id=(dp, to), device_id_type=MESH)
+        return carried
+
+    def greet_dp(step, carried):
+        to = lax.rem(dp + step, dp_count)
+        pl.semaphore_signal(barrier, inc=1, device_id=(to, me), device_id_type=MESH)
+        return carried
+
+    lax.fori_loop(1, count, greet_seq, 0)
+    lax.fori_loop(1, dp_count, greet_dp, 0)
+    loads = [
+        pltpu.make_async_copy(w_out_hbm, w_out_ref, load_sem.at[0]),
+        pltpu.make_async_copy(w_up_hbm, w_up_ref, load_sem.at[1]),
+        pltpu.make_async_copy(w_down_hbm, w_down_ref, load_sem.at[2]),
+    ]
+    for load in loads:
+        load.start()
+
+    def exchange(src, dst, send_sem, recv_sem, target):
+        return remote(src, dst, send_sem, recv_sem, (dp, target))
+
+    tokens = tokens_ref[0].astype(jnp.float32)
+    unit, rstd = normalise(tokens)
+    unit_one_ref[...] = unit
+    rstd_one_ref[...] = rstd
+    normed_all[me] = (unit * gain_one_ref[...] + bias_one_ref[...]).astype(low)
+    pl.semaphore_wait(barrier, count + dp_count - 2)
+
+    def pass_y(block):
+        return exchange(normed_all.at[block], normed_all.at[block], norm_y.at[block], norm_r.at[block], z * 2 + 1 - y)
+
+    def pass_up(block):
+        return exchange(normed_all.at[block], normed_all.at[block], norm_up.at[block], norm_r.at[block], me + 2)
+
+    def pass_down(block):
+        return exchange(normed_all.at[block], normed_all.at[block], norm_down.at[block], norm_r.at[block], me - 2)
+
+    def arrived(block):
+        exchange(normed_all.at[block], normed_all.at[block], norm_y.at[block], norm_r.at[block], block).wait_recv()
+
+    def has_up(zz):
+        return zz < depth - 1
+
+    pl.when(has_up(z))(lambda: pass_up(me).start())
+    pl.when(z > 0)(lambda: pass_down(me).start())
+    pass_y(me).start()
+
+    def relay(distance):
+        def from_below():
+            block = me - 2 * distance
+            arrived(block)
+            pl.when(has_up(z))(lambda: pass_up(block).start())
+            pass_y(block).start()
+
+        def from_above():
+            block = me + 2 * distance
+            arrived(block)
+            pl.when(z > 0)(lambda: pass_down(block).start())
+            pass_y(block).start()
+
+        pl.when(z - distance >= 0)(from_below)
+        pl.when(z + distance < depth)(from_above)
+
+    odd_head = lax.rem(me, 2) == 1
+    pair_at_lane = pl.multiple_of((me // 2) * wide, wide)
+
+    def head_columns(part, right):
+        columns = w_qkv_ref[:, pl.ds(part * width + pair_at_lane, wide)].astype(jnp.float32)
+        swapped = swap_halves(columns)
+        return jnp.where(odd_head, columns, swapped) if right else jnp.where(odd_head, swapped, columns)
+
+    w_head[:, :wide] = join_heads(head_columns(1, False), head_columns(0, True) * score_scale).astype(low)
+    zero_query = swap_halves(w_qkv_ref[:, :wide].astype(jnp.float32)) * score_scale
+    w_head[:, wide:] = join_heads(w_qkv_ref[:, width : width + wide].astype(jnp.float32), zero_query).astype(low)
+    w_value[...] = head_columns(2, False).astype(low)
+    bias = b_val_ref[:, pl.ds(pair_at_lane, wide)]
+    b_value[...] = jnp.where(odd_head, swap_halves(bias), bias)
+
+    ids = seg_ref[...]
+    start_one = jnp.sum(jnp.where(ids < 1, 1.0, 0.0), axis=1, keepdims=True)
+    start_two = jnp.sum(jnp.where(ids < 2, 1.0, 0.0), axis=1, keepdims=True)
+    square = (rows, rows)
+    row_at = lax.broadcasted_iota(jnp.int32, square, 0)
+    col_at = lax.broadcasted_iota(jnp.int32, square, 1)
+    lower[...] = jnp.where(row_at > col_at, -coeff, 0.0).astype(low)
+    upper[...] = jnp.where(row_at < col_at, -coeff, 0.0).astype(low)
+    lane = lax.broadcasted_iota(jnp.int32, (rows, wide), 1)
+
+    def masks(i, j):
+        query_pos = lax.broadcasted_iota(jnp.int32, (rows, 1), 0).astype(jnp.float32) + (i * rows).astype(jnp.float32)
+        key_pos = lax.broadcasted_iota(jnp.int32, square, 1).astype(jnp.float32) + (j * rows).astype(jnp.float32)
+        begin = jnp.where(
+            query_pos >= start_two, start_two, jnp.where(query_pos >= start_one, start_one, 0.0)
+        )
+        inside = key_pos >= begin
+        return inside & (key_pos <= query_pos), inside & (key_pos < query_pos)
+
+    def needs_mask(i, j):
+        return (j == 0) | (j == i) | (i == count - 1)
+
+    def pair_at(i, j):
+        return i * (i + 1) // 2 + j
+
+    carry[...] = jnp.zeros_like(carry)
+    row_top[...] = jnp.full_like(row_top, neg_large)
+
+    def project(block):
+        normed = normed_all[block]
+        both = dot_nn(normed, w_head[...]).astype(low)
+        key_query[block] = both[:, :wide]
+        query = swap_halves(both[:, :wide].astype(jnp.float32))
+        wide_q[block] = jnp.where(lane < HD, query, 0.0).astype(low)
+        query_t[block] = query.T[:HD].astype(low)
+        first[block] = both[:, wide:]
+        query = swap_halves(both[:, wide:].astype(jnp.float32))
+        wide_first[block] = jnp.where(lane < HD, query, 0.0).astype(low)
+        first_t[block] = query.T[:HD].astype(low)
+        value = dot_nn(normed, w_value[...]) + b_value[...]
+        vals[block] = jnp.where(lane < HD, value, jnp.where(lane < HD + 2, 1.0, 0.0)).astype(low)
+
+    def forward_tile(i, j, masked):
+        start_scores = dot_nt(wide_first[i], first[j])
+        soft = jnp.maximum(start_scores, 0.0) + jnp.log(1.0 + jnp.exp(-jnp.abs(start_scores)))
+        gate = jnp.exp(start_scores - soft)
+        if masked:
+            attend, select = masks(i, j)
+            soft = jnp.where(select, soft, 0.0)
+            gate = jnp.where(select, gate, 0.0)
+        gates[pair_at(i, j)] = gate.astype(low)
+        soft_low = soft.astype(low)
+        forgot = dot_nn(lower[...], soft_low) + carry[j]
+        carry[j] = forgot[rows - 1 :] - coeff * soft_low[rows - 1 :].astype(jnp.float32)
+        scores = dot_nt(wide_q[i], key_query[j]) + forgot
+        if masked:
+            scores = jnp.where(attend, scores, neg_large)
+        logit[pair_at(i, j)] = scores
+        top = row_top[i]
+        for start in range(0, rows, wide):
+            top = jnp.maximum(top, scores[:, start : start + wide])
+        row_top[i] = top
+
+    def weigh_row(i):
+        top = jnp.max(row_top[i], axis=1, keepdims=True)
+        row_acc[...] = jnp.zeros_like(row_acc)
+
+        def weigh(j, inner):
+            prob = jnp.exp(logit[pair_at(i, j)] - top).astype(low)
+            probs[pair_at(i, j)] = prob
+            row_acc[...] += dot_nn(prob, vals[j])
+            return inner
+
+        lax.fori_loop(0, i + 1, weigh, 0)
+        mixed = row_acc[...]
+        inverse = 1.0 / mixed[:, HD : HD + 1]
+        mixed = mixed * inverse
+        mixed_keep[i] = jnp.where(lane < HD, mixed, inverse)
+        send_mix[i] = fold_rows(mixed).astype(low)
+
+        @pl.when(i != me)
+        def _():
+            exchange(send_mix.at[i], recv_mix.at[me], mix_s.at[i], mix_r.at[me], i).start()
+
+    upwards = 1 - z // (depth // 2)
+    at_end = (z == 0) | (z == depth - 1)
+    pl.when(jnp.logical_not(at_end))(functools.partial(relay, 1))
+
+    def forward_step(step, carried):
+        block = upwards * step + (1 - upwards) * (count - 1 - step)
+        group = step // 2
+
+        @pl.when(lax.rem(block, 2) != y)
+        def _():
+            arrived(block)
+            for distance in range(1, depth):
+                pl.when(at_end & (group + 1 == distance))(functools.partial(relay, distance))
+                pl.when(jnp.logical_not(at_end) & (group + 2 == distance))(functools.partial(relay, distance))
+
+        project(block)
+
+        def tiles(k, inner):
+            i = upwards * step + (1 - upwards) * (block + k)
+            j = upwards * k + (1 - upwards) * block
+            pl.when(needs_mask(i, j))(functools.partial(forward_tile, i, j, True))
+            pl.when(jnp.logical_not(needs_mask(i, j)))(functools.partial(forward_tile, i, j, False))
+            return inner
+
+        lax.fori_loop(0, step + 1, tiles, 0)
+        pl.when(upwards == 1)(functools.partial(weigh_row, block))
+        return carried
+
+    lax.fori_loop(0, count, forward_step, 0)
+
+    def late_weigh(i, carried):
+        weigh_row(i)
+        return carried
+
+    lax.fori_loop(0, (1 - upwards) * count, late_weigh, 0)
+    recv_mix[me] = send_mix[me]
+
+    for load in loads:
+        load.wait()
+
+    def wait_mixed(step, carried):
+        source = lax.rem(me + step, count)
+        exchange(send_mix.at[source], recv_mix.at[source], mix_s.at[source], mix_r.at[source], source).wait_recv()
+        return carried
+
+    lax.fori_loop(1, count, wait_mixed, 0)
+    for pair in range(pairs):
+        even = recv_mix[2 * pair].astype(jnp.float32)
+        odd = recv_mix[2 * pair + 1].astype(jnp.float32)
+        columns = pl.ds(pair * wide, wide)
+        mixed_ref[pl.ds(0, half), columns] = join_heads(even, swap_halves(odd)).astype(low)
+        mixed_ref[pl.ds(half, half), columns] = join_heads(swap_halves(even), odd).astype(low)
+    middle = tokens_ref[0].astype(jnp.float32) + dot_nn(mixed_ref[...], w_out_ref[...]) + b_out_ref[...]
+    middle_ref[...] = middle
+    unit, rstd = normalise(middle)
+    unit_two_ref[...] = unit
+    rstd_two_ref[...] = rstd
+    normed_two_ref[...] = (unit * gain_two_ref[...] + bias_two_ref[...]).astype(low)
+    out_acc[...] = jnp.zeros_like(out_acc)
+    gn_acc[...] = jnp.zeros_like(gn_acc)
+    near_sum = StagedSum(at, near_mine, near_final, [near_core, near_two, near_three, near_four, near_five], near_s, near_r)
+    rest_sum = StagedSum(at, rest_mine, rest_final, [rest_core, rest_two, rest_three, rest_four, rest_five], rest_s, rest_r)
+    mid_vec = VectorSum(at, vec_mid_mine, vec_mid_seq, vec_mid_sum, vec_mid_dp, vec_s, vec_r, 0)
+    in_vec = VectorSum(at, vec_in_mine, vec_in_seq, vec_in_sum, vec_in_dp, vec_s, vec_r, 2)
+    chunk = width
+    chunks = hidden_width // chunk
+    near_rows, rest_rows = near_mine.shape[0] // 2, rest_mine.shape[0] // 2
+
+    def dense(sums, base, c, carried):
+        start = pl.multiple_of((base + c) * chunk, chunk)
+        cols = pl.ds(start, chunk)
+        hidden = dot_nn(normed_two_ref[...], w_up_ref[:, cols]) + b_up_ref[:, cols]
+        cdf = exact_cdf(hidden)
+        slope = cdf + hidden * jnp.exp(-0.5 * hidden * hidden) * (1.0 / math.sqrt(2.0 * math.pi))
+        active = (hidden * cdf).astype(low)
+        out_acc[...] += dot_nn(active, w_down_ref[cols, :])
+        grad_hidden = (dot_nt(cot_ref[0], w_down_ref[cols, :]) * slope).astype(low)
+        here = pl.multiple_of(c * chunk, chunk)
+        sums[pl.ds(here, chunk), :] = dot_tn(active, cot_ref[0]).astype(low)
+        there = pl.multiple_of(sums.shape[0] // 2 + here, 16)
+        sums[pl.ds(there, chunk), :] = dot_tn(normed_two_ref[...], grad_hidden).astype(low)
+        vec_mid_mine[pl.ds(base + c, 1), :] = jnp.sum(grad_hidden.astype(jnp.float32), axis=0, keepdims=True)
+        gn_acc[...] += dot_nt(grad_hidden, w_up_ref[:, cols])
+        return carried
+
+    lax.fori_loop(0, chunks // 2, functools.partial(dense, near_mine, 0), 0)
+    near_sum.send(0)
+    lax.fori_loop(0, chunks // 2, functools.partial(dense, rest_mine, chunks // 2), 0)
+    near_sum.send(1)
+    cot = cot_ref[0].astype(jnp.float32)
+    grad = gn_acc[...]
+    unit = unit_two_ref[...]
+    middle = cot + normalise_back(grad, unit, rstd_two_ref[...], gain_two_ref[...])
+    output_ref[0] = (middle_ref[...] + out_acc[...] + b_down_ref[...]).astype(low)
+    middle_ref[...] = middle
+    branch = middle.astype(low)
+    for pair in range(pairs):
+        back = dot_nt(branch, w_out_ref[pl.ds(pair * wide, wide), :]).astype(low).astype(jnp.float32)
+        top, bottom = back[:half], back[half:]
+        send_gmix[2 * pair] = join_heads(top, swap_halves(bottom)).astype(low)
+        send_gmix[2 * pair + 1] = join_heads(swap_halves(top), bottom).astype(low)
+
+    def send_grads(step, carried):
+        to = lax.rem(me + step, count)
+        exchange(send_gmix.at[to], recv_gmix.at[me], gmix_s.at[to], gmix_r.at[me], to).start()
+        return carried
+
+    lax.fori_loop(1, count, send_grads, 0)
+    recv_gmix[me] = send_gmix[me]
+    w_out_grad = dot_tn(mixed_ref[...], branch).astype(low)
+    quarter = (chunks // 2) * chunk
+    rest_mine[pl.ds(quarter, width // 2), :] = w_out_grad[: width // 2]
+    rest_mine[pl.ds(rest_rows + quarter, width // 2), :] = w_out_grad[width // 2 :]
+    rest_sum.send(0)
+    vec_mid_mine[pl.ds(chunks, 1), :] = jnp.sum(cot, axis=0, keepdims=True)
+    vec_mid_mine[pl.ds(chunks + 1, 1), :] = jnp.sum(grad * unit, axis=0, keepdims=True)
+    vec_mid_mine[pl.ds(chunks + 2, 1), :] = jnp.sum(grad, axis=0, keepdims=True)
+    vec_mid_mine[pl.ds(chunks + 3, 1), :] = jnp.sum(branch.astype(jnp.float32), axis=0, keepdims=True)
+    mid_vec.start_seq()
+    rest_sum.send(1)
+
+    dkv_acc[...] = jnp.zeros_like(dkv_acc)
+    dk0_acc[...] = jnp.zeros_like(dk0_acc)
+    back_carry[...] = jnp.zeros_like(back_carry)
+    wkv_acc[...] = jnp.zeros_like(wkv_acc)
+    wqq_acc[...] = jnp.zeros_like(wqq_acc)
+    wk0_acc[...] = jnp.zeros_like(wk0_acc)
+
+    def backward_tile(i, j):
+        prob = probs[pair_at(i, j)]
+        grad_logits = (prob.astype(jnp.float32) * dot_nt(grad_rows[...], vals[j])).astype(low)
+        dkv_acc[j, :HD] += dot_nn(grad_rows_t[...], prob)
+        dkv_acc[j, HD:] += dot_nn(query_t[i], grad_logits)
+        dq_acc[...] += dot_nn(grad_logits, key_query[j])
+        later = dot_nn(upper[...], grad_logits) + back_carry[j]
+        back_carry[j] = later[:1] - coeff * grad_logits[:1].astype(jnp.float32)
+        gated = (later * gates[pair_at(i, j)].astype(jnp.float32)).astype(low)
+        dq0_acc[...] += dot_nn(gated, first[j])
+        dk0_acc[j] += dot_nn(first_t[i], gated)
+
+    def send_first_sum(i):
+        exchange(send_first.at[i], y_first.at[i], fback_y.at[i], fback_yr.at[i], i).wait_recv()
+        send_first[i] = (send_first[i].astype(jnp.float32) + y_first[i].astype(jnp.float32)).astype(low)
+
+        @pl.when(i != me)
+        def _():
+            exchange(send_first.at[i], recv_first.at[z], fback_s.at[i], fback_r.at[z], i).start()
+
+        @pl.when(i == me)
+        def _():
+            recv_first[z] = send_first[i]
+
+    def backward_row(step, carried):
+        i = count - 1 - step
+
+        @pl.when(i != me)
+        def _():
+            exchange(send_gmix.at[i], recv_gmix.at[i], gmix_s.at[i], gmix_r.at[i], i).wait_recv()
+
+        grad = jnp.where(lane < HD, spread_rows(recv_gmix[i].astype(jnp.float32)), 0.0)
+        kept = mixed_keep[i]
+        inverse = kept[:, HD : HD + 1]
+        delta = -jnp.sum(grad * kept, axis=1, keepdims=True) * inverse
+        grad = grad * inverse
+        grad_rows_t[...] = grad.T[:HD].astype(low)
+        delta_high = delta.astype(low).astype(jnp.float32)
+        grad = jnp.where(lane == HD, delta_high, jnp.where(lane == HD + 1, delta - delta_high, grad))
+        grad_rows[...] = grad.astype(low)
+        dq_acc[...] = jnp.zeros_like(dq_acc)
+        dq0_acc[...] = jnp.zeros_like(dq0_acc)
+
+        def tiles(j, inner):
+            backward_tile(i, j)
+            return inner
+
+        lax.fori_loop(0, i + 1, tiles, 0)
+        flat = dkv_acc[i]
+        flipped = flat.T
+        queries = join_heads(dq_acc[...], swap_halves(dq0_acc[...])) * score_scale
+        first_keys = dk0_acc[i]
+        first_flipped = jnp.concatenate([first_keys, first_keys], axis=0).T
+        send_back[i, :rows] = join_heads(queries, flipped).astype(low)
+        send_back[i, rows:] = fold_rows(flipped).astype(low)
+        send_first[i] = join_heads(swap_halves(queries), first_flipped).astype(low)
+
+        @pl.when(i != me)
+        def _():
+            exchange(send_back.at[i], recv_back.at[me], back_s.at[i], back_r.at[me], i).start()
+
+        @pl.when(lax.rem(i, 2) != y)
+        def _():
+            exchange(send_first.at[i], y_first.at[i], fback_y.at[i], fback_yr.at[i], z * 2 + 1 - y).start()
+
+        normed = normed_all[i]
+        wkv_acc[...] += dot_nn(flat.astype(low), normed)
+        wqq_acc[...] += dot_nn(queries.T.astype(low), normed)
+        wk0_acc[...] += dot_nn(first_keys.astype(low), normed)
+        pl.when((step >= 2) & (lax.rem(i, 2) == y))(lambda: send_first_sum(i + 2))
+        pl.when(step == 0)(lambda: near_sum.send(2))
+        pl.when(step == 1)(lambda: rest_sum.send(2))
+        pl.when(step == 2)(mid_vec.start_dp)
+        pl.when(step == 3)(lambda: near_sum.send(3))
+        pl.when(step == 5)(lambda: rest_sum.send(3))
+        return carried
+
+    lax.fori_loop(0, count, backward_row, 0)
+    recv_back[me] = send_back[me]
+
+    piece = HD // 4
+    for part in range(4):
+        for place, (source, start) in enumerate(((wqq_acc, 0), (wkv_acc, HD), (wkv_acc, 0))):
+            rows_in = pl.ds(part * 3 * piece + place * piece, piece)
+            in_mine[rows_in, :] = source[start + part * piece : start + (part + 1) * piece].astype(low)
+    extra_mine[:HD] = wqq_acc[HD:].astype(low)
+    extra_mine[HD:] = wk0_acc[...].astype(low)
+    core_half, x_half = 6 * piece, 3 * piece
+    in_core_copy = remote(rows_of(in_mine, (1 - at.core) * core_half, core_half), in_core, part_s.at[0], part_r.at[0], at.core_peer)
+    in_core_copy.start()
+
+    def extra_over_seq(to, slot):
+        return exchange(rows_of(extra_mine, to * piece, piece), extra_seq.at[slot], extra_s.at[to], extra_r.at[slot], to)
+
+    def extra_gather(to, owner):
+        return exchange(rows_of(extra_all, owner * piece, piece), rows_of(extra_all, owner * piece, piece), gather_s.at[to], gather_r.at[owner], to)
+
+    def extra_over_dp(to, slot):
+        return remote(extra_sum, extra_dp.at[slot], edp_s.at[to], edp_r.at[slot], (to, me))
+
+    each_seq = functools.partial(in_vec.each, count, me)
+    each_dp = functools.partial(in_vec.each, dp_count, dp)
+    each_seq(lambda to: extra_over_seq(to, me).start())
+    extra_seq[me] = extra_mine[pl.ds(pl.multiple_of(me * piece, 16), piece), :]
+    for i in (1, 0):
+        pl.when(y == i)(functools.partial(send_first_sum, i))
+    in_core_copy.wait_recv()
+    in_start = at.core * core_half
+    add_rows(in_mine, in_start, in_core, 0, core_half)
+    in_x_copy = remote(rows_of(in_mine, in_start + (1 - at.x) * x_half, x_half), in_x, part_s.at[1], part_r.at[1], at.x_peer)
+    in_x_copy.start()
+    near_sum.send(4)
+    in_start = in_start + at.x * x_half
+    in_x_copy.wait_recv()
+
+    shard = x_half
+    in_three = ((at.core * 2 + at.two_bit) * 2 + at.three_bit) * depth * shard
+    in_own = in_three + z * shard
+
+    def last_add(k, carried):
+        here = pl.ds(pl.multiple_of(in_own + k * 16, 16), 16)
+        mine = pl.ds(pl.multiple_of(in_start + k * 16, 16), 16)
+        there = pl.ds(pl.multiple_of(k * 16, 16), 16)
+        in_final[here, :] = (in_mine[mine, :].astype(jnp.float32) + in_x[there, :].astype(jnp.float32)).astype(low)
+        return carried
+
+    lax.fori_loop(0, shard // 16, last_add, 0)
+
+    def in_deep(step):
+        to_z = lax.rem(z + step, depth)
+        block = rows_of(in_final, in_own, shard)
+        return remote(block, block, in_s.at[step - 1], in_r.at[step - 1], (dp, to_z * 2 + y))
+
+    def in_gather(start, size, slot, peer):
+        block = rows_of(in_final, start, size)
+        return remote(block, block, in_s.at[slot], in_r.at[slot], peer)
+
+    in_two = (at.core * 2 + at.two_bit) * 2 * depth * shard
+    in_one = at.core * 4 * depth * shard
+    in_up = [
+        in_gather(in_three, depth * shard, depth - 1, at.three_peer),
+        in_gather(in_two, 2 * depth * shard, depth, at.two_peer),
+        in_gather(in_one, 4 * depth * shard, depth + 1, at.core_peer),
+    ]
+    for step in range(1, depth):
+        in_deep(step).start()
+    each_seq(lambda source: extra_over_seq(source, source).wait_recv())
+    summed = extra_seq[0].astype(jnp.float32)
+    for k in range(1, count):
+        summed = summed + extra_seq[k].astype(jnp.float32)
+    extra_sum[...] = summed
+    each_dp(lambda to: extra_over_dp(to, dp).start())
+    extra_dp[dp] = summed
+    rest_sum.send(4)
+    near_sum.turn()
+
+    def wait_back(step, carried):
+        source = lax.rem(me + step, count)
+        exchange(send_back.at[source], recv_back.at[source], back_s.at[source], back_r.at[source], source).wait_recv()
+        return carried
+
+    lax.fori_loop(1, count, wait_back, 0)
+
+    def wait_first(step, carried):
+        source = lax.rem(z + step, depth)
+        exchange(send_first.at[source], recv_first.at[source], fback_s.at[source], fback_r.at[source], source * 2 + y).wait_recv()
+        return carried
+
+    lax.fori_loop(1, depth, wait_first, 0)
+    first_sum = recv_first[0].astype(jnp.float32)
+    for source in range(1, depth):
+        first_sum = first_sum + recv_first[source].astype(jnp.float32)
+    for pair in range(pairs):
+        even = recv_back[2 * pair, :rows].astype(jnp.float32)
+        odd = recv_back[2 * pair + 1, :rows].astype(jnp.float32)
+        if pair == 0:
+            even = even + first_sum
+        columns = wide * pair
+        joined_ref[:, pl.ds(columns, wide)] = join_heads(even, swap_halves(odd)).astype(low)
+        joined_ref[:, pl.ds(width + columns, wide)] = join_heads(swap_halves(even), odd).astype(low)
+        even = recv_back[2 * pair, rows:].astype(jnp.float32)
+        odd = recv_back[2 * pair + 1, rows:].astype(jnp.float32)
+        columns = pl.ds(2 * width + columns, wide)
+        joined_ref[pl.ds(0, half), columns] = join_heads(even, swap_halves(odd)).astype(low)
+        joined_ref[pl.ds(half, half), columns] = join_heads(swap_halves(even), odd).astype(low)
+    grad = dot_nt(joined_ref[...], w_qkv_ref[...])
+    unit = unit_one_ref[...]
+    vec_in_mine[...] = jnp.zeros_like(vec_in_mine)
+    vec_in_mine[pl.ds(0, 1), :] = jnp.sum(grad * unit, axis=0, keepdims=True)
+    vec_in_mine[pl.ds(1, 1), :] = jnp.sum(grad, axis=0, keepdims=True)
+    vec_in_mine[pl.ds(2, 1), :] = jnp.sum(joined_ref[:, pl.ds(2 * width, width)].astype(jnp.float32), axis=0, keepdims=True)
+    in_vec.start_seq()
+    tokens_grad_ref[0] = middle_ref[...] + normalise_back(grad, unit, rstd_one_ref[...], gain_one_ref[...])
+
+    for step in range(1, depth):
+        in_deep(step).wait_recv()
+    in_up[0].start()
+    near_sum.gather(3)
+    rest_sum.turn()
+    each_dp(lambda source: extra_over_dp(source, source).wait_recv())
+    summed = extra_dp[0]
+    for k in range(1, dp_count):
+        summed = summed + extra_dp[k]
+    extra_all[pl.ds(pl.multiple_of(me * piece, 16), piece), :] = summed.astype(low)
+    each_seq(lambda to: extra_gather(to, me).start())
+    in_vec.start_dp()
+    in_up[0].wait_recv()
+    in_up[1].start()
+    near_sum.gather(2)
+    rest_sum.gather(3)
+    vec_mid_ref[...] = mid_vec.finish()
+    near_sum.gather(1)
+    rest_sum.gather(2)
+    in_up[1].wait_recv()
+    in_up[2].start()
+    near_sum.gather(0)
+    rest_sum.gather(1)
+    near_sum.finish()
+    half_hidden = hidden_width // 2
+    stores = [
+        pltpu.make_async_copy(near_final.at[pl.ds(0, half_hidden)], w_down_out.at[pl.ds(0, half_hidden)], store_sem.at[0]),
+        pltpu.make_async_copy(near_final.at[pl.ds(near_rows, half_hidden)], w_up_out.at[pl.ds(0, half_hidden)], store_sem.at[1]),
+    ]
+    for store in stores:
+        store.start()
+    each_seq(lambda source: extra_gather(source, source).wait_recv())
+    in_up[2].wait_recv()
+    late = [
+        pltpu.make_async_copy(in_final, w_qkv_out, store_sem.at[2]),
+        pltpu.make_async_copy(extra_all, first_out, store_sem.at[3]),
+    ]
+    for store in late:
+        store.start()
+    stores += late
+    rest_sum.gather(0)
+    vec_in_ref[...] = in_vec.finish()
+    rest_sum.finish()
+    late = [
+        pltpu.make_async_copy(rest_final.at[pl.ds(0, half_hidden)], w_down_out.at[pl.ds(half_hidden, half_hidden)], store_sem.at[4]),
+        pltpu.make_async_copy(rest_final.at[pl.ds(rest_rows, half_hidden)], w_up_out.at[pl.ds(half_hidden, half_hidden)], store_sem.at[5]),
+        pltpu.make_async_copy(rest_final.at[pl.ds(quarter, width // 2)], w_out_out.at[pl.ds(0, width // 2)], store_sem.at[6]),
+        pltpu.make_async_copy(rest_final.at[pl.ds(rest_rows + quarter, width // 2)], w_out_out.at[pl.ds(width // 2, width // 2)], store_sem.at[7]),
+    ]
+    for store in late:
+        store.start()
+    stores += late
+
+    pl.when(has_up(z))(lambda: pass_up(me).wait_send())
+    pl.when(z > 0)(lambda: pass_down(me).wait_send())
+    pass_y(me).wait_send()
+    for distance in range(1, depth):
+
+        def below(distance=distance):
+            pl.when(has_up(z))(lambda: pass_up(me - 2 * distance).wait_send())
+            pass_y(me - 2 * distance).wait_send()
+
+        def above(distance=distance):
+            pl.when(z > 0)(lambda: pass_down(me + 2 * distance).wait_send())
+            pass_y(me + 2 * distance).wait_send()
+
+        pl.when(z - distance >= 0)(below)
+        pl.when(z + distance < depth)(above)
+
+    def drain(step, carried):
+        to = lax.rem(me + step, count)
+        exchange(send_mix.at[to], recv_mix.at[me], mix_s.at[to], mix_r.at[me], to).wait_send()
+        exchange(send_gmix.at[to], recv_gmix.at[me], gmix_s.at[to], gmix_r.at[me], to).wait_send()
+        exchange(send_back.at[to], recv_back.at[me], back_s.at[to], back_r.at[me], to).wait_send()
+        extra_over_seq(to, me).wait_send()
+        extra_gather(to, me).wait_send()
+        return carried
+
+    lax.fori_loop(1, count, drain, 0)
+
+    def drain_first(step, carried):
+        to = lax.rem(z + step, depth) * 2 + y
+        exchange(send_first.at[to], recv_first.at[z], fback_s.at[to], fback_r.at[z], to).wait_send()
+        return carried
+
+    def drain_first_y(step, carried):
+        to = step * 2 + 1 - y
+        exchange(send_first.at[to], y_first.at[to], fback_y.at[to], fback_yr.at[to], z * 2 + 1 - y).wait_send()
+        return carried
+
+    lax.fori_loop(1, depth, drain_first, 0)
+    lax.fori_loop(0, depth, drain_first_y, 0)
+    each_dp(lambda to: extra_over_dp(to, dp).wait_send())
+    in_core_copy.wait_send()
+    in_x_copy.wait_send()
+    for step in range(1, depth):
+        in_deep(step).wait_send()
+    for copy in in_up:
+        copy.wait_send()
+    near_sum.drain()
+    rest_sum.drain()
+    mid_vec.drain()
+    in_vec.drain()
+    for store in stores:
+        store.wait()
+
+
+def widen_kernel(
+    w_down_in, w_up_in, w_out_in, w_qkv_in, first_in, w_down_out, w_up_out, w_out_out, w_qkv_out,
+    down_low, up_low, out_low, qkv_low, first_low, down_wide, up_wide, out_wide, qkv_wide, load_sem, store_sem,
+):
+    width = out_low.shape[0]
+    blocks = down_low.shape[0] // width
+    loads = []
+    for k, (source, target) in enumerate(
+        ((w_qkv_in, qkv_low), (first_in, first_low), (w_out_in, out_low), (w_down_in, down_low), (w_up_in, up_low))
+    ):
+        loads.append(pltpu.make_async_copy(source, target, load_sem.at[k]))
+        loads[-1].start()
+    stores = []
+
+    def store(source, target):
+        stores.append(pltpu.make_async_copy(source, target, store_sem.at[len(stores)]))
+        stores[-1].start()
+
+    def convert(source, target, at, columns):
+        def step(k, carried):
+            here = pl.ds(pl.multiple_of(at + k * 64, 64), 64)
+            there = pl.ds(pl.multiple_of(k * 64, 64), 64)
+            if columns is None:
+                target[here, :] = source[here, :].astype(jnp.float32)
+            else:
+                target[there, pl.ds(columns, width)] = source[here, :].astype(jnp.float32)
+            return carried
+
+        lax.fori_loop(0, width // 64, step, 0)
+
+    loads[0].wait()
+    loads[1].wait()
+    piece = HD // 4
+    wide = 2 * HD
+    for part in range(3):
+        for pair in range(width // wide):
+            found = []
+            for head in (2 * pair, 2 * pair + 1):
+                z, y = head // 2, head % 2
+                for owner in range(4):
+                    core, x = owner // 2, owner % 2
+                    two, three = (x, y) if core == 0 else (y, x)
+                    depth = width // wide
+                    start = ((((core * 2 + two) * 2 + three) * depth + z) * 3 + part) * piece
+                    block = qkv_low[start : start + piece].astype(jnp.float32)
+                    if head == 0 and part < 2:
+                        at = part * HD + owner * piece
+                        block = block + first_low[at : at + piece].astype(jnp.float32)
+                    found.append(block)
+            columns = part * width + pair * wide
+            qkv_wide[:, columns : columns + wide] = jnp.concatenate(found, axis=0).T
+    store(qkv_wide, w_qkv_out)
+    loads[2].wait()
+    convert(out_low, out_wide, 0, None)
+    store(out_wide, w_out_out)
+    loads[3].wait()
+    for block in range(blocks):
+        convert(down_low, down_wide, block * width, None)
+        here = pl.ds(block * width, width)
+        store(down_wide.at[here], w_down_out.at[here])
+    loads[4].wait()
+    for block in range(blocks):
+        convert(up_low, up_wide, block * width, block * width)
+        here = pl.ds(block * width, width)
+        store(up_wide.at[:, here], w_up_out.at[:, here])
+    for one in stores:
+        one.wait()
+
+
+def exchange_heads(
+    tokens, segment_ids, gain_one, bias_one, w_qkv, b_val, w_out, b_out,
+    gain_two, bias_two, w_up, b_up, w_down, b_down, cotangent,
+):
+    count, dp_count = lax.axis_size("seq"), lax.axis_size("dp")
+    rows, width = tokens.shape[1], tokens.shape[2]
+    hidden = w_up.shape[1]
+    half = rows // 2
+    tiles = count * (count + 1) // 2
+    wide = 2 * HD
+    f32 = jnp.float32
+    packed = rows + half
+    near, rest = hidden, hidden + width
+    depth = count // 2
+
+    def vmem(*shape, dtype=low):
+        return pltpu.VMEM(shape, dtype)
+
+    def sems(*shape):
+        return pltpu.SemaphoreType.DMA(shape)
+
+    scratch = [
+        vmem(width, width), vmem(width, hidden), vmem(hidden, width), sems(3), sems(8),
+        vmem(count, rows, width), vmem(width, 2 * wide), vmem(width, wide), vmem(1, wide, dtype=f32),
+        vmem(count, rows, wide), vmem(count, rows, wide), vmem(count, rows, wide),
+        vmem(count, HD, rows), vmem(count, HD, rows), vmem(count, rows, wide), vmem(count, rows, wide),
+        vmem(tiles, rows, rows), vmem(tiles, rows, rows), vmem(tiles, rows, rows, dtype=f32),
+        vmem(count, 1, rows, dtype=f32), vmem(count, rows, wide, dtype=f32), vmem(rows, wide, dtype=f32), vmem(count, rows, wide, dtype=f32),
+        vmem(count, half, wide), vmem(count, half, wide), vmem(count, half, wide), vmem(count, half, wide), vmem(rows, wide), vmem(HD, rows),
+        vmem(rows, wide, dtype=f32), vmem(rows, wide, dtype=f32), vmem(count, wide, rows, dtype=f32), vmem(count, HD, rows, dtype=f32), vmem(count, 1, rows, dtype=f32),
+        vmem(count, packed, wide), vmem(count, packed, wide), vmem(count, rows, wide), vmem(count, rows, wide), vmem(depth, rows, wide),
+        vmem(rows, rows), vmem(rows, rows),
+        vmem(rows, width, dtype=f32), vmem(rows, 1, dtype=f32), vmem(rows, width, dtype=f32), vmem(rows, 1, dtype=f32),
+        vmem(rows, width), vmem(rows, width), vmem(rows, width, dtype=f32), vmem(rows, width, dtype=f32), vmem(rows, width, dtype=f32), vmem(rows, 3 * width),
+    ]
+    for total in (near, rest):
+        scratch += [vmem(total, width), vmem(total, width)]
+        scratch += [vmem(total >> stage, width) for stage in range(1, 6)]
+    scratch += [
+        vmem(wide, width, dtype=f32), vmem(wide, width, dtype=f32), vmem(HD, width, dtype=f32),
+        vmem(3 * HD, width), vmem(3 * HD // 2, width), vmem(3 * HD // 4, width), vmem(3 * width, width),
+        vmem(wide, width), vmem(count, wide // count, width), vmem(wide // count, width, dtype=f32), vmem(dp_count, wide // count, width, dtype=f32), vmem(wide, width),
+    ]
+    for _ in range(2):
+        scratch += [vmem(8, width, dtype=f32), vmem(count, 8, width, dtype=f32), vmem(8, width, dtype=f32), vmem(dp_count, 8, width, dtype=f32)]
+    scratch += [sems(count)] * 18
+    scratch += [sems(10)] * 4 + [sems(depth + 2), sems(depth + 2), sems(2), sems(2), sems(4, count), sems(4, count), sems(dp_count), sems(dp_count)]
+    in_vmem = pl.BlockSpec(memory_space=pltpu.VMEM)
+    anywhere = pl.BlockSpec(memory_space=pl.ANY)
+    specs = [in_vmem] * 15
+    for at in (6, 10, 12):
+        specs[at] = anywhere
+    shape = jax.ShapeDtypeStruct
+    results = pl.pallas_call(
+        layer_kernel,
+        out_shape=[
+            shape((1, rows, width), low), shape((1, rows, width), f32), shape((8, width), f32), shape((8, width), f32),
+            shape((hidden, width), low), shape((hidden, width), low), shape((width, width), low), shape((3 * width, width), low), shape((wide, width), low),
+        ],
+        in_specs=specs,
+        out_specs=[in_vmem] * 4 + [anywhere] * 5,
+        scratch_shapes=scratch,
+        compiler_params=pltpu.CompilerParams(
+            collective_id=0, has_side_effects=True, vmem_limit_bytes=vmem_bytes
+        ),
+    )(
+        tokens, segment_ids, gain_one[None], bias_one[None], w_qkv, b_val[None], w_out, b_out[None],
+        gain_two[None], bias_two[None], w_up, b_up[None], w_down, b_down[None], cotangent,
+    )
+    output, tokens_grad, vec_mid, vec_in = results[:4]
+    w_down_grad, w_up_grad, w_out_grad, w_qkv_grad = pl.pallas_call(
+        widen_kernel,
+        out_shape=[shape((hidden, width), f32), shape((width, hidden), f32), shape((width, width), f32), shape((width, 3 * width), f32)],
+        in_specs=[anywhere] * 5,
+        out_specs=[anywhere] * 4,
+        scratch_shapes=[
+            vmem(hidden, width), vmem(hidden, width), vmem(width, width), vmem(3 * width, width), vmem(wide, width),
+            vmem(hidden, width, dtype=f32), vmem(width, hidden, dtype=f32), vmem(width, width, dtype=f32), vmem(width, 3 * width, dtype=f32),
+            sems(5), sems(16),
+        ],
+        compiler_params=pltpu.CompilerParams(vmem_limit_bytes=vmem_bytes),
+    )(*results[4:])
+    chunks = hidden // width
+    return (
+        output,
+        tokens_grad,
+        vec_in[0],
+        vec_in[1],
+        w_qkv_grad,
+        vec_in[2],
+        w_out_grad,
+        vec_mid[chunks + 3],
+        vec_mid[chunks + 1],
+        vec_mid[chunks + 2],
+        w_up_grad,
+        vec_mid[:chunks].reshape(hidden),
+        w_down_grad,
+        vec_mid[chunks],
+    )
+
+
+def picks_heads(mesh, length, width, hidden):
+    dp_count, count = mesh.shape["dp"], mesh.shape["seq"]
+    power = length & (length - 1) == 0
+    return dp_count == 4 and count == 8 and width == count * HD and hidden == 4 * width and power
+
+
 def solution(mesh):
     placed = (
         P("dp", "seq", None),
@@ -390,8 +1430,15 @@
         P(),
         P("dp", "seq", None),
     )
+
+    def layer(tokens, *others):
+        width, hidden = tokens.shape[-1], others[9].shape[-1]
+        length = tokens.shape[1] * mesh.shape["seq"]
+        body = exchange_heads if picks_heads(mesh, length, width, hidden) else local
+        return body(tokens, *others)
+
     return jax.shard_map(
-        local,
+        layer,
         mesh=mesh,
         in_specs=placed,
         out_specs=(

time: 792 us -> 195 us (0.25)
  blocking collectives: 296 us -> 0 us
  waiting for transfers between devices: 282 us -> 0 us
  Pallas kernels: 0 us -> 189 us
  local copies, waits for them, and re-layouts: 95.8 us -> 4.33 us
  matrix products: 59.5 us -> 0 us
  other arithmetic: 20.3 us -> 0 us
  loops' own time: 18.3 us -> 0 us
  between operations: 14.4 us -> 0.68 us
    all_gather x3 -> x0, blocking collectives: 254 us -> none  [the longest x2 219 us: prefix(): everything = lax.all_gather(array.astype(jnp.bfloat16), axis)]
    pallas_call x0 -> x2, Pallas kernels: none -> 189 us  [the longest x1 182 us: exchange_heads(): pl.pallas_call(layer_kernel, out_shape=[shape((1, rows, width), low), sha...]
    psum x1 -> x0, waiting for transfers between devices: 188 us -> none  [local(): lax.psum((gain_one_grad, bias_one_grad, w_qkv_grad, b_val_grad, w_out_gra...]
    reduce_scatter x2 -> x0, waiting for transfers between devices: 93 us -> none  [the longest x1 70.9 us: local(): lax.psum_scatter(key_total.astype(jnp.bfloat16), 'seq', scatter_dimension...]
    dot_general x31 -> x0, matrix products: 59.5 us -> none  [the longest x1 6.12 us: local(): jnp.dot(normed_two_low, w_up, preferred_element_type=jnp.float32) + b_up]
    dynamic_update_slice x21 -> x0, local copies, waits for them, and re-layouts: 45.4 us -> none  [the longest x8 15.7 us: select_block(): lax.dynamic_update_slice_in_dim(zero_scores, scores, offset, 1)]
    psum x1 -> x0, blocking collectives: 41.7 us -> none  [local(): lax.psum((gain_one_grad, bias_one_grad, w_qkv_grad, b_val_grad, w_out_gra...]
    another operation x13 -> x0, loops' own time: 18.3 us -> none  [the longest x1 7.95 us: local(): running, unused = lax.scan(select_block, running, offsets)]
  transfers between devices with their start and end apart: 5 -> 0, of which waited for: 3 -> 0; matrix products, arithmetic and copies ran while one was open for 10% -> 0% of each run, Pallas kernels for 0% -> 0%
where the time goes in v2:
time: 195 us; the launch traced here: 194 us
  Pallas kernels  189 us (97%)
  local copies, waits for them, and re-layouts  4.33 us (2%)
    pallas_call x1, Pallas kernels, exchange_heads(): pl.pallas_call(layer_kernel, out_shape=[shape((1, rows, width), low), sha...  182 us
    pallas_call x1, Pallas kernels, exchange_heads(): pl.pallas_call(widen_kernel, out_shape=[shape((hidden, width), f32), shap...  6.82 us

profile of v2, /device:TPU:0, one launch (start us, length us, event | category | flops | bytes accessed | tf_op | source)
XLA Modules:
  0.0 193.8 jit_solution(1645650175559914118)
XLA Ops:
  0.7 182.0 %shard_map.254 = (bf16[1,256,512]{2,1,0:T(8,128)(2,1)}, f32[1,256,512]{2,1,0:T(8,128)}, f32[8,512]{1,0:T(8,128)}, f32[8,512]{1,0:T(8,128)}, bf16[2048,512]{1,0:T...) custom-call(bf16[1,256,512]{2,1,0:T(8,128)(2,1)} %tokens_ref.1, ...), custom_call_target="tpu_custom_call" | custom-call | tf_op jit(solution)/shard_map/pallas_call | solution.py:1361
  182.6 0.7 slice_bitcast_fusion
  183.4 1.5 fusion
  184.9 0.6 copy.29
  185.5 0.0 copy-start.1
  185.5 0.0 copy-start
  185.5 6.8 %shard_map.255 = (f32[2048,512]{1,0:T(8,128)}, f32[512,2048]{1,0:T(8,128)}, f32[512,512]{1,0:T(8,128)}, f32[512,1536]{1,0:T(8,128)}) custom-call(bf16[2048,512]{1,0:T(8,128)(2,1)} %get-tuple-element.30.w_down_in, bf16[2048,512]{1,0:T(8,128)(2,1)} %get-tuple-element.31.w_up_in, bf16[512,512]{1,0:T(8,128)(2,1)} %get-tuple-element.32.w_out_in, ...), custom_call_target="tpu_custom_call" | custom-call | tf_op jit(solution)/shard_map/pallas_call | solution.py:1378
  192.3 0.0 copy-done.1
  192.3 0.7 copy.32
  193.0 0.0 copy-done
  193.0 0.8 copy.33
Async XLA Ops:
  185.5 6.8 %copy-start.1 = (bf16[1,256,512]{2,1,0:T(8,128)(2,1)S(1)}, bf16[1,256,512]{2,1,0:T(8,128)(2,1)}, u32[]{:S(2)}) copy-start(bf16[1,256,512]{2,1,0:T(8,128)(2,1)} %get-tuple-element.64) | copy-start | bytes 786436
  185.5 7.5 %copy-start = (f32[1,256,512]{2,1,0:T(8,128)S(1)}, f32[1,256,512]{2,1,0:T(8,128)}, u32[]{:S(2)}) copy-start(f32[1,256,512]{2,1,0:T(8,128)} %get-tuple-element.65) | copy-start | bytes 1572868

commit v3 on v2

--- a/solution.py
+++ b/solution.py
@@ -434,15 +434,16 @@
     return ref.at[pl.ds(pl.multiple_of(at, 16), size)]
 
 
-def add_rows(into, at, source, source_at, size, piece=16):
+def add_rows(into, into_at, parts, size):
     def step(k, carried):
-        here = pl.ds(pl.multiple_of(at + k * piece, 16), piece)
-        there = pl.ds(pl.multiple_of(source_at + k * piece, 16), piece)
-        summed = into[here, :].astype(jnp.float32) + source[there, :].astype(jnp.float32)
-        into[here, :] = summed.astype(low)
+        summed = None
+        for ref, at in parts:
+            block = ref[pl.ds(pl.multiple_of(at + k * 16, 16), 16), :].astype(jnp.float32)
+            summed = block if summed is None else summed + block
+        into[pl.ds(pl.multiple_of(into_at + k * 16, 16), 16), :] = summed.astype(low)
         return carried
 
-    lax.fori_loop(0, size // piece, step, 0)
+    lax.fori_loop(0, size // 16, step, 0)
 
 
 class Places:
@@ -472,63 +473,78 @@
 
 
 class StagedSum:
-    def __init__(self, at, mine, final, got, send_sem, recv_sem):
+    def __init__(self, at, mine, final, got, sems):
         self.mine, self.final, self.got = mine, final, got
-        total = mine.shape[0]
         bits = (at.core, at.two_bit, at.three_bit, at.z_low, at.z_high)
-        peers = (at.core_peer, at.two_peer, at.three_peer, at.z_near, at.z_far)
-        start, size = 0, total
-        self.down, self.up, self.keeps = [], [], []
-        for stage, (bit, peer) in enumerate(zip(bits, peers)):
+        self.peers = (at.core_peer, at.two_peer, at.three_peer, at.z_near, at.z_far)
+        self.stages = len(bits)
+        self.down_s, self.down_r, self.up_s, self.up_r = sems
+        start, size = 0, final.shape[0]
+        self.keep, self.give, self.size = [], [], []
+        for bit in bits:
             size //= 2
-            keep, give = start + bit * size, start + (1 - bit) * size
-            self.keeps.append((start, keep, give, size))
-            self.down.append(
-                remote(rows_of(mine, give, size), got[stage], send_sem.at[stage], recv_sem.at[stage], peer)
-            )
-            self.up.append(
-                remote(
-                    rows_of(final, keep, size), rows_of(final, keep, size),
-                    send_sem.at[5 + stage], recv_sem.at[5 + stage], peer,
-                )
-            )
-            start = keep
+            self.keep.append(start + bit * size)
+            self.give.append(start + (1 - bit) * size)
+            self.size.append(size)
+            start = start + bit * size
+        self.give.append(start)
+        self.size.append(size)
+
+    def down(self, stage, block):
+        if stage == 0:
+            source, there, size = self.give[0], 0, self.size[0]
+        else:
+            there, size = self.give[block] - self.keep[stage], self.size[block]
+            source = self.give[stage] + there
+        return remote(
+            rows_of(self.mine, source, size), rows_of(self.got[stage], there, size),
+            self.down_s.at[stage, block], self.down_r.at[stage, block], self.peers[stage],
+        )
+
+    def up(self, stage, block):
+        here = rows_of(self.final, self.give[block], self.size[block])
+        return remote(here, here, self.up_s.at[stage, block], self.up_r.at[stage, block], self.peers[stage])
+
+    def blocks(self, stage):
+        return (1,) if stage == 0 else range(stage + 1, self.stages + 1)
 
     def send(self, stage):
         if stage > 0:
-            self.down[stage - 1].wait_recv()
-            begin, keep_before = self.keeps[stage - 1][1], self.keeps[stage]
-            _, keep, give, size = keep_before
-            add_rows(self.mine, give, self.got[stage - 1], give - begin, size)
-            self.down[stage].start()
-            add_rows(self.mine, keep, self.got[stage - 1], keep - begin, size)
-        else:
-            self.down[0].start()
+            self.collect(stage, self.mine)
+        for block in self.blocks(stage):
+            self.down(stage, block).start()
+
+    def collect(self, block, into):
+        parts = [(self.mine, self.give[block])]
+        for stage in range(block):
+            if stage > 0 or block == 1:
+                self.down(stage, block).wait_recv()
+            parts.append((self.got[stage], self.give[block] - self.keep[stage]))
+        add_rows(into, self.give[block], parts, self.size[block])
 
     def turn(self):
-        self.down[4].wait_recv()
-        _, keep, _, size = self.keeps[4]
-
-        def step(k, carried):
-            there = pl.ds(pl.multiple_of(k * 16, 16), 16)
-            here = pl.ds(pl.multiple_of(keep + k * 16, 16), 16)
-            summed = self.mine[here, :].astype(jnp.float32) + self.got[4][there, :].astype(jnp.float32)
-            self.final[here, :] = summed.astype(low)
-            return carried
-
-        lax.fori_loop(0, size // 16, step, 0)
-        self.up[4].start()
+        self.collect(self.stages, self.final)
+        self.spread(self.stages)
+
+    def spread(self, block):
+        for stage in reversed(range(block)):
+            self.up(stage, block).start()
+
+    def arrive(self, stage):
+        for block in range(stage + 1, self.stages + 1):
+            self.up(stage, block).wait_recv()
 
     def gather(self, stage):
-        self.up[stage + 1].wait_recv()
-        self.up[stage].start()
-
-    def finish(self):
-        self.up[0].wait_recv()
-
-    def drain(self, first=0):
-        for copy in self.down[first:] + self.up:
-            copy.wait_send()
+        self.arrive(stage)
+        self.spread(stage)
+
+    def drain(self, summed=True):
+        for stage in range(self.stages):
+            if summed:
+                for block in self.blocks(stage):
+                    self.down(stage, block).wait_send()
+            for block in range(stage + 1, self.stages + 1):
+                self.up(stage, block).wait_send()
 
 
 class VectorSum:
@@ -582,6 +598,24 @@
         at = self.at
         self.each(at.count, at.me, lambda to: self.over_seq(to, at.me).wait_send())
         self.each(at.dp_count, at.dp, lambda to: self.over_dp(to, at.dp).wait_send())
+
+
+before_backward = ("N2", "R1",)
+between_steps = (
+    ("N3",),
+    ("R2", "O1",),
+    ("N4",),
+    ("R3", "O2",),
+    ("Nt",),
+    ("R4", "V1", "O3",),
+    ("Ne",),
+    ("Rt", "O4",),
+)
+after_backward = (
+    "I0", "E0", "F", "Nd", "I1", "Re", "Ot", "It", "E1", "Nc", "Rd", "T",
+    "Oe", "Ie", "Nb", "Rc", "Od", "E2", "Id", "W1", "Rb", "Oc", "Ic", "Ob",
+    "Ib", "Vf", "Nf", "Rf", "Of", "If", "Ef", "Wf",
+)
 
 
 def layer_kernel(
@@ -613,23 +647,24 @@
 ):
     (
         w_out_ref, w_up_ref, w_down_ref, load_sem, store_sem,
-        normed_all, w_head, w_value, b_value, key_query, first, vals, query_t, first_t, wide_q, wide_first,
-        probs, gates, logit, carry, row_top, row_acc, mixed_keep,
+        normed_all, w_head, w_value, b_value, queries, keys, keys_zero, vals, queries_t,
+        probs, gates, logit, carry, row_wide, row_acc,
         send_mix, recv_mix, send_gmix, recv_gmix, grad_rows, grad_rows_t,
-        dq_acc, dq0_acc, dkv_acc, dk0_acc, back_carry,
+        back_carry,
         send_back, recv_back, send_first, y_first, recv_first,
         lower, upper,
-        unit_one_ref, rstd_one_ref, unit_two_ref, rstd_two_ref,
+        unit_two_ref, rstd_two_ref,
         mixed_ref, normed_two_ref, middle_ref, out_acc, gn_acc, joined_ref,
         near_mine, near_final, near_core, near_two, near_three, near_four, near_five,
         rest_mine, rest_final, rest_core, rest_two, rest_three, rest_four, rest_five,
-        wkv_acc, wqq_acc, wk0_acc, in_mine, in_core, in_x, in_final,
+        out_mine, out_final, out_core, out_two, out_three, out_four, out_five,
+        wkv_acc, wqq_acc, in_mine, in_core, in_x, in_final,
         extra_mine, extra_seq, extra_sum, extra_dp, extra_all,
         vec_mid_mine, vec_mid_seq, vec_mid_sum, vec_mid_dp,
         vec_in_mine, vec_in_seq, vec_in_sum, vec_in_dp,
         norm_y, norm_up, norm_down, norm_r, mix_s, mix_r, gmix_s, gmix_r,
         back_s, back_r, fback_y, fback_yr, fback_s, fback_r, extra_s, extra_r, gather_s, gather_r,
-        near_s, near_r, rest_s, rest_r, in_s, in_r, part_s, part_r, vec_s, vec_r, edp_s, edp_r,
+        *sums_sems, in_s, in_r, part_s, part_r, vec_s, vec_r, edp_s, edp_r,
     ) = scratch
     at = Places()
     dp_count, count, dp, me = at.dp_count, at.count, at.dp, at.me
@@ -667,9 +702,7 @@
         return remote(src, dst, send_sem, recv_sem, (dp, target))
 
     tokens = tokens_ref[0].astype(jnp.float32)
-    unit, rstd = normalise(tokens)
-    unit_one_ref[...] = unit
-    rstd_one_ref[...] = rstd
+    unit, _ = normalise(tokens)
     normed_all[me] = (unit * gain_one_ref[...] + bias_one_ref[...]).astype(low)
     pl.semaphore_wait(barrier, count + dp_count - 2)
 
@@ -711,15 +744,16 @@
     odd_head = lax.rem(me, 2) == 1
     pair_at_lane = pl.multiple_of((me // 2) * wide, wide)
 
-    def head_columns(part, right):
+    def head_columns(part):
         columns = w_qkv_ref[:, pl.ds(part * width + pair_at_lane, wide)].astype(jnp.float32)
-        swapped = swap_halves(columns)
-        return jnp.where(odd_head, columns, swapped) if right else jnp.where(odd_head, swapped, columns)
-
-    w_head[:, :wide] = join_heads(head_columns(1, False), head_columns(0, True) * score_scale).astype(low)
-    zero_query = swap_halves(w_qkv_ref[:, :wide].astype(jnp.float32)) * score_scale
-    w_head[:, wide:] = join_heads(w_qkv_ref[:, width : width + wide].astype(jnp.float32), zero_query).astype(low)
-    w_value[...] = head_columns(2, False).astype(low)
+        return jnp.where(odd_head, swap_halves(columns), columns)
+
+    def zero_columns(part):
+        return swap_halves(w_qkv_ref[:, part * width : part * width + wide].astype(jnp.float32))
+
+    w_head[:, :wide] = (join_heads(head_columns(0), zero_columns(0)) * score_scale).astype(low)
+    w_head[:, wide:] = join_heads(head_columns(1), zero_columns(1)).astype(low)
+    w_value[...] = head_columns(2).astype(low)
     bias = b_val_ref[:, pl.ds(pair_at_lane, wide)]
     b_value[...] = jnp.where(odd_head, swap_halves(bias), bias)
 
@@ -734,73 +768,98 @@
     lane = lax.broadcasted_iota(jnp.int32, (rows, wide), 1)
 
     def masks(i, j):
-        query_pos = lax.broadcasted_iota(jnp.int32, (rows, 1), 0).astype(jnp.float32) + (i * rows).astype(jnp.float32)
-        key_pos = lax.broadcasted_iota(jnp.int32, square, 1).astype(jnp.float32) + (j * rows).astype(jnp.float32)
-        begin = jnp.where(
-            query_pos >= start_two, start_two, jnp.where(query_pos >= start_one, start_one, 0.0)
-        )
+        query_pos = lax.broadcasted_iota(jnp.int32, (rows, 1), 0).astype(jnp.float32) + ((i - j) * rows).astype(jnp.float32)
+        key_start = (j * rows).astype(jnp.float32)
+        begin_one, begin_two = start_one - key_start, start_two - key_start
+        begin = jnp.where(query_pos >= begin_two, begin_two, jnp.where(query_pos >= begin_one, begin_one, -key_start))
+        key_pos = col_at.astype(jnp.float32)
         inside = key_pos >= begin
         return inside & (key_pos <= query_pos), inside & (key_pos < query_pos)
 
-    def needs_mask(i, j):
-        return (j == 0) | (j == i) | (i == count - 1)
-
     def pair_at(i, j):
         return i * (i + 1) // 2 + j
 
     carry[...] = jnp.zeros_like(carry)
-    row_top[...] = jnp.full_like(row_top, neg_large)
+    row_wide[...] = jnp.full_like(row_wide, neg_large)
 
     def project(block):
         normed = normed_all[block]
-        both = dot_nn(normed, w_head[...]).astype(low)
-        key_query[block] = both[:, :wide]
-        query = swap_halves(both[:, :wide].astype(jnp.float32))
-        wide_q[block] = jnp.where(lane < HD, query, 0.0).astype(low)
-        query_t[block] = query.T[:HD].astype(low)
-        first[block] = both[:, wide:]
-        query = swap_halves(both[:, wide:].astype(jnp.float32))
-        wide_first[block] = jnp.where(lane < HD, query, 0.0).astype(low)
-        first_t[block] = query.T[:HD].astype(low)
+        both = dot_nn(normed, w_head[...])
+        query = both[:, :wide]
+        queries[block] = query.astype(low)
+        queries_t[block] = query.T.astype(low)
+        key = both[:, wide:]
+        keys[block] = jnp.where(lane < HD, key, 0.0).astype(low)
+        keys_zero[block] = jnp.where(lane < HD, 0.0, key).astype(low)
         value = dot_nn(normed, w_value[...]) + b_value[...]
         vals[block] = jnp.where(lane < HD, value, jnp.where(lane < HD + 2, 1.0, 0.0)).astype(low)
 
-    def forward_tile(i, j, masked):
-        start_scores = dot_nt(wide_first[i], first[j])
-        soft = jnp.maximum(start_scores, 0.0) + jnp.log(1.0 + jnp.exp(-jnp.abs(start_scores)))
-        gate = jnp.exp(start_scores - soft)
-        if masked:
-            attend, select = masks(i, j)
-            soft = jnp.where(select, soft, 0.0)
-            gate = jnp.where(select, gate, 0.0)
-        gates[pair_at(i, j)] = gate.astype(low)
-        soft_low = soft.astype(low)
-        forgot = dot_nn(lower[...], soft_low) + carry[j]
-        carry[j] = forgot[rows - 1 :] - coeff * soft_low[rows - 1 :].astype(jnp.float32)
-        scores = dot_nt(wide_q[i], key_query[j]) + forgot
-        if masked:
-            scores = jnp.where(attend, scores, neg_large)
-        logit[pair_at(i, j)] = scores
-        top = row_top[i]
-        for start in range(0, rows, wide):
-            top = jnp.maximum(top, scores[:, start : start + wide])
-        row_top[i] = top
+    def kept_at(i):
+        return pair_at(i, 0) - i // (count - 1) * (count - 2)
+
+    def grads_at(j):
+        return pair_at(count - 1, j)
+
+    def forward_group(group, masked):
+        spots = [pair_at(i, j) for i, j in group]
+        zero_scores = [dot_nt(queries[i], keys_zero[j]) for i, j in group]
+        scores = [dot_nt(queries[i], keys[j]) for i, j in group]
+        softs, gate_rows, attends = [], [], {}
+        for k, (i, j) in enumerate(group):
+            score = zero_scores[k]
+            soft = jnp.maximum(score, 0.0) + jnp.log(1.0 + jnp.exp(-jnp.abs(score)))
+            gate = jnp.exp(score - soft)
+            if k in masked:
+                attends[k], select = masks(i, j)
+                soft = jnp.where(select, soft, 0.0)
+                gate = jnp.where(select, gate, 0.0)
+            softs.append(soft.astype(low))
+            gate_rows.append(gate)
+        falls = [dot_nn(lower[...], soft) for soft in softs]
+        for k, spot in enumerate(spots):
+            gates[spot] = gate_rows[k].astype(low)
+        for k, (i, j) in enumerate(group):
+            forgot = falls[k] + carry[j]
+            carry[j] = forgot[rows - 1 :] - coeff * softs[k][rows - 1 :].astype(jnp.float32)
+            scores[k] = scores[k] + forgot
+            if k in masked:
+                scores[k] = jnp.where(attends[k], scores[k], neg_large)
+        for k, spot in enumerate(spots):
+            logit[spot] = scores[k]
+        for k, (i, _) in enumerate(group):
+            top = row_wide[i]
+            for start in range(0, rows, wide):
+                top = jnp.maximum(top, scores[k][:, start : start + wide])
+            row_wide[i] = top
+
+    def in_groups(total, act):
+        def four(group, carried):
+            act(group * 4, 4)
+            return carried
+
+        lax.fori_loop(0, total // 4, four, 0)
+        for left in (1, 2, 3):
+            pl.when(lax.rem(total, 4) == left)(lambda left=left: act(total - left, left))
 
     def weigh_row(i):
-        top = jnp.max(row_top[i], axis=1, keepdims=True)
+        top = jnp.max(row_wide[i], axis=1, keepdims=True)
         row_acc[...] = jnp.zeros_like(row_acc)
 
-        def weigh(j, inner):
-            prob = jnp.exp(logit[pair_at(i, j)] - top).astype(low)
-            probs[pair_at(i, j)] = prob
-            row_acc[...] += dot_nn(prob, vals[j])
-            return inner
-
-        lax.fori_loop(0, i + 1, weigh, 0)
+        def weigh(start, size):
+            found = [jnp.exp(logit[pair_at(i, start + k)] - top).astype(low) for k in range(size)]
+            added = None
+            for k, prob in enumerate(found):
+                product = dot_nn(prob, vals[start + k])
+                added = product if added is None else added + product
+            for k, prob in enumerate(found):
+                probs[pair_at(i, start + k)] = prob
+            row_acc[...] += added
+
+        in_groups(i + 1, weigh)
         mixed = row_acc[...]
         inverse = 1.0 / mixed[:, HD : HD + 1]
         mixed = mixed * inverse
-        mixed_keep[i] = jnp.where(lane < HD, mixed, inverse)
+        logit[kept_at(i), :, :wide] = jnp.where(lane < HD, mixed, inverse)
         send_mix[i] = fold_rows(mixed).astype(low)
 
         @pl.when(i != me)
@@ -824,14 +883,25 @@
 
         project(block)
 
-        def tiles(k, inner):
-            i = upwards * step + (1 - upwards) * (block + k)
-            j = upwards * k + (1 - upwards) * block
-            pl.when(needs_mask(i, j))(functools.partial(forward_tile, i, j, True))
-            pl.when(jnp.logical_not(needs_mask(i, j)))(functools.partial(forward_tile, i, j, False))
-            return inner
-
-        lax.fori_loop(0, step + 1, tiles, 0)
+        def group(start, size, all_masked=False):
+            members = []
+            for k in range(size):
+                i = upwards * step + (1 - upwards) * (block + start + k)
+                j = upwards * (start + k) + (1 - upwards) * block
+                members.append((i, j))
+            forward_group(members, range(size) if all_masked else (0, size - 1))
+
+        last = step == count - 1
+        pl.when(jnp.logical_not(last))(lambda: in_groups(step + 1, group))
+
+        @pl.when(last)
+        def _():
+            def four(start, carried):
+                group(start * 4, 4, True)
+                return carried
+
+            lax.fori_loop(0, count // 4, four, 0)
+
         pl.when(upwards == 1)(functools.partial(weigh_row, block))
         return carried
 
@@ -867,13 +937,15 @@
     normed_two_ref[...] = (unit * gain_two_ref[...] + bias_two_ref[...]).astype(low)
     out_acc[...] = jnp.zeros_like(out_acc)
     gn_acc[...] = jnp.zeros_like(gn_acc)
-    near_sum = StagedSum(at, near_mine, near_final, [near_core, near_two, near_three, near_four, near_five], near_s, near_r)
-    rest_sum = StagedSum(at, rest_mine, rest_final, [rest_core, rest_two, rest_three, rest_four, rest_five], rest_s, rest_r)
+    near_sum = StagedSum(at, near_mine, near_final, (near_core, near_two, near_three, near_four, near_five), sums_sems[:4])
+    rest_sum = StagedSum(at, rest_mine, rest_final, (rest_core, rest_two, rest_three, rest_four, rest_five), sums_sems[4:8])
+    out_sum = StagedSum(at, out_mine, out_final, (out_core, out_two, out_three, out_four, out_five), sums_sems[8:12])
+    in_sum = StagedSum(at, None, in_final, None, (None, None, in_s, in_r))
     mid_vec = VectorSum(at, vec_mid_mine, vec_mid_seq, vec_mid_sum, vec_mid_dp, vec_s, vec_r, 0)
     in_vec = VectorSum(at, vec_in_mine, vec_in_seq, vec_in_sum, vec_in_dp, vec_s, vec_r, 2)
     chunk = width
     chunks = hidden_width // chunk
-    near_rows, rest_rows = near_mine.shape[0] // 2, rest_mine.shape[0] // 2
+    half_hidden = hidden_width // 2
 
     def dense(sums, base, c, carried):
         start = pl.multiple_of((base + c) * chunk, chunk)
@@ -895,6 +967,7 @@
     lax.fori_loop(0, chunks // 2, functools.partial(dense, near_mine, 0), 0)
     near_sum.send(0)
     lax.fori_loop(0, chunks // 2, functools.partial(dense, rest_mine, chunks // 2), 0)
+    rest_sum.send(0)
     near_sum.send(1)
     cot = cot_ref[0].astype(jnp.float32)
     grad = gn_acc[...]
@@ -916,36 +989,79 @@
 
     lax.fori_loop(1, count, send_grads, 0)
     recv_gmix[me] = send_gmix[me]
-    w_out_grad = dot_tn(mixed_ref[...], branch).astype(low)
-    quarter = (chunks // 2) * chunk
-    rest_mine[pl.ds(quarter, width // 2), :] = w_out_grad[: width // 2]
-    rest_mine[pl.ds(rest_rows + quarter, width // 2), :] = w_out_grad[width // 2 :]
-    rest_sum.send(0)
+    out_mine[...] = dot_tn(mixed_ref[...], branch).astype(low)
+    out_sum.send(0)
     vec_mid_mine[pl.ds(chunks, 1), :] = jnp.sum(cot, axis=0, keepdims=True)
     vec_mid_mine[pl.ds(chunks + 1, 1), :] = jnp.sum(grad * unit, axis=0, keepdims=True)
     vec_mid_mine[pl.ds(chunks + 2, 1), :] = jnp.sum(grad, axis=0, keepdims=True)
     vec_mid_mine[pl.ds(chunks + 3, 1), :] = jnp.sum(branch.astype(jnp.float32), axis=0, keepdims=True)
     mid_vec.start_seq()
-    rest_sum.send(1)
-
-    dkv_acc[...] = jnp.zeros_like(dkv_acc)
-    dk0_acc[...] = jnp.zeros_like(dk0_acc)
+
+    def steps_of(sums):
+        found = {str(stage): functools.partial(sums.send, stage) for stage in range(1, 5)}
+        found["t"] = sums.turn
+        found |= {"abcde"[stage]: functools.partial(sums.gather, stage) for stage in range(1, 5)}
+        found["f"] = functools.partial(sums.arrive, 0)
+        return found
+
+    acts = {}
+    for name, sums in (("N", near_sum), ("R", rest_sum), ("O", out_sum), ("I", in_sum)):
+        acts |= {name + step: act for step, act in steps_of(sums).items()}
+    acts["V1"] = mid_vec.start_dp
+
+    def run(names):
+        for name in names:
+            acts[name]()
+
+    run(before_backward)
+
+    kv_rows = 3 * HD
+    logit[pl.ds(grads_at(0), count), :kv_rows] = jnp.zeros((count, kv_rows, rows), jnp.float32)
+    row_wide[...] = jnp.zeros_like(row_wide)
     back_carry[...] = jnp.zeros_like(back_carry)
     wkv_acc[...] = jnp.zeros_like(wkv_acc)
     wqq_acc[...] = jnp.zeros_like(wqq_acc)
-    wk0_acc[...] = jnp.zeros_like(wk0_acc)
-
-    def backward_tile(i, j):
-        prob = probs[pair_at(i, j)]
-        grad_logits = (prob.astype(jnp.float32) * dot_nt(grad_rows[...], vals[j])).astype(low)
-        dkv_acc[j, :HD] += dot_nn(grad_rows_t[...], prob)
-        dkv_acc[j, HD:] += dot_nn(query_t[i], grad_logits)
-        dq_acc[...] += dot_nn(grad_logits, key_query[j])
-        later = dot_nn(upper[...], grad_logits) + back_carry[j]
-        back_carry[j] = later[:1] - coeff * grad_logits[:1].astype(jnp.float32)
-        gated = (later * gates[pair_at(i, j)].astype(jnp.float32)).astype(low)
-        dq0_acc[...] += dot_nn(gated, first[j])
-        dk0_acc[j] += dot_nn(first_t[i], gated)
+
+    def prepare(i):
+        @pl.when(i != me)
+        def _():
+            exchange(send_gmix.at[i], recv_gmix.at[i], gmix_s.at[i], gmix_r.at[i], i).wait_recv()
+
+        grad = jnp.where(lane < HD, spread_rows(recv_gmix[i].astype(jnp.float32)), 0.0)
+        kept = logit[kept_at(i), :, :wide]
+        inverse = kept[:, HD : HD + 1]
+        delta = -jnp.sum(grad * kept, axis=1, keepdims=True) * inverse
+        grad = grad * inverse
+        grad_rows_t[i] = grad.T[:HD].astype(low)
+        delta_high = delta.astype(low).astype(jnp.float32)
+        grad = jnp.where(lane == HD, delta_high, jnp.where(lane == HD + 1, delta - delta_high, grad))
+        grad_rows[i] = grad.astype(low)
+
+    def backward_group(group):
+        spots = [pair_at(i, j) for i, j in group]
+        found = [probs[spot] for spot in spots]
+        grads = [dot_nt(grad_rows[i], vals[j]) for i, j in group]
+        grads = [(prob.astype(jnp.float32) * grad).astype(low) for prob, grad in zip(found, grads)]
+        laters = [dot_nn(upper[...], grad) for grad in grads]
+        gated = []
+        for k, (i, j) in enumerate(group):
+            later = laters[k] + back_carry[j]
+            back_carry[j] = later[:1] - coeff * grads[k][:1].astype(jnp.float32)
+            gated.append((later * gates[spots[k]].astype(jnp.float32)).astype(low))
+        query_parts = [dot_nn(grads[k], keys[j]) + dot_nn(gated[k], keys_zero[j]) for k, (_, j) in enumerate(group)]
+        key_parts = [
+            (
+                dot_nn(grad_rows_t[i], found[k]),
+                dot_nn(queries_t[i, :HD], grads[k]),
+                dot_nn(queries_t[i, HD:], gated[k]),
+            )
+            for k, (i, _) in enumerate(group)
+        ]
+        for k, (i, _) in enumerate(group):
+            row_wide[i] += query_parts[k]
+        for k, (_, j) in enumerate(group):
+            for part in range(3):
+                logit[grads_at(j), part * HD : (part + 1) * HD] += key_parts[k][part]
 
     def send_first_sum(i):
         exchange(send_first.at[i], y_first.at[i], fback_y.at[i], fback_yr.at[i], i).wait_recv()
@@ -959,228 +1075,196 @@
         def _():
             recv_first[z] = send_first[i]
 
-    def backward_row(step, carried):
-        i = count - 1 - step
-
-        @pl.when(i != me)
+    def block_of(step):
+        return upwards * (count - 1 - step) + (1 - upwards) * step
+
+    def backward_step(step, carried):
+        block = block_of(step)
+        pl.when(upwards == 1)(functools.partial(prepare, block))
+
+        def group(start, size):
+            members = []
+            for k in range(size):
+                i = upwards * block + (1 - upwards) * (count - 1 - start - k)
+                j = upwards * (start + k) + (1 - upwards) * block
+                members.append((i, j))
+            backward_group(members)
+
+        in_groups(count - step, group)
+        flat = logit[grads_at(block), :kv_rows]
+        flipped = flat[: 2 * HD].T
+        first_flipped = flat[HD:].T
+        grad_queries = row_wide[block] * score_scale
+        send_back[block, :rows] = join_heads(grad_queries, flipped).astype(low)
+        send_back[block, rows:] = fold_rows(flipped).astype(low)
+        send_first[block] = join_heads(swap_halves(grad_queries), first_flipped).astype(low)
+
+        @pl.when(block != me)
         def _():
-            exchange(send_gmix.at[i], recv_gmix.at[i], gmix_s.at[i], gmix_r.at[i], i).wait_recv()
-
-        grad = jnp.where(lane < HD, spread_rows(recv_gmix[i].astype(jnp.float32)), 0.0)
-        kept = mixed_keep[i]
-        inverse = kept[:, HD : HD + 1]
-        delta = -jnp.sum(grad * kept, axis=1, keepdims=True) * inverse
-        grad = grad * inverse
-        grad_rows_t[...] = grad.T[:HD].astype(low)
-        delta_high = delta.astype(low).astype(jnp.float32)
-        grad = jnp.where(lane == HD, delta_high, jnp.where(lane == HD + 1, delta - delta_high, grad))
-        grad_rows[...] = grad.astype(low)
-        dq_acc[...] = jnp.zeros_like(dq_acc)
-        dq0_acc[...] = jnp.zeros_like(dq0_acc)
-
-        def tiles(j, inner):
-            backward_tile(i, j)
-            return inner
-
-        lax.fori_loop(0, i + 1, tiles, 0)
-        flat = dkv_acc[i]
-        flipped = flat.T
-        queries = join_heads(dq_acc[...], swap_halves(dq0_acc[...])) * score_scale
-        first_keys = dk0_acc[i]
-        first_flipped = jnp.concatenate([first_keys, first_keys], axis=0).T
-        send_back[i, :rows] = join_heads(queries, flipped).astype(low)
-        send_back[i, rows:] = fold_rows(flipped).astype(low)
-        send_first[i] = join_heads(swap_halves(queries), first_flipped).astype(low)
-
-        @pl.when(i != me)
+            exchange(send_back.at[block], recv_back.at[me], back_s.at[block], back_r.at[me], block).start()
+
+        @pl.when(lax.rem(block, 2) != y)
         def _():
-            exchange(send_back.at[i], recv_back.at[me], back_s.at[i], back_r.at[me], i).start()
-
-        @pl.when(lax.rem(i, 2) != y)
-        def _():
-            exchange(send_first.at[i], y_first.at[i], fback_y.at[i], fback_yr.at[i], z * 2 + 1 - y).start()
-
-        normed = normed_all[i]
+            exchange(send_first.at[block], y_first.at[block], fback_y.at[block], fback_yr.at[block], z * 2 + 1 - y).start()
+
+        normed = normed_all[block]
         wkv_acc[...] += dot_nn(flat.astype(low), normed)
-        wqq_acc[...] += dot_nn(queries.T.astype(low), normed)
-        wk0_acc[...] += dot_nn(first_keys.astype(low), normed)
-        pl.when((step >= 2) & (lax.rem(i, 2) == y))(lambda: send_first_sum(i + 2))
-        pl.when(step == 0)(lambda: near_sum.send(2))
-        pl.when(step == 1)(lambda: rest_sum.send(2))
-        pl.when(step == 2)(mid_vec.start_dp)
-        pl.when(step == 3)(lambda: near_sum.send(3))
-        pl.when(step == 5)(lambda: rest_sum.send(3))
+        wqq_acc[...] += dot_nn(grad_queries.T.astype(low), normed)
+        pl.when((step >= 2) & (lax.rem(block, 2) == y))(lambda: send_first_sum(block_of(step - 2)))
+        for number, names in enumerate(between_steps):
+            if names:
+                pl.when(step == number)(functools.partial(run, names))
         return carried
 
-    lax.fori_loop(0, count, backward_row, 0)
+    def prepare_all(i, carried):
+        prepare(count - 1 - i)
+        return carried
+
+    lax.fori_loop(0, (1 - upwards) * count, prepare_all, 0)
+    lax.fori_loop(0, count, backward_step, 0)
     recv_back[me] = send_back[me]
 
     piece = HD // 4
-    for part in range(4):
-        for place, (source, start) in enumerate(((wqq_acc, 0), (wkv_acc, HD), (wkv_acc, 0))):
-            rows_in = pl.ds(part * 3 * piece + place * piece, piece)
-            in_mine[rows_in, :] = source[start + part * piece : start + (part + 1) * piece].astype(low)
-    extra_mine[:HD] = wqq_acc[HD:].astype(low)
-    extra_mine[HD:] = wk0_acc[...].astype(low)
     core_half, x_half = 6 * piece, 3 * piece
+    in_start = at.core * core_half
     in_core_copy = remote(rows_of(in_mine, (1 - at.core) * core_half, core_half), in_core, part_s.at[0], part_r.at[0], at.core_peer)
-    in_core_copy.start()
+    in_x_copy = remote(rows_of(in_mine, in_start + (1 - at.x) * x_half, x_half), in_x, part_s.at[1], part_r.at[1], at.x_peer)
+    each_seq = functools.partial(in_vec.each, count, me)
+    each_dp = functools.partial(in_vec.each, dp_count, dp)
 
     def extra_over_seq(to, slot):
         return exchange(rows_of(extra_mine, to * piece, piece), extra_seq.at[slot], extra_s.at[to], extra_r.at[slot], to)
 
     def extra_gather(to, owner):
-        return exchange(rows_of(extra_all, owner * piece, piece), rows_of(extra_all, owner * piece, piece), gather_s.at[to], gather_r.at[owner], to)
+        block = rows_of(extra_all, owner * piece, piece)
+        return exchange(block, block, gather_s.at[to], gather_r.at[owner], to)
 
     def extra_over_dp(to, slot):
         return remote(extra_sum, extra_dp.at[slot], edp_s.at[to], edp_r.at[slot], (to, me))
 
-    each_seq = functools.partial(in_vec.each, count, me)
-    each_dp = functools.partial(in_vec.each, dp_count, dp)
-    each_seq(lambda to: extra_over_seq(to, me).start())
-    extra_seq[me] = extra_mine[pl.ds(pl.multiple_of(me * piece, 16), piece), :]
-    for i in (1, 0):
-        pl.when(y == i)(functools.partial(send_first_sum, i))
-    in_core_copy.wait_recv()
-    in_start = at.core * core_half
-    add_rows(in_mine, in_start, in_core, 0, core_half)
-    in_x_copy = remote(rows_of(in_mine, in_start + (1 - at.x) * x_half, x_half), in_x, part_s.at[1], part_r.at[1], at.x_peer)
-    in_x_copy.start()
-    near_sum.send(4)
-    in_start = in_start + at.x * x_half
-    in_x_copy.wait_recv()
-
-    shard = x_half
-    in_three = ((at.core * 2 + at.two_bit) * 2 + at.three_bit) * depth * shard
-    in_own = in_three + z * shard
-
-    def last_add(k, carried):
-        here = pl.ds(pl.multiple_of(in_own + k * 16, 16), 16)
-        mine = pl.ds(pl.multiple_of(in_start + k * 16, 16), 16)
-        there = pl.ds(pl.multiple_of(k * 16, 16), 16)
-        in_final[here, :] = (in_mine[mine, :].astype(jnp.float32) + in_x[there, :].astype(jnp.float32)).astype(low)
-        return carried
-
-    lax.fori_loop(0, shard // 16, last_add, 0)
-
-    def in_deep(step):
-        to_z = lax.rem(z + step, depth)
-        block = rows_of(in_final, in_own, shard)
-        return remote(block, block, in_s.at[step - 1], in_r.at[step - 1], (dp, to_z * 2 + y))
-
-    def in_gather(start, size, slot, peer):
-        block = rows_of(in_final, start, size)
-        return remote(block, block, in_s.at[slot], in_r.at[slot], peer)
-
-    in_two = (at.core * 2 + at.two_bit) * 2 * depth * shard
-    in_one = at.core * 4 * depth * shard
-    in_up = [
-        in_gather(in_three, depth * shard, depth - 1, at.three_peer),
-        in_gather(in_two, 2 * depth * shard, depth, at.two_peer),
-        in_gather(in_one, 4 * depth * shard, depth + 1, at.core_peer),
-    ]
-    for step in range(1, depth):
-        in_deep(step).start()
-    each_seq(lambda source: extra_over_seq(source, source).wait_recv())
-    summed = extra_seq[0].astype(jnp.float32)
-    for k in range(1, count):
-        summed = summed + extra_seq[k].astype(jnp.float32)
-    extra_sum[...] = summed
-    each_dp(lambda to: extra_over_dp(to, dp).start())
-    extra_dp[dp] = summed
-    rest_sum.send(4)
-    near_sum.turn()
+    def in_zero():
+        for part in range(4):
+            for place, (source, start) in enumerate(((wqq_acc, 0), (wkv_acc, HD), (wkv_acc, 0))):
+                rows_in = pl.ds(part * 3 * piece + place * piece, piece)
+                in_mine[rows_in, :] = source[start + part * piece : start + (part + 1) * piece].astype(low)
+        in_core_copy.start()
+
+    def extra_zero():
+        extra_mine[:HD] = wqq_acc[HD:].astype(low)
+        extra_mine[HD:] = wkv_acc[2 * HD :].astype(low)
+        each_seq(lambda to: extra_over_seq(to, me).start())
+        extra_seq[me] = extra_mine[pl.ds(pl.multiple_of(me * piece, 16), piece), :]
+
+    def last_first_sums():
+        for step in (count - 2, count - 1):
+            pl.when(lax.rem(block_of(step), 2) == y)(functools.partial(send_first_sum, block_of(step)))
+
+    def in_one():
+        in_core_copy.wait_recv()
+        add_rows(in_mine, in_start, [(in_mine, in_start), (in_core, 0)], core_half)
+        in_x_copy.start()
+
+    def in_turn():
+        in_x_copy.wait_recv()
+        add_rows(in_final, in_sum.give[5], [(in_mine, in_start + at.x * x_half), (in_x, 0)], x_half)
+        in_sum.spread(5)
+
+    def extra_one():
+        each_seq(lambda source: extra_over_seq(source, source).wait_recv())
+        summed = extra_seq[0].astype(jnp.float32)
+        for k in range(1, count):
+            summed = summed + extra_seq[k].astype(jnp.float32)
+        extra_sum[...] = summed
+        each_dp(lambda to: extra_over_dp(to, dp).start())
+        extra_dp[dp] = summed
+
+    def extra_two():
+        each_dp(lambda source: extra_over_dp(source, source).wait_recv())
+        summed = extra_dp[0]
+        for k in range(1, dp_count):
+            summed = summed + extra_dp[k]
+        extra_all[pl.ds(pl.multiple_of(me * piece, 16), piece), :] = summed.astype(low)
+        each_seq(lambda to: extra_gather(to, me).start())
 
     def wait_back(step, carried):
         source = lax.rem(me + step, count)
         exchange(send_back.at[source], recv_back.at[source], back_s.at[source], back_r.at[source], source).wait_recv()
         return carried
 
-    lax.fori_loop(1, count, wait_back, 0)
-
     def wait_first(step, carried):
         source = lax.rem(z + step, depth)
         exchange(send_first.at[source], recv_first.at[source], fback_s.at[source], fback_r.at[source], source * 2 + y).wait_recv()
         return carried
 
-    lax.fori_loop(1, depth, wait_first, 0)
-    first_sum = recv_first[0].astype(jnp.float32)
-    for source in range(1, depth):
-        first_sum = first_sum + recv_first[source].astype(jnp.float32)
-    for pair in range(pairs):
-        even = recv_back[2 * pair, :rows].astype(jnp.float32)
-        odd = recv_back[2 * pair + 1, :rows].astype(jnp.float32)
-        if pair == 0:
-            even = even + first_sum
-        columns = wide * pair
-        joined_ref[:, pl.ds(columns, wide)] = join_heads(even, swap_halves(odd)).astype(low)
-        joined_ref[:, pl.ds(width + columns, wide)] = join_heads(swap_halves(even), odd).astype(low)
-        even = recv_back[2 * pair, rows:].astype(jnp.float32)
-        odd = recv_back[2 * pair + 1, rows:].astype(jnp.float32)
-        columns = pl.ds(2 * width + columns, wide)
-        joined_ref[pl.ds(0, half), columns] = join_heads(even, swap_halves(odd)).astype(low)
-        joined_ref[pl.ds(half, half), columns] = join_heads(swap_halves(even), odd).astype(low)
-    grad = dot_nt(joined_ref[...], w_qkv_ref[...])
-    unit = unit_one_ref[...]
-    vec_in_mine[...] = jnp.zeros_like(vec_in_mine)
-    vec_in_mine[pl.ds(0, 1), :] = jnp.sum(grad * unit, axis=0, keepdims=True)
-    vec_in_mine[pl.ds(1, 1), :] = jnp.sum(grad, axis=0, keepdims=True)
-    vec_in_mine[pl.ds(2, 1), :] = jnp.sum(joined_ref[:, pl.ds(2 * width, width)].astype(jnp.float32), axis=0, keepdims=True)
-    in_vec.start_seq()
-    tokens_grad_ref[0] = middle_ref[...] + normalise_back(grad, unit, rstd_one_ref[...], gain_one_ref[...])
-
-    for step in range(1, depth):
-        in_deep(step).wait_recv()
-    in_up[0].start()
-    near_sum.gather(3)
-    rest_sum.turn()
-    each_dp(lambda source: extra_over_dp(source, source).wait_recv())
-    summed = extra_dp[0]
-    for k in range(1, dp_count):
-        summed = summed + extra_dp[k]
-    extra_all[pl.ds(pl.multiple_of(me * piece, 16), piece), :] = summed.astype(low)
-    each_seq(lambda to: extra_gather(to, me).start())
-    in_vec.start_dp()
-    in_up[0].wait_recv()
-    in_up[1].start()
-    near_sum.gather(2)
-    rest_sum.gather(3)
-    vec_mid_ref[...] = mid_vec.finish()
-    near_sum.gather(1)
-    rest_sum.gather(2)
-    in_up[1].wait_recv()
-    in_up[2].start()
-    near_sum.gather(0)
-    rest_sum.gather(1)
-    near_sum.finish()
-    half_hidden = hidden_width // 2
-    stores = [
-        pltpu.make_async_copy(near_final.at[pl.ds(0, half_hidden)], w_down_out.at[pl.ds(0, half_hidden)], store_sem.at[0]),
-        pltpu.make_async_copy(near_final.at[pl.ds(near_rows, half_hidden)], w_up_out.at[pl.ds(0, half_hidden)], store_sem.at[1]),
-    ]
-    for store in stores:
-        store.start()
-    each_seq(lambda source: extra_gather(source, source).wait_recv())
-    in_up[2].wait_recv()
-    late = [
-        pltpu.make_async_copy(in_final, w_qkv_out, store_sem.at[2]),
-        pltpu.make_async_copy(extra_all, first_out, store_sem.at[3]),
-    ]
-    for store in late:
-        store.start()
-    stores += late
-    rest_sum.gather(0)
-    vec_in_ref[...] = in_vec.finish()
-    rest_sum.finish()
-    late = [
-        pltpu.make_async_copy(rest_final.at[pl.ds(0, half_hidden)], w_down_out.at[pl.ds(half_hidden, half_hidden)], store_sem.at[4]),
-        pltpu.make_async_copy(rest_final.at[pl.ds(rest_rows, half_hidden)], w_up_out.at[pl.ds(half_hidden, half_hidden)], store_sem.at[5]),
-        pltpu.make_async_copy(rest_final.at[pl.ds(quarter, width // 2)], w_out_out.at[pl.ds(0, width // 2)], store_sem.at[6]),
-        pltpu.make_async_copy(rest_final.at[pl.ds(rest_rows + quarter, width // 2)], w_out_out.at[pl.ds(width // 2, width // 2)], store_sem.at[7]),
-    ]
-    for store in late:
-        store.start()
-    stores += late
+    def first_norm_back():
+        lax.fori_loop(1, count, wait_back, 0)
+        lax.fori_loop(1, depth, wait_first, 0)
+        first_sum = recv_first[0].astype(jnp.float32)
+        for source in range(1, depth):
+            first_sum = first_sum + recv_first[source].astype(jnp.float32)
+        for pair in range(pairs):
+            even = recv_back[2 * pair, :rows].astype(jnp.float32)
+            odd = recv_back[2 * pair + 1, :rows].astype(jnp.float32)
+            if pair == 0:
+                even = even + first_sum
+            columns = wide * pair
+            joined_ref[:, pl.ds(columns, wide)] = join_heads(even, swap_halves(odd)).astype(low)
+            joined_ref[:, pl.ds(width + columns, wide)] = join_heads(swap_halves(even), odd).astype(low)
+            even = recv_back[2 * pair, rows:].astype(jnp.float32)
+            odd = recv_back[2 * pair + 1, rows:].astype(jnp.float32)
+            columns = pl.ds(2 * width + columns, wide)
+            joined_ref[pl.ds(0, half), columns] = join_heads(even, swap_halves(odd)).astype(low)
+            joined_ref[pl.ds(half, half), columns] = join_heads(swap_halves(even), odd).astype(low)
+        grad = dot_nt(joined_ref[...], w_qkv_ref[...])
+        unit, rstd = normalise(tokens_ref[0].astype(jnp.float32))
+        vec_in_mine[...] = jnp.zeros_like(vec_in_mine)
+        vec_in_mine[pl.ds(0, 1), :] = jnp.sum(grad * unit, axis=0, keepdims=True)
+        vec_in_mine[pl.ds(1, 1), :] = jnp.sum(grad, axis=0, keepdims=True)
+        value_grads = joined_ref[:, pl.ds(2 * width, width)].astype(jnp.float32)
+        vec_in_mine[pl.ds(2, 1), :] = jnp.sum(value_grads, axis=0, keepdims=True)
+        in_vec.start_seq()
+        tokens_grad_ref[0] = middle_ref[...] + normalise_back(grad, unit, rstd, gain_one_ref[...])
+
+    stores = []
+
+    def store(source, target):
+        stores.append(pltpu.make_async_copy(source, target, store_sem.at[len(stores)]))
+        stores[-1].start()
+
+    def finish_near():
+        near_sum.arrive(0)
+        store(near_final.at[pl.ds(0, half_hidden)], w_down_out.at[pl.ds(0, half_hidden)])
+        store(near_final.at[pl.ds(half_hidden, half_hidden)], w_up_out.at[pl.ds(0, half_hidden)])
+
+    def finish_rest():
+        rest_sum.arrive(0)
+        store(rest_final.at[pl.ds(0, half_hidden)], w_down_out.at[pl.ds(half_hidden, half_hidden)])
+        store(rest_final.at[pl.ds(half_hidden, half_hidden)], w_up_out.at[pl.ds(half_hidden, half_hidden)])
+
+    def finish_out():
+        out_sum.arrive(0)
+        store(out_final, w_out_out)
+
+    def finish_in():
+        in_sum.arrive(0)
+        store(in_final, w_qkv_out)
+
+    def finish_extra():
+        each_seq(lambda source: extra_gather(source, source).wait_recv())
+        store(extra_all, first_out)
+
+    def finish_mid_vec():
+        vec_mid_ref[...] = mid_vec.finish()
+
+    def finish_in_vec():
+        vec_in_ref[...] = in_vec.finish()
+
+    acts |= {
+        "I0": in_zero, "I1": in_one, "It": in_turn, "E0": extra_zero, "E1": extra_one, "E2": extra_two,
+        "F": last_first_sums, "T": first_norm_back, "W1": in_vec.start_dp, "Vf": finish_mid_vec, "Wf": finish_in_vec,
+        "Nf": finish_near, "Rf": finish_rest, "Of": finish_out, "If": finish_in, "Ef": finish_extra,
+    }
+    run(after_backward)
 
     pl.when(has_up(z))(lambda: pass_up(me).wait_send())
     pl.when(z > 0)(lambda: pass_down(me).wait_send())
@@ -1224,12 +1308,10 @@
     each_dp(lambda to: extra_over_dp(to, dp).wait_send())
     in_core_copy.wait_send()
     in_x_copy.wait_send()
-    for step in range(1, depth):
-        in_deep(step).wait_send()
-    for copy in in_up:
-        copy.wait_send()
     near_sum.drain()
     rest_sum.drain()
+    out_sum.drain()
+    in_sum.drain(False)
     mid_vec.drain()
     in_vec.drain()
     for store in stores:
@@ -1279,7 +1361,7 @@
                     core, x = owner // 2, owner % 2
                     two, three = (x, y) if core == 0 else (y, x)
                     depth = width // wide
-                    start = ((((core * 2 + two) * 2 + three) * depth + z) * 3 + part) * piece
+                    start = ((((core * 2 + two) * 2 + three) * depth + z % 2 * 2 + z // 2) * 3 + part) * piece
                     block = qkv_low[start : start + piece].astype(jnp.float32)
                     if head == 0 and part < 2:
                         at = part * HD + owner * piece
@@ -1317,7 +1399,6 @@
     wide = 2 * HD
     f32 = jnp.float32
     packed = rows + half
-    near, rest = hidden, hidden + width
     depth = count // 2
 
     def vmem(*shape, dtype=low):
@@ -1329,29 +1410,28 @@
     scratch = [
         vmem(width, width), vmem(width, hidden), vmem(hidden, width), sems(3), sems(8),
         vmem(count, rows, width), vmem(width, 2 * wide), vmem(width, wide), vmem(1, wide, dtype=f32),
-        vmem(count, rows, wide), vmem(count, rows, wide), vmem(count, rows, wide),
-        vmem(count, HD, rows), vmem(count, HD, rows), vmem(count, rows, wide), vmem(count, rows, wide),
+        vmem(count, rows, wide), vmem(count, rows, wide), vmem(count, rows, wide), vmem(count, rows, wide), vmem(count, wide, rows),
         vmem(tiles, rows, rows), vmem(tiles, rows, rows), vmem(tiles, rows, rows, dtype=f32),
-        vmem(count, 1, rows, dtype=f32), vmem(count, rows, wide, dtype=f32), vmem(rows, wide, dtype=f32), vmem(count, rows, wide, dtype=f32),
-        vmem(count, half, wide), vmem(count, half, wide), vmem(count, half, wide), vmem(count, half, wide), vmem(rows, wide), vmem(HD, rows),
-        vmem(rows, wide, dtype=f32), vmem(rows, wide, dtype=f32), vmem(count, wide, rows, dtype=f32), vmem(count, HD, rows, dtype=f32), vmem(count, 1, rows, dtype=f32),
+        vmem(count, 1, rows, dtype=f32), vmem(count, rows, wide, dtype=f32), vmem(rows, wide, dtype=f32),
+        vmem(count, half, wide), vmem(count, half, wide), vmem(count, half, wide), vmem(count, half, wide), vmem(count, rows, wide), vmem(count, HD, rows),
+        vmem(count, 1, rows, dtype=f32),
         vmem(count, packed, wide), vmem(count, packed, wide), vmem(count, rows, wide), vmem(count, rows, wide), vmem(depth, rows, wide),
         vmem(rows, rows), vmem(rows, rows),
-        vmem(rows, width, dtype=f32), vmem(rows, 1, dtype=f32), vmem(rows, width, dtype=f32), vmem(rows, 1, dtype=f32),
+        vmem(rows, width, dtype=f32), vmem(rows, 1, dtype=f32),
         vmem(rows, width), vmem(rows, width), vmem(rows, width, dtype=f32), vmem(rows, width, dtype=f32), vmem(rows, width, dtype=f32), vmem(rows, 3 * width),
     ]
-    for total in (near, rest):
+    for total in (hidden, hidden, width):
         scratch += [vmem(total, width), vmem(total, width)]
         scratch += [vmem(total >> stage, width) for stage in range(1, 6)]
     scratch += [
-        vmem(wide, width, dtype=f32), vmem(wide, width, dtype=f32), vmem(HD, width, dtype=f32),
+        vmem(3 * HD, width, dtype=f32), vmem(wide, width, dtype=f32),
         vmem(3 * HD, width), vmem(3 * HD // 2, width), vmem(3 * HD // 4, width), vmem(3 * width, width),
         vmem(wide, width), vmem(count, wide // count, width), vmem(wide // count, width, dtype=f32), vmem(dp_count, wide // count, width, dtype=f32), vmem(wide, width),
     ]
     for _ in range(2):
         scratch += [vmem(8, width, dtype=f32), vmem(count, 8, width, dtype=f32), vmem(8, width, dtype=f32), vmem(dp_count, 8, width, dtype=f32)]
     scratch += [sems(count)] * 18
-    scratch += [sems(10)] * 4 + [sems(depth + 2), sems(depth + 2), sems(2), sems(2), sems(4, count), sems(4, count), sems(dp_count), sems(dp_count)]
+    scratch += [sems(5, 6)] * 14 + [sems(2), sems(2), sems(4, count), sems(4, count), sems(dp_count), sems(dp_count)]
     in_vmem = pl.BlockSpec(memory_space=pltpu.VMEM)
     anywhere = pl.BlockSpec(memory_space=pl.ANY)
     specs = [in_vmem] * 15

time: 195 us -> 155 us (0.79)
  Pallas kernels: 189 us -> 150 us
    pallas_call x1, Pallas kernels: 182 us -> 143 us  [exchange_heads(): pl.pallas_call(layer_kernel, out_shape=[shape((1, rows, width), low), sha...]
where the time goes in v3:
time: 155 us
  Pallas kernels  150 us (97%)
  local copies, waits for them, and re-layouts  4.33 us (3%)
    pallas_call x1, Pallas kernels, exchange_heads(): pl.pallas_call(layer_kernel, out_shape=[shape((1, rows, width), low), sha...  143 us
    pallas_call x1, Pallas kernels, exchange_heads(): pl.pallas_call(widen_kernel, out_shape=[shape((hidden, width), f32), shap...  6.82 us

profile of v3, /device:TPU:0, one launch (start us, length us, event | category | flops | bytes accessed | tf_op | source)
XLA Modules:
  0.0 154.8 jit_solution(7510917215786453268)
XLA Ops:
  0.7 142.9 %shard_map.254 = (bf16[1,256,512]{2,1,0:T(8,128)(2,1)}, f32[1,256,512]{2,1,0:T(8,128)}, f32[8,512]{1,0:T(8,128)}, f32[8,512]{1,0:T(8,128)}, bf16[2048,512]{1,0:T...) custom-call(bf16[1,256,512]{2,1,0:T(8,128)(2,1)} %tokens_ref.1, ...), custom_call_target="tpu_custom_call" | custom-call | tf_op jit(solution)/shard_map/pallas_call | solution.py:1441
  143.6 0.7 slice_bitcast_fusion
  144.3 1.5 fusion
  145.8 0.6 copy.29
  146.4 0.0 copy-start.1
  146.4 0.0 copy-start
  146.4 6.8 %shard_map.255 = (f32[2048,512]{1,0:T(8,128)}, f32[512,2048]{1,0:T(8,128)}, f32[512,512]{1,0:T(8,128)}, f32[512,1536]{1,0:T(8,128)}) custom-call(bf16[2048,512]{1,0:T(8,128)(2,1)} %get-tuple-element.30.w_down_in, bf16[2048,512]{1,0:T(8,128)(2,1)} %get-tuple-element.31.w_up_in, bf16[512,512]{1,0:T(8,128)(2,1)} %get-tuple-element.32.w_out_in, ...), custom_call_target="tpu_custom_call" | custom-call | tf_op jit(solution)/shard_map/pallas_call | solution.py:1458
  153.3 0.0 copy-done.1
  153.3 0.7 copy.32
  154.0 0.0 copy-done
  154.0 0.8 copy.33
Async XLA Ops:
  146.4 6.8 %copy-start.1 = (bf16[1,256,512]{2,1,0:T(8,128)(2,1)S(1)}, bf16[1,256,512]{2,1,0:T(8,128)(2,1)}, u32[]{:S(2)}) copy-start(bf16[1,256,512]{2,1,0:T(8,128)(2,1)} %get-tuple-element.64) | copy-start | bytes 786436
  146.4 7.5 %copy-start = (f32[1,256,512]{2,1,0:T(8,128)S(1)}, f32[1,256,512]{2,1,0:T(8,128)}, u32[]{:S(2)}) copy-start(f32[1,256,512]{2,1,0:T(8,128)} %get-tuple-element.65) | copy-start | bytes 1572868

commit v4 on v3

--- a/solution.py
+++ b/solution.py
@@ -434,16 +434,22 @@
     return ref.at[pl.ds(pl.multiple_of(at, 16), size)]
 
 
+def wait_all(like, sem):
+    pltpu.make_async_copy(like, like, sem).wait()
+
+
 def add_rows(into, into_at, parts, size):
+    piece = next(rows for rows in (64, 48, 32, 16) if size % rows == 0)
+
     def step(k, carried):
         summed = None
         for ref, at in parts:
-            block = ref[pl.ds(pl.multiple_of(at + k * 16, 16), 16), :].astype(jnp.float32)
+            block = ref[pl.ds(pl.multiple_of(at + k * piece, 16), piece), :].astype(jnp.float32)
             summed = block if summed is None else summed + block
-        into[pl.ds(pl.multiple_of(into_at + k * 16, 16), 16), :] = summed.astype(low)
+        into[pl.ds(pl.multiple_of(into_at + k * piece, 16), piece), :] = summed.astype(low)
         return carried
 
-    lax.fori_loop(0, size // 16, step, 0)
+    lax.fori_loop(0, size // piece, step, 0)
 
 
 class Places:
@@ -473,13 +479,18 @@
 
 
 class StagedSum:
-    def __init__(self, at, mine, final, got, sems):
+    def __init__(self, at, x_first, mine, final, got, sems):
         self.mine, self.final, self.got = mine, final, got
-        bits = (at.core, at.two_bit, at.three_bit, at.z_low, at.z_high)
-        self.peers = (at.core_peer, at.two_peer, at.three_peer, at.z_near, at.z_far)
+        if x_first:
+            bits = (at.core, at.x, at.y, at.z_low, at.z_high)
+            self.peers = (at.core_peer, at.x_peer, at.y_peer, at.z_near, at.z_far)
+        else:
+            bits = (at.core, at.two_bit, at.three_bit, at.z_low, at.z_high)
+            self.peers = (at.core_peer, at.two_peer, at.three_peer, at.z_near, at.z_far)
         self.stages = len(bits)
         self.down_s, self.down_r, self.up_s, self.up_r = sems
-        start, size = 0, final.shape[0]
+        self.total = final.shape[0]
+        start, size = 0, self.total
         self.keep, self.give, self.size = [], [], []
         for bit in bits:
             size //= 2
@@ -498,12 +509,12 @@
             source = self.give[stage] + there
         return remote(
             rows_of(self.mine, source, size), rows_of(self.got[stage], there, size),
-            self.down_s.at[stage, block], self.down_r.at[stage, block], self.peers[stage],
+            self.down_s.at[0], self.down_r.at[block - 1], self.peers[stage],
         )
 
     def up(self, stage, block):
         here = rows_of(self.final, self.give[block], self.size[block])
-        return remote(here, here, self.up_s.at[stage, block], self.up_r.at[stage, block], self.peers[stage])
+        return remote(here, here, self.up_s.at[0], self.up_r.at[stage], self.peers[stage])
 
     def blocks(self, stage):
         return (1,) if stage == 0 else range(stage + 1, self.stages + 1)
@@ -517,9 +528,9 @@
     def collect(self, block, into):
         parts = [(self.mine, self.give[block])]
         for stage in range(block):
-            if stage > 0 or block == 1:
-                self.down(stage, block).wait_recv()
             parts.append((self.got[stage], self.give[block] - self.keep[stage]))
+        came = self.size[0] if block == 1 else (block - 1) * self.size[block]
+        wait_all(self.final.at[pl.ds(0, came)], self.down_r.at[block - 1])
         add_rows(into, self.give[block], parts, self.size[block])
 
     def turn(self):
@@ -531,20 +542,17 @@
             self.up(stage, block).start()
 
     def arrive(self, stage):
-        for block in range(stage + 1, self.stages + 1):
-            self.up(stage, block).wait_recv()
+        wait_all(rows_of(self.final, self.give[stage], self.size[stage]), self.up_r.at[stage])
 
     def gather(self, stage):
         self.arrive(stage)
         self.spread(stage)
 
-    def drain(self, summed=True):
-        for stage in range(self.stages):
-            if summed:
-                for block in self.blocks(stage):
-                    self.down(stage, block).wait_send()
-            for block in range(stage + 1, self.stages + 1):
-                self.up(stage, block).wait_send()
+    def drain(self):
+        left = self.final.at[pl.ds(0, self.total - self.size[-1])]
+        if self.mine is not None:
+            wait_all(left, self.down_s.at[0])
+        wait_all(left, self.up_s.at[0])
 
 
 class VectorSum:
@@ -552,16 +560,17 @@
         self.at, self.mine, self.seq_got, self.seq_sum, self.dp_got = at, mine, seq_got, seq_sum, dp_got
         self.send_sem, self.recv_sem, self.base = send_sem, recv_sem, base
 
-    def over_seq(self, to, slot):
+    def over_seq(self, to):
+        at = self.at
         return remote(
-            self.mine, self.seq_got.at[slot], self.send_sem.at[self.base, to], self.recv_sem.at[self.base, slot],
-            (self.at.dp, to),
+            self.mine, self.seq_got.at[at.me], self.send_sem.at[self.base], self.recv_sem.at[self.base], (at.dp, to)
         )
 
-    def over_dp(self, to, slot):
+    def over_dp(self, to):
+        at = self.at
         return remote(
-            self.seq_sum, self.dp_got.at[slot], self.send_sem.at[self.base + 1, to],
-            self.recv_sem.at[self.base + 1, slot], (to, self.at.me),
+            self.seq_sum, self.dp_got.at[at.dp], self.send_sem.at[self.base + 1], self.recv_sem.at[self.base + 1],
+            (to, at.me),
         )
 
     def each(self, count, mine, act):
@@ -573,49 +582,56 @@
 
     def start_seq(self):
         at = self.at
-        self.each(at.count, at.me, lambda to: self.over_seq(to, at.me).start())
+        self.each(at.count, at.me, lambda to: self.over_seq(to).start())
         self.seq_got[at.me] = self.mine[...]
 
     def start_dp(self):
         at = self.at
-        self.each(at.count, at.me, lambda source: self.over_seq(source, source).wait_recv())
+        wait_all(self.seq_got.at[pl.ds(0, at.count - 1)], self.recv_sem.at[self.base])
         summed = self.seq_got[0]
         for k in range(1, at.count):
             summed = summed + self.seq_got[k]
         self.seq_sum[...] = summed
-        self.each(at.dp_count, at.dp, lambda to: self.over_dp(to, at.dp).start())
+        self.each(at.dp_count, at.dp, lambda to: self.over_dp(to).start())
         self.dp_got[at.dp] = summed
 
     def finish(self):
         at = self.at
-        self.each(at.dp_count, at.dp, lambda source: self.over_dp(source, source).wait_recv())
+        wait_all(self.dp_got.at[pl.ds(0, at.dp_count - 1)], self.recv_sem.at[self.base + 1])
         summed = self.dp_got[0]
         for k in range(1, at.dp_count):
             summed = summed + self.dp_got[k]
         return summed
 
     def drain(self):
-        at = self.at
-        self.each(at.count, at.me, lambda to: self.over_seq(to, at.me).wait_send())
-        self.each(at.dp_count, at.dp, lambda to: self.over_dp(to, at.dp).wait_send())
-
-
-before_backward = ("N2", "R1",)
+        wait_all(self.seq_got.at[pl.ds(0, self.at.count - 1)], self.send_sem.at[self.base])
+        wait_all(self.dp_got.at[pl.ds(0, self.at.dp_count - 1)], self.send_sem.at[self.base + 1])
+
+
+before_backward = ("N2", "R1")
+within_steps = (
+    (),
+    (),
+    (),
+    (),
+)
 between_steps = (
-    ("N3",),
-    ("R2", "O1",),
-    ("N4",),
-    ("R3", "O2",),
-    ("Nt",),
-    ("R4", "V1", "O3",),
-    ("Ne",),
-    ("Rt", "O4",),
+    ("B0", "N3"),
+    ("B1", "R2", "O1"),
+    ("B2", "F0", "N4"),
+    ("B3", "F1", "R3", "O2"),
+    ("B4", "F2", "Nt"),
+    ("B5", "F3", "R4", "V1", "O3"),
+    ("B6", "F4", "Ne"),
+    ("B7", "F5", "Rt", "O4"),
 )
 after_backward = (
-    "I0", "E0", "F", "Nd", "I1", "Re", "Ot", "It", "E1", "Nc", "Rd", "T",
-    "Oe", "Ie", "Nb", "Rc", "Od", "E2", "Id", "W1", "Rb", "Oc", "Ic", "Ob",
-    "Ib", "Vf", "Nf", "Rf", "Of", "If", "Ef", "Wf",
+    "I0", "E0", "F6", "F7", "Nd", "I1", "Re", "Ot", "It", "E1", "Nc", "Rd",
+    "T", "Oe", "Ie", "Nb", "Rc", "Od", "E2", "Id", "W1", "Rb", "Oc", "Ic",
+    "Ob", "Ib", "Vf", "Nf", "Rf", "Of", "If", "Ef", "Wf",
 )
+
+near_x, rest_x, out_x = False, False, False
 
 
 def layer_kernel(
@@ -662,9 +678,9 @@
         extra_mine, extra_seq, extra_sum, extra_dp, extra_all,
         vec_mid_mine, vec_mid_seq, vec_mid_sum, vec_mid_dp,
         vec_in_mine, vec_in_seq, vec_in_sum, vec_in_dp,
-        norm_y, norm_up, norm_down, norm_r, mix_s, mix_r, gmix_s, gmix_r,
-        back_s, back_r, fback_y, fback_yr, fback_s, fback_r, extra_s, extra_r, gather_s, gather_r,
-        *sums_sems, in_s, in_r, part_s, part_r, vec_s, vec_r, edp_s, edp_r,
+        norm_s, norm_r, mix_s, mix_r, gmix_s, gmix_r,
+        back_s, back_r, fback_y, fback_yr, fback_s, fback_r, extra_s, extra_r,
+        *sums_sems, in_s, in_r, part_s, part_r, vec_s, vec_r,
     ) = scratch
     at = Places()
     dp_count, count, dp, me = at.dp_count, at.count, at.dp, at.me
@@ -707,16 +723,16 @@
     pl.semaphore_wait(barrier, count + dp_count - 2)
 
     def pass_y(block):
-        return exchange(normed_all.at[block], normed_all.at[block], norm_y.at[block], norm_r.at[block], z * 2 + 1 - y)
+        return exchange(normed_all.at[block], normed_all.at[block], norm_s.at[0], norm_r.at[block], z * 2 + 1 - y)
 
     def pass_up(block):
-        return exchange(normed_all.at[block], normed_all.at[block], norm_up.at[block], norm_r.at[block], me + 2)
+        return exchange(normed_all.at[block], normed_all.at[block], norm_s.at[1], norm_r.at[block], me + 2)
 
     def pass_down(block):
-        return exchange(normed_all.at[block], normed_all.at[block], norm_down.at[block], norm_r.at[block], me - 2)
+        return exchange(normed_all.at[block], normed_all.at[block], norm_s.at[2], norm_r.at[block], me - 2)
 
     def arrived(block):
-        exchange(normed_all.at[block], normed_all.at[block], norm_y.at[block], norm_r.at[block], block).wait_recv()
+        wait_all(normed_all.at[block], norm_r.at[block])
 
     def has_up(zz):
         return zz < depth - 1
@@ -832,9 +848,11 @@
                 top = jnp.maximum(top, scores[k][:, start : start + wide])
             row_wide[i] = top
 
-    def in_groups(total, act):
+    def in_groups(total, act, after_four=None):
         def four(group, carried):
             act(group * 4, 4)
+            if after_four is not None:
+                pl.when((group == 0) & (total > 4))(after_four)
             return carried
 
         lax.fori_loop(0, total // 4, four, 0)
@@ -864,7 +882,7 @@
 
         @pl.when(i != me)
         def _():
-            exchange(send_mix.at[i], recv_mix.at[me], mix_s.at[i], mix_r.at[me], i).start()
+            exchange(send_mix.at[i], recv_mix.at[me], mix_s.at[0], mix_r.at[0], i).start()
 
     upwards = 1 - z // (depth // 2)
     at_end = (z == 0) | (z == depth - 1)
@@ -917,12 +935,7 @@
     for load in loads:
         load.wait()
 
-    def wait_mixed(step, carried):
-        source = lax.rem(me + step, count)
-        exchange(send_mix.at[source], recv_mix.at[source], mix_s.at[source], mix_r.at[source], source).wait_recv()
-        return carried
-
-    lax.fori_loop(1, count, wait_mixed, 0)
+    wait_all(recv_mix.at[pl.ds(0, count - 1)], mix_r.at[0])
     for pair in range(pairs):
         even = recv_mix[2 * pair].astype(jnp.float32)
         odd = recv_mix[2 * pair + 1].astype(jnp.float32)
@@ -937,10 +950,10 @@
     normed_two_ref[...] = (unit * gain_two_ref[...] + bias_two_ref[...]).astype(low)
     out_acc[...] = jnp.zeros_like(out_acc)
     gn_acc[...] = jnp.zeros_like(gn_acc)
-    near_sum = StagedSum(at, near_mine, near_final, (near_core, near_two, near_three, near_four, near_five), sums_sems[:4])
-    rest_sum = StagedSum(at, rest_mine, rest_final, (rest_core, rest_two, rest_three, rest_four, rest_five), sums_sems[4:8])
-    out_sum = StagedSum(at, out_mine, out_final, (out_core, out_two, out_three, out_four, out_five), sums_sems[8:12])
-    in_sum = StagedSum(at, None, in_final, None, (None, None, in_s, in_r))
+    near_sum = StagedSum(at, near_x, near_mine, near_final, (near_core, near_two, near_three, near_four, near_five), sums_sems[:4])
+    rest_sum = StagedSum(at, rest_x, rest_mine, rest_final, (rest_core, rest_two, rest_three, rest_four, rest_five), sums_sems[4:8])
+    out_sum = StagedSum(at, out_x, out_mine, out_final, (out_core, out_two, out_three, out_four, out_five), sums_sems[8:12])
+    in_sum = StagedSum(at, False, None, in_final, None, (None, None, in_s, in_r))
     mid_vec = VectorSum(at, vec_mid_mine, vec_mid_seq, vec_mid_sum, vec_mid_dp, vec_s, vec_r, 0)
     in_vec = VectorSum(at, vec_in_mine, vec_in_seq, vec_in_sum, vec_in_dp, vec_s, vec_r, 2)
     chunk = width
@@ -984,7 +997,7 @@
 
     def send_grads(step, carried):
         to = lax.rem(me + step, count)
-        exchange(send_gmix.at[to], recv_gmix.at[me], gmix_s.at[to], gmix_r.at[me], to).start()
+        exchange(send_gmix.at[to], recv_gmix.at[me], gmix_s.at[0], gmix_r.at[me], to).start()
         return carried
 
     lax.fori_loop(1, count, send_grads, 0)
@@ -1025,7 +1038,7 @@
     def prepare(i):
         @pl.when(i != me)
         def _():
-            exchange(send_gmix.at[i], recv_gmix.at[i], gmix_s.at[i], gmix_r.at[i], i).wait_recv()
+            wait_all(recv_gmix.at[i], gmix_r.at[i])
 
         grad = jnp.where(lane < HD, spread_rows(recv_gmix[i].astype(jnp.float32)), 0.0)
         kept = logit[kept_at(i), :, :wide]
@@ -1064,12 +1077,12 @@
                 logit[grads_at(j), part * HD : (part + 1) * HD] += key_parts[k][part]
 
     def send_first_sum(i):
-        exchange(send_first.at[i], y_first.at[i], fback_y.at[i], fback_yr.at[i], i).wait_recv()
+        wait_all(y_first.at[i], fback_yr.at[i])
         send_first[i] = (send_first[i].astype(jnp.float32) + y_first[i].astype(jnp.float32)).astype(low)
 
         @pl.when(i != me)
         def _():
-            exchange(send_first.at[i], recv_first.at[z], fback_s.at[i], fback_r.at[z], i).start()
+            exchange(send_first.at[i], recv_first.at[z], fback_s.at[0], fback_r.at[0], i).start()
 
         @pl.when(i == me)
         def _():
@@ -1077,6 +1090,29 @@
 
     def block_of(step):
         return upwards * (count - 1 - step) + (1 - upwards) * step
+
+    def send_home(step):
+        block = block_of(step)
+
+        @pl.when(block != me)
+        def _():
+            exchange(send_back.at[block], recv_back.at[me], back_s.at[0], back_r.at[0], block).start()
+
+        @pl.when(lax.rem(block, 2) != y)
+        def _():
+            exchange(send_first.at[block], y_first.at[block], fback_y.at[0], fback_yr.at[block], z * 2 + 1 - y).start()
+
+    def send_first_home(step):
+        block = block_of(step)
+        pl.when(lax.rem(block, 2) == y)(functools.partial(send_first_sum, block))
+
+    for step in range(count):
+        acts[f"B{step}"] = functools.partial(send_home, step)
+        acts[f"F{step}"] = functools.partial(send_first_home, step)
+
+    def between(step, number, names):
+        if names:
+            pl.when(step == number)(functools.partial(run, names))
 
     def backward_step(step, carried):
         block = block_of(step)
@@ -1090,7 +1126,11 @@
                 members.append((i, j))
             backward_group(members)
 
-        in_groups(count - step, group)
+        def half_way():
+            for number, names in enumerate(within_steps):
+                between(step, number, names)
+
+        in_groups(count - step, group, half_way)
         flat = logit[grads_at(block), :kv_rows]
         flipped = flat[: 2 * HD].T
         first_flipped = flat[HD:].T
@@ -1099,21 +1139,11 @@
         send_back[block, rows:] = fold_rows(flipped).astype(low)
         send_first[block] = join_heads(swap_halves(grad_queries), first_flipped).astype(low)
 
-        @pl.when(block != me)
-        def _():
-            exchange(send_back.at[block], recv_back.at[me], back_s.at[block], back_r.at[me], block).start()
-
-        @pl.when(lax.rem(block, 2) != y)
-        def _():
-            exchange(send_first.at[block], y_first.at[block], fback_y.at[block], fback_yr.at[block], z * 2 + 1 - y).start()
-
         normed = normed_all[block]
         wkv_acc[...] += dot_nn(flat.astype(low), normed)
         wqq_acc[...] += dot_nn(grad_queries.T.astype(low), normed)
-        pl.when((step >= 2) & (lax.rem(block, 2) == y))(lambda: send_first_sum(block_of(step - 2)))
         for number, names in enumerate(between_steps):
-            if names:
-                pl.when(step == number)(functools.partial(run, names))
+            between(step, number, names)
         return carried
 
     def prepare_all(i, carried):
@@ -1132,15 +1162,15 @@
     each_seq = functools.partial(in_vec.each, count, me)
     each_dp = functools.partial(in_vec.each, dp_count, dp)
 
-    def extra_over_seq(to, slot):
-        return exchange(rows_of(extra_mine, to * piece, piece), extra_seq.at[slot], extra_s.at[to], extra_r.at[slot], to)
-
-    def extra_gather(to, owner):
-        block = rows_of(extra_all, owner * piece, piece)
-        return exchange(block, block, gather_s.at[to], gather_r.at[owner], to)
-
-    def extra_over_dp(to, slot):
-        return remote(extra_sum, extra_dp.at[slot], edp_s.at[to], edp_r.at[slot], (to, me))
+    def extra_over_seq(to):
+        return exchange(rows_of(extra_mine, to * piece, piece), extra_seq.at[me], extra_s.at[0], extra_r.at[0], to)
+
+    def extra_over_dp(to):
+        return remote(extra_sum, extra_dp.at[dp], extra_s.at[1], extra_r.at[1], (to, me))
+
+    def extra_gather(to):
+        block = rows_of(extra_all, me * piece, piece)
+        return exchange(block, block, extra_s.at[2], extra_r.at[2], to)
 
     def in_zero():
         for part in range(4):
@@ -1152,12 +1182,8 @@
     def extra_zero():
         extra_mine[:HD] = wqq_acc[HD:].astype(low)
         extra_mine[HD:] = wkv_acc[2 * HD :].astype(low)
-        each_seq(lambda to: extra_over_seq(to, me).start())
+        each_seq(lambda to: extra_over_seq(to).start())
         extra_seq[me] = extra_mine[pl.ds(pl.multiple_of(me * piece, 16), piece), :]
-
-    def last_first_sums():
-        for step in (count - 2, count - 1):
-            pl.when(lax.rem(block_of(step), 2) == y)(functools.partial(send_first_sum, block_of(step)))
 
     def in_one():
         in_core_copy.wait_recv()
@@ -1170,35 +1196,25 @@
         in_sum.spread(5)
 
     def extra_one():
-        each_seq(lambda source: extra_over_seq(source, source).wait_recv())
+        wait_all(extra_seq.at[pl.ds(0, count - 1)], extra_r.at[0])
         summed = extra_seq[0].astype(jnp.float32)
         for k in range(1, count):
             summed = summed + extra_seq[k].astype(jnp.float32)
         extra_sum[...] = summed
-        each_dp(lambda to: extra_over_dp(to, dp).start())
+        each_dp(lambda to: extra_over_dp(to).start())
         extra_dp[dp] = summed
 
     def extra_two():
-        each_dp(lambda source: extra_over_dp(source, source).wait_recv())
+        wait_all(extra_dp.at[pl.ds(0, dp_count - 1)], extra_r.at[1])
         summed = extra_dp[0]
         for k in range(1, dp_count):
             summed = summed + extra_dp[k]
         extra_all[pl.ds(pl.multiple_of(me * piece, 16), piece), :] = summed.astype(low)
-        each_seq(lambda to: extra_gather(to, me).start())
-
-    def wait_back(step, carried):
-        source = lax.rem(me + step, count)
-        exchange(send_back.at[source], recv_back.at[source], back_s.at[source], back_r.at[source], source).wait_recv()
-        return carried
-
-    def wait_first(step, carried):
-        source = lax.rem(z + step, depth)
-        exchange(send_first.at[source], recv_first.at[source], fback_s.at[source], fback_r.at[source], source * 2 + y).wait_recv()
-        return carried
+        each_seq(lambda to: extra_gather(to).start())
 
     def first_norm_back():
-        lax.fori_loop(1, count, wait_back, 0)
-        lax.fori_loop(1, depth, wait_first, 0)
+        wait_all(recv_back.at[pl.ds(0, count - 1)], back_r.at[0])
+        wait_all(recv_first.at[pl.ds(0, depth - 1)], fback_r.at[0])
         first_sum = recv_first[0].astype(jnp.float32)
         for source in range(1, depth):
             first_sum = first_sum + recv_first[source].astype(jnp.float32)
@@ -1250,7 +1266,7 @@
         store(in_final, w_qkv_out)
 
     def finish_extra():
-        each_seq(lambda source: extra_gather(source, source).wait_recv())
+        wait_all(extra_all.at[pl.ds(0, (count - 1) * piece)], extra_r.at[2])
         store(extra_all, first_out)
 
     def finish_mid_vec():
@@ -1261,57 +1277,30 @@
 
     acts |= {
         "I0": in_zero, "I1": in_one, "It": in_turn, "E0": extra_zero, "E1": extra_one, "E2": extra_two,
-        "F": last_first_sums, "T": first_norm_back, "W1": in_vec.start_dp, "Vf": finish_mid_vec, "Wf": finish_in_vec,
+        "T": first_norm_back, "W1": in_vec.start_dp, "Vf": finish_mid_vec, "Wf": finish_in_vec,
         "Nf": finish_near, "Rf": finish_rest, "Of": finish_out, "If": finish_in, "Ef": finish_extra,
     }
     run(after_backward)
 
-    pl.when(has_up(z))(lambda: pass_up(me).wait_send())
-    pl.when(z > 0)(lambda: pass_down(me).wait_send())
-    pass_y(me).wait_send()
-    for distance in range(1, depth):
-
-        def below(distance=distance):
-            pl.when(has_up(z))(lambda: pass_up(me - 2 * distance).wait_send())
-            pass_y(me - 2 * distance).wait_send()
-
-        def above(distance=distance):
-            pl.when(z > 0)(lambda: pass_down(me + 2 * distance).wait_send())
-            pass_y(me + 2 * distance).wait_send()
-
-        pl.when(z - distance >= 0)(below)
-        pl.when(z + distance < depth)(above)
-
-    def drain(step, carried):
-        to = lax.rem(me + step, count)
-        exchange(send_mix.at[to], recv_mix.at[me], mix_s.at[to], mix_r.at[me], to).wait_send()
-        exchange(send_gmix.at[to], recv_gmix.at[me], gmix_s.at[to], gmix_r.at[me], to).wait_send()
-        exchange(send_back.at[to], recv_back.at[me], back_s.at[to], back_r.at[me], to).wait_send()
-        extra_over_seq(to, me).wait_send()
-        extra_gather(to, me).wait_send()
-        return carried
-
-    lax.fori_loop(1, count, drain, 0)
-
-    def drain_first(step, carried):
-        to = lax.rem(z + step, depth) * 2 + y
-        exchange(send_first.at[to], recv_first.at[z], fback_s.at[to], fback_r.at[z], to).wait_send()
-        return carried
-
-    def drain_first_y(step, carried):
-        to = step * 2 + 1 - y
-        exchange(send_first.at[to], y_first.at[to], fback_y.at[to], fback_yr.at[to], z * 2 + 1 - y).wait_send()
-        return carried
-
-    lax.fori_loop(1, depth, drain_first, 0)
-    lax.fori_loop(0, depth, drain_first_y, 0)
-    each_dp(lambda to: extra_over_dp(to, dp).wait_send())
+    wait_all(normed_all.at[pl.ds(0, depth)], norm_s.at[0])
+    for at_z in range(depth - 1):
+        went = normed_all.at[pl.ds(0, at_z + 1)]
+        pl.when(z == at_z)(functools.partial(wait_all, went, norm_s.at[1]))
+        pl.when(z == depth - 1 - at_z)(functools.partial(wait_all, went, norm_s.at[2]))
+    wait_all(send_mix.at[pl.ds(0, count - 1)], mix_s.at[0])
+    wait_all(send_gmix.at[pl.ds(0, count - 1)], gmix_s.at[0])
+    wait_all(send_back.at[pl.ds(0, count - 1)], back_s.at[0])
+    wait_all(send_first.at[pl.ds(0, depth)], fback_y.at[0])
+    wait_all(send_first.at[pl.ds(0, depth - 1)], fback_s.at[0])
+    wait_all(extra_seq.at[pl.ds(0, count - 1)], extra_s.at[0])
+    wait_all(extra_dp.at[pl.ds(0, dp_count - 1)], extra_s.at[1])
+    wait_all(extra_all.at[pl.ds(0, (count - 1) * piece)], extra_s.at[2])
     in_core_copy.wait_send()
     in_x_copy.wait_send()
     near_sum.drain()
     rest_sum.drain()
     out_sum.drain()
-    in_sum.drain(False)
+    in_sum.drain()
     mid_vec.drain()
     in_vec.drain()
     for store in stores:
@@ -1430,8 +1419,10 @@
     ]
     for _ in range(2):
         scratch += [vmem(8, width, dtype=f32), vmem(count, 8, width, dtype=f32), vmem(8, width, dtype=f32), vmem(dp_count, 8, width, dtype=f32)]
-    scratch += [sems(count)] * 18
-    scratch += [sems(5, 6)] * 14 + [sems(2), sems(2), sems(4, count), sems(4, count), sems(dp_count), sems(dp_count)]
+    scratch += [sems(3), sems(count), sems(1), sems(1), sems(1), sems(count)]
+    scratch += [sems(1), sems(1), sems(1), sems(count), sems(1), sems(1), sems(3), sems(3)]
+    scratch += [sems(1), sems(5)] * 6
+    scratch += [sems(1), sems(5), sems(2), sems(2), sems(4), sems(4)]
     in_vmem = pl.BlockSpec(memory_space=pltpu.VMEM)
     anywhere = pl.BlockSpec(memory_space=pl.ANY)
     specs = [in_vmem] * 15

time: 155 us -> 151 us (0.974)
  Pallas kernels: 150 us -> 146 us
    pallas_call x1, Pallas kernels: 143 us -> 139 us  [exchange_heads(): pl.pallas_call(layer_kernel, out_shape=[shape((1, rows, width), low), sha...]
where the time goes in v4:
time: 151 us
  Pallas kernels  146 us (97%)
  local copies, waits for them, and re-layouts  4.33 us (3%)
    pallas_call x1, Pallas kernels, exchange_heads(): pl.pallas_call(layer_kernel, out_shape=[shape((1, rows, width), low), sha...  139 us
    pallas_call x1, Pallas kernels, exchange_heads(): pl.pallas_call(widen_kernel, out_shape=[shape((hidden, width), f32), shap...  6.82 us

profile of v4, /device:TPU:0, one launch (start us, length us, event | category | flops | bytes accessed | tf_op | source)
XLA Modules:
  0.0 150.6 jit_solution(10034313546549164045)
XLA Ops:
  0.7 138.8 %shard_map.254 = (bf16[1,256,512]{2,1,0:T(8,128)(2,1)}, f32[1,256,512]{2,1,0:T(8,128)}, f32[8,512]{1,0:T(8,128)}, f32[8,512]{1,0:T(8,128)}, bf16[2048,512]{1,0:T...) custom-call(bf16[1,256,512]{2,1,0:T(8,128)(2,1)} %tokens_ref.1, ...), custom_call_target="tpu_custom_call" | custom-call | tf_op jit(solution)/shard_map/pallas_call | solution.py:1432
  139.4 0.7 slice_bitcast_fusion
  140.1 1.5 fusion
  141.7 0.6 copy.29
  142.3 0.0 copy-start.1
  142.3 0.0 copy-start
  142.3 6.8 %shard_map.255 = (f32[2048,512]{1,0:T(8,128)}, f32[512,2048]{1,0:T(8,128)}, f32[512,512]{1,0:T(8,128)}, f32[512,1536]{1,0:T(8,128)}) custom-call(bf16[2048,512]{1,0:T(8,128)(2,1)} %get-tuple-element.30.w_down_in, bf16[2048,512]{1,0:T(8,128)(2,1)} %get-tuple-element.31.w_up_in, bf16[512,512]{1,0:T(8,128)(2,1)} %get-tuple-element.32.w_out_in, ...), custom_call_target="tpu_custom_call" | custom-call | tf_op jit(solution)/shard_map/pallas_call | solution.py:1449
  149.1 0.0 copy-done.1
  149.1 0.7 copy.32
  149.8 0.0 copy-done
  149.8 0.8 copy.33
Async XLA Ops:
  142.3 6.8 %copy-start.1 = (bf16[1,256,512]{2,1,0:T(8,128)(2,1)S(1)}, bf16[1,256,512]{2,1,0:T(8,128)(2,1)}, u32[]{:S(2)}) copy-start(bf16[1,256,512]{2,1,0:T(8,128)(2,1)} %get-tuple-element.64) | copy-start | bytes 786436
  142.3 7.5 %copy-start = (f32[1,256,512]{2,1,0:T(8,128)S(1)}, f32[1,256,512]{2,1,0:T(8,128)}, u32[]{:S(2)}) copy-start(f32[1,256,512]{2,1,0:T(8,128)} %get-tuple-element.65) | copy-start | bytes 1572868

commit v5 on v4

--- a/solution.py
+++ b/solution.py
@@ -620,15 +620,15 @@
     ("B1", "R2", "O1"),
     ("B2", "F0", "N4"),
     ("B3", "F1", "R3", "O2"),
-    ("B4", "F2", "Nt"),
-    ("B5", "F3", "R4", "V1", "O3"),
-    ("B6", "F4", "Ne"),
-    ("B7", "F5", "Rt", "O4"),
+    ("B4", "F2"),
+    ("B5", "F3", "Nt", "V1"),
+    ("B6", "F4", "R4", "O3"),
+    ("B7", "F5"),
 )
 after_backward = (
-    "I0", "E0", "F6", "F7", "Nd", "I1", "Re", "Ot", "It", "E1", "Nc", "Rd",
-    "T", "Oe", "Ie", "Nb", "Rc", "Od", "E2", "Id", "W1", "Rb", "Oc", "Ic",
-    "Ob", "Ib", "Vf", "Nf", "Rf", "Of", "If", "Ef", "Wf",
+    "I0", "E0", "F6", "F7", "Ne", "Rt", "O4", "I1", "Nd", "Re", "Ot", "It",
+    "E1", "Nc", "Rd", "Oe", "Rc", "T", "Ie", "Nb", "Od", "E2", "Id", "W1",
+    "Rb", "Oc", "Ic", "Ob", "Ib", "Vf", "Nf", "Rf", "Of", "If", "Ef", "Wf",
 )
 
 near_x, rest_x, out_x = False, False, False
@@ -639,7 +639,7 @@
     seg_ref,
     gain_one_ref,
     bias_one_ref,
-    w_qkv_ref,
+    w_qkv_hbm,
     b_val_ref,
     w_out_hbm,
     b_out_ref,
@@ -649,7 +649,7 @@
     b_up_ref,
     w_down_hbm,
     b_down_ref,
-    cot_ref,
+    cot_hbm,
     output_ref,
     tokens_grad_ref,
     vec_mid_ref,
@@ -662,7 +662,7 @@
     *scratch,
 ):
     (
-        w_out_ref, w_up_ref, w_down_ref, load_sem, store_sem,
+        w_out_ref, w_up_ref, w_down_ref, w_qkv_ref, cot_ref, load_sem, store_sem,
         normed_all, w_head, w_value, b_value, queries, keys, keys_zero, vals, queries_t,
         probs, gates, logit, carry, row_wide, row_acc,
         send_mix, recv_mix, send_gmix, recv_gmix, grad_rows, grad_rows_t,
@@ -706,7 +706,10 @@
 
     lax.fori_loop(1, count, greet_seq, 0)
     lax.fori_loop(1, dp_count, greet_dp, 0)
+    projection_load = pltpu.make_async_copy(w_qkv_hbm, w_qkv_ref, load_sem.at[3])
+    projection_load.start()
     loads = [
+        pltpu.make_async_copy(cot_hbm, cot_ref, load_sem.at[4]),
         pltpu.make_async_copy(w_out_hbm, w_out_ref, load_sem.at[0]),
         pltpu.make_async_copy(w_up_hbm, w_up_ref, load_sem.at[1]),
         pltpu.make_async_copy(w_down_hbm, w_down_ref, load_sem.at[2]),
@@ -756,6 +759,8 @@
 
         pl.when(z - distance >= 0)(from_below)
         pl.when(z + distance < depth)(from_above)
+
+    projection_load.wait()
 
     odd_head = lax.rem(me, 2) == 1
     pair_at_lane = pl.multiple_of((me // 2) * wide, wide)
@@ -1308,14 +1313,19 @@
 
 
 def widen_kernel(
-    w_down_in, w_up_in, w_out_in, w_qkv_in, first_in, w_down_out, w_up_out, w_out_out, w_qkv_out,
-    down_low, up_low, out_low, qkv_low, first_low, down_wide, up_wide, out_wide, qkv_wide, load_sem, store_sem,
+    output_in, tokens_grad_in, vec_mid_ref, vec_in_ref, w_down_in, w_up_in, w_out_in, w_qkv_in, first_in,
+    output_out, tokens_grad_out, gain_one_out, bias_one_out, b_val_out, b_out_out, gain_two_out, bias_two_out, b_up_out, b_down_out,
+    w_down_out, w_up_out, w_out_out, w_qkv_out,
+    down_low, up_low, out_low, qkv_low, first_low, tokens_grad_held, output_held, down_wide, up_wide, out_wide, qkv_wide, load_sem, store_sem,
 ):
     width = out_low.shape[0]
     blocks = down_low.shape[0] // width
     loads = []
     for k, (source, target) in enumerate(
-        ((w_qkv_in, qkv_low), (first_in, first_low), (w_out_in, out_low), (w_down_in, down_low), (w_up_in, up_low))
+        (
+            (w_down_in, down_low), (w_up_in, up_low), (w_qkv_in, qkv_low), (first_in, first_low), (w_out_in, out_low),
+            (tokens_grad_in, tokens_grad_held), (output_in, output_held),
+        )
     ):
         loads.append(pltpu.make_async_copy(source, target, load_sem.at[k]))
         loads[-1].start()
@@ -1324,6 +1334,13 @@
     def store(source, target):
         stores.append(pltpu.make_async_copy(source, target, store_sem.at[len(stores)]))
         stores[-1].start()
+
+    for row, target in enumerate((gain_one_out, bias_one_out, b_val_out)):
+        target[...] = vec_in_ref[row : row + 1, :]
+    for row in range(blocks):
+        b_up_out[:, row * width : (row + 1) * width] = vec_mid_ref[row : row + 1, :]
+    for row, target in enumerate((b_down_out, gain_two_out, bias_two_out, b_out_out)):
+        target[...] = vec_mid_ref[blocks + row : blocks + row + 1, :]
 
     def convert(source, target, at, columns):
         def step(k, carried):
@@ -1338,7 +1355,24 @@
         lax.fori_loop(0, width // 64, step, 0)
 
     loads[0].wait()
+    for block in range(blocks):
+        convert(down_low, down_wide, block * width, None)
+        here = pl.ds(block * width, width)
+        store(down_wide.at[here], w_down_out.at[here])
     loads[1].wait()
+    for block in range(blocks):
+        convert(up_low, up_wide, block * width, block * width)
+        here = pl.ds(block * width, width)
+        store(up_wide.at[:, here], w_up_out.at[:, here])
+    loads[4].wait()
+    convert(out_low, out_wide, 0, None)
+    store(out_wide, w_out_out)
+    loads[5].wait()
+    store(tokens_grad_held, tokens_grad_out)
+    loads[6].wait()
+    store(output_held, output_out)
+    loads[2].wait()
+    loads[3].wait()
     piece = HD // 4
     wide = 2 * HD
     for part in range(3):
@@ -1359,19 +1393,6 @@
             columns = part * width + pair * wide
             qkv_wide[:, columns : columns + wide] = jnp.concatenate(found, axis=0).T
     store(qkv_wide, w_qkv_out)
-    loads[2].wait()
-    convert(out_low, out_wide, 0, None)
-    store(out_wide, w_out_out)
-    loads[3].wait()
-    for block in range(blocks):
-        convert(down_low, down_wide, block * width, None)
-        here = pl.ds(block * width, width)
-        store(down_wide.at[here], w_down_out.at[here])
-    loads[4].wait()
-    for block in range(blocks):
-        convert(up_low, up_wide, block * width, block * width)
-        here = pl.ds(block * width, width)
-        store(up_wide.at[:, here], w_up_out.at[:, here])
     for one in stores:
         one.wait()
 
@@ -1397,7 +1418,7 @@
         return pltpu.SemaphoreType.DMA(shape)
 
     scratch = [
-        vmem(width, width), vmem(width, hidden), vmem(hidden, width), sems(3), sems(8),
+        vmem(width, width), vmem(width, hidden), vmem(hidden, width), vmem(width, 3 * width), vmem(1, rows, width), sems(5), sems(8),
         vmem(count, rows, width), vmem(width, 2 * wide), vmem(width, wide), vmem(1, wide, dtype=f32),
         vmem(count, rows, wide), vmem(count, rows, wide), vmem(count, rows, wide), vmem(count, rows, wide), vmem(count, wide, rows),
         vmem(tiles, rows, rows), vmem(tiles, rows, rows), vmem(tiles, rows, rows, dtype=f32),
@@ -1426,7 +1447,7 @@
     in_vmem = pl.BlockSpec(memory_space=pltpu.VMEM)
     anywhere = pl.BlockSpec(memory_space=pl.ANY)
     specs = [in_vmem] * 15
-    for at in (6, 10, 12):
+    for at in (4, 6, 10, 12, 14):
         specs[at] = anywhere
     shape = jax.ShapeDtypeStruct
     results = pl.pallas_call(
@@ -1445,35 +1466,30 @@
         tokens, segment_ids, gain_one[None], bias_one[None], w_qkv, b_val[None], w_out, b_out[None],
         gain_two[None], bias_two[None], w_up, b_up[None], w_down, b_down[None], cotangent,
     )
-    output, tokens_grad, vec_mid, vec_in = results[:4]
-    w_down_grad, w_up_grad, w_out_grad, w_qkv_grad = pl.pallas_call(
+    vector = shape((1, width), f32)
+    widened = pl.pallas_call(
         widen_kernel,
-        out_shape=[shape((hidden, width), f32), shape((width, hidden), f32), shape((width, width), f32), shape((width, 3 * width), f32)],
-        in_specs=[anywhere] * 5,
-        out_specs=[anywhere] * 4,
+        out_shape=[
+            shape((1, rows, width), low), shape((1, rows, width), f32), vector, vector, vector, vector, vector, vector, shape((1, hidden), f32), vector,
+            shape((hidden, width), f32), shape((width, hidden), f32), shape((width, width), f32), shape((width, 3 * width), f32),
+        ],
+        in_specs=[anywhere] * 2 + [in_vmem] * 2 + [anywhere] * 5,
+        out_specs=[anywhere] * 2 + [in_vmem] * 8 + [anywhere] * 4,
         scratch_shapes=[
-            vmem(hidden, width), vmem(hidden, width), vmem(width, width), vmem(3 * width, width), vmem(wide, width),
+            vmem(hidden, width), vmem(hidden, width), vmem(width, width), vmem(3 * width, width), vmem(wide, width), vmem(1, rows, width, dtype=f32), vmem(1, rows, width),
             vmem(hidden, width, dtype=f32), vmem(width, hidden, dtype=f32), vmem(width, width, dtype=f32), vmem(width, 3 * width, dtype=f32),
-            sems(5), sems(16),
+            sems(7), sems(12),
         ],
         compiler_params=pltpu.CompilerParams(vmem_limit_bytes=vmem_bytes),
-    )(*results[4:])
-    chunks = hidden // width
+    )(*results)
+    output, tokens_grad = widened[:2]
+    gain_one_grad, bias_one_grad, b_val_grad, b_out_grad, gain_two_grad, bias_two_grad, b_up_grad, b_down_grad = (
+        row.reshape(row.shape[1]) for row in widened[2:10]
+    )
+    w_down_grad, w_up_grad, w_out_grad, w_qkv_grad = widened[10:]
     return (
-        output,
-        tokens_grad,
-        vec_in[0],
-        vec_in[1],
-        w_qkv_grad,
-        vec_in[2],
-        w_out_grad,
-        vec_mid[chunks + 3],
-        vec_mid[chunks + 1],
-        vec_mid[chunks + 2],
-        w_up_grad,
-        vec_mid[:chunks].reshape(hidden),
-        w_down_grad,
-        vec_mid[chunks],
+        output, tokens_grad, gain_one_grad, bias_one_grad, w_qkv_grad, b_val_grad, w_out_grad, b_out_grad,
+        gain_two_grad, bias_two_grad, w_up_grad, b_up_grad, w_down_grad, b_down_grad,
     )
 
 

time: 151 us -> 146 us (0.967)
  local copies, waits for them, and re-layouts: 4.33 us -> 0 us
    unnamed x8 -> x0, local copies, waits for them, and re-layouts: 2.83 us -> none
    pallas_call x1, Pallas kernels: 139 us -> 137 us  [exchange_heads(): pl.pallas_call(layer_kernel, out_shape=[shape((1, rows, width), low), sha...]
where the time goes in v5:
time: 146 us
  Pallas kernels  145 us (99%)
    pallas_call x1, Pallas kernels, exchange_heads(): pl.pallas_call(layer_kernel, out_shape=[shape((1, rows, width), low), sha...  137 us
    pallas_call x1, Pallas kernels, exchange_heads(): pl.pallas_call(widen_kernel, out_shape=[shape((1, rows, width), low), sha...  8.08 us

profile of v5, /device:TPU:0, one launch (start us, length us, event | category | flops | bytes accessed | tf_op | source)
XLA Modules:
  0.0 145.7 jit_solution(14947135911312009880)
XLA Ops:
  0.7 136.8 %shard_map.254 = (bf16[1,256,512]{2,1,0:T(8,128)(2,1)}, f32[1,256,512]{2,1,0:T(8,128)}, f32[8,512]{1,0:T(8,128)}, f32[8,512]{1,0:T(8,128)}, bf16[2048,512]{1,0:T...) custom-call(bf16[1,256,512]{2,1,0:T(8,128)(2,1)} %tokens_ref.1, ...), custom_call_target="tpu_custom_call" | custom-call | tf_op jit(solution)/shard_map/pallas_call | solution.py:1453
  137.5 8.1 %shard_map.255 = (bf16[1,256,512]{2,1,0:T(8,128)(2,1)}, f32[1,256,512]{2,1,0:T(8,128)}, f32[1,512]{1,0:T(1,128)}, f32[1,512]{1,0:T(1,128)}, f32[1,512]{1,0:T(1,1...) custom-call(bf16[1,256,512]{2,1,0:T(8,128)(2,1)} %get-tuple-element., ...), custom_call_target="tpu_custom_call" | custom-call | tf_op jit(solution)/shard_map/pallas_call | solution.py:1470

commit v6 on v5

--- a/solution.py
+++ b/solution.py
@@ -725,37 +725,47 @@
     normed_all[me] = (unit * gain_one_ref[...] + bias_one_ref[...]).astype(low)
     pl.semaphore_wait(barrier, count + dp_count - 2)
 
-    def pass_y(block):
-        return exchange(normed_all.at[block], normed_all.at[block], norm_s.at[0], norm_r.at[block], z * 2 + 1 - y)
-
-    def pass_up(block):
-        return exchange(normed_all.at[block], normed_all.at[block], norm_s.at[1], norm_r.at[block], me + 2)
-
-    def pass_down(block):
-        return exchange(normed_all.at[block], normed_all.at[block], norm_s.at[2], norm_r.at[block], me - 2)
-
-    def arrived(block):
-        wait_all(normed_all.at[block], norm_r.at[block])
+    def part_of(block, part):
+        return normed_all.at[block, pl.ds(part * half, half)]
+
+    def pass_on(block, part, way, target):
+        here = part_of(block, part)
+        return exchange(here, here, norm_s.at[way], norm_r.at[block * 2 + part], target)
+
+    def pass_y(block, part):
+        pass_on(block, part, 0, z * 2 + 1 - y).start()
+
+    def pass_up(block, part):
+        pass_on(block, part, 1, me + 2).start()
+
+    def pass_down(block, part):
+        pass_on(block, part, 2, me - 2).start()
+
+    def arrived(block, part):
+        wait_all(part_of(block, part), norm_r.at[block * 2 + part])
 
     def has_up(zz):
         return zz < depth - 1
 
-    pl.when(has_up(z))(lambda: pass_up(me).start())
-    pl.when(z > 0)(lambda: pass_down(me).start())
-    pass_y(me).start()
+    for part in range(2):
+        pl.when(has_up(z))(functools.partial(pass_up, me, part))
+        pl.when(z > 0)(functools.partial(pass_down, me, part))
+        pass_y(me, part)
 
     def relay(distance):
         def from_below():
             block = me - 2 * distance
-            arrived(block)
-            pl.when(has_up(z))(lambda: pass_up(block).start())
-            pass_y(block).start()
+            for part in range(2):
+                arrived(block, part)
+                pl.when(has_up(z))(functools.partial(pass_up, block, part))
+                pass_y(block, part)
 
         def from_above():
             block = me + 2 * distance
-            arrived(block)
-            pl.when(z > 0)(lambda: pass_down(block).start())
-            pass_y(block).start()
+            for part in range(2):
+                arrived(block, part)
+                pl.when(z > 0)(functools.partial(pass_down, block, part))
+                pass_y(block, part)
 
         pl.when(z - distance >= 0)(from_below)
         pl.when(z + distance < depth)(from_above)
@@ -899,7 +909,8 @@
 
         @pl.when(lax.rem(block, 2) != y)
         def _():
-            arrived(block)
+            arrived(block, 0)
+            arrived(block, 1)
             for distance in range(1, depth):
                 pl.when(at_end & (group + 1 == distance))(functools.partial(relay, distance))
                 pl.when(jnp.logical_not(at_end) & (group + 2 == distance))(functools.partial(relay, distance))
@@ -1218,6 +1229,7 @@
         each_seq(lambda to: extra_gather(to).start())
 
     def first_norm_back():
+        unit, rstd = normalise(tokens_ref[0].astype(jnp.float32))
         wait_all(recv_back.at[pl.ds(0, count - 1)], back_r.at[0])
         wait_all(recv_first.at[pl.ds(0, depth - 1)], fback_r.at[0])
         first_sum = recv_first[0].astype(jnp.float32)
@@ -1237,7 +1249,6 @@
             joined_ref[pl.ds(0, half), columns] = join_heads(even, swap_halves(odd)).astype(low)
             joined_ref[pl.ds(half, half), columns] = join_heads(swap_halves(even), odd).astype(low)
         grad = dot_nt(joined_ref[...], w_qkv_ref[...])
-        unit, rstd = normalise(tokens_ref[0].astype(jnp.float32))
         vec_in_mine[...] = jnp.zeros_like(vec_in_mine)
         vec_in_mine[pl.ds(0, 1), :] = jnp.sum(grad * unit, axis=0, keepdims=True)
         vec_in_mine[pl.ds(1, 1), :] = jnp.sum(grad, axis=0, keepdims=True)
@@ -1440,7 +1451,7 @@
     ]
     for _ in range(2):
         scratch += [vmem(8, width, dtype=f32), vmem(count, 8, width, dtype=f32), vmem(8, width, dtype=f32), vmem(dp_count, 8, width, dtype=f32)]
-    scratch += [sems(3), sems(count), sems(1), sems(1), sems(1), sems(count)]
+    scratch += [sems(3), sems(2 * count), sems(1), sems(1), sems(1), sems(count)]
     scratch += [sems(1), sems(1), sems(1), sems(count), sems(1), sems(1), sems(3), sems(3)]
     scratch += [sems(1), sems(5)] * 6
     scratch += [sems(1), sems(5), sems(2), sems(2), sems(4), sems(4)]

time: 146 us -> 144 us (0.986)
  Pallas kernels: 145 us -> 143 us
    pallas_call x1, Pallas kernels: 137 us -> 135 us  [exchange_heads(): pl.pallas_call(layer_kernel, out_shape=[shape((1, rows, width), low), sha...]
where the time goes in v6:
time: 144 us; the launch traced here: 143 us
  Pallas kernels  143 us (99%)
    pallas_call x1, Pallas kernels, exchange_heads(): pl.pallas_call(layer_kernel, out_shape=[shape((1, rows, width), low), sha...  135 us
    pallas_call x1, Pallas kernels, exchange_heads(): pl.pallas_call(widen_kernel, out_shape=[shape((1, rows, width), low), sha...  8.08 us

profile of v6, /device:TPU:0, one launch (start us, length us, event | category | flops | bytes accessed | tf_op | source)
XLA Modules:
  0.0 143.5 jit_solution(16893547967351785126)
XLA Ops:
  0.7 134.6 %shard_map.254 = (bf16[1,256,512]{2,1,0:T(8,128)(2,1)}, f32[1,256,512]{2,1,0:T(8,128)}, f32[8,512]{1,0:T(8,128)}, f32[8,512]{1,0:T(8,128)}, bf16[2048,512]{1,0:T...) custom-call(bf16[1,256,512]{2,1,0:T(8,128)(2,1)} %tokens_ref.1, ...), custom_call_target="tpu_custom_call" | custom-call | tf_op jit(solution)/shard_map/pallas_call | solution.py:1464
  135.2 8.1 %shard_map.255 = (bf16[1,256,512]{2,1,0:T(8,128)(2,1)}, f32[1,256,512]{2,1,0:T(8,128)}, f32[1,512]{1,0:T(1,128)}, f32[1,512]{1,0:T(1,128)}, f32[1,512]{1,0:T(1,1...) custom-call(bf16[1,256,512]{2,1,0:T(8,128)(2,1)} %get-tuple-element., ...), custom_call_target="tpu_custom_call" | custom-call | tf_op jit(solution)/shard_map/pallas_call | solution.py:1481

commit v7 on v6

--- a/solution.py
+++ b/solution.py
@@ -997,7 +997,6 @@
     near_sum.send(0)
     lax.fori_loop(0, chunks // 2, functools.partial(dense, rest_mine, chunks // 2), 0)
     rest_sum.send(0)
-    near_sum.send(1)
     cot = cot_ref[0].astype(jnp.float32)
     grad = gn_acc[...]
     unit = unit_two_ref[...]
@@ -1017,6 +1016,7 @@
         return carried
 
     lax.fori_loop(1, count, send_grads, 0)
+    near_sum.send(1)
     recv_gmix[me] = send_gmix[me]
     out_mine[...] = dot_tn(mixed_ref[...], branch).astype(low)
     out_sum.send(0)

time: 144 us -> 143 us (level)
  no operation moved by 1% of the time
where the time goes in v7:
time: 143 us
  Pallas kernels  142 us (99%)
    pallas_call x1, Pallas kernels, exchange_heads(): pl.pallas_call(layer_kernel, out_shape=[shape((1, rows, width), low), sha...  134 us
    pallas_call x1, Pallas kernels, exchange_heads(): pl.pallas_call(widen_kernel, out_shape=[shape((1, rows, width), low), sha...  8.08 us

profile of v7, /device:TPU:0, one launch (start us, length us, event | category | flops | bytes accessed | tf_op | source)
XLA Modules:
  0.0 142.9 jit_solution(2008355592899864132)
XLA Ops:
  0.7 134.0 %shard_map.254 = (bf16[1,256,512]{2,1,0:T(8,128)(2,1)}, f32[1,256,512]{2,1,0:T(8,128)}, f32[8,512]{1,0:T(8,128)}, f32[8,512]{1,0:T(8,128)}, bf16[2048,512]{1,0:T...) custom-call(bf16[1,256,512]{2,1,0:T(8,128)(2,1)} %tokens_ref.1, ...), custom_call_target="tpu_custom_call" | custom-call | tf_op jit(solution)/shard_map/pallas_call | solution.py:1464
  134.7 8.1 %shard_map.255 = (bf16[1,256,512]{2,1,0:T(8,128)(2,1)}, f32[1,256,512]{2,1,0:T(8,128)}, f32[1,512]{1,0:T(1,128)}, f32[1,512]{1,0:T(1,128)}, f32[1,512]{1,0:T(1,1...) custom-call(bf16[1,256,512]{2,1,0:T(8,128)(2,1)} %get-tuple-element., ...), custom_call_target="tpu_custom_call" | custom-call | tf_op jit(solution)/shard_map/pallas_call | solution.py:1481
